TPU v7x, 32 devices: a whole 2x2x4 slice. The times are simulated.
32 devices in a mesh: seq: 16 (over z, y, x), head: 2 (over core).
Axes of the slice: x: 2, y: 2, z: 4, core: 2. Of those that a mesh axis runs over, the one named last changes fastest.
Arguments:
- tokens: bfloat16 [2, 4096, 512], P(None, 'seq'), may hold values from -8 to 8
- counts: int32 [2], replicated, may hold values from 512 to 4096, as said below
- ln_gain: float32 [512], replicated, may hold values from 0.5 to 1.5
- ln_bias: float32 [512], replicated, may hold values from -1.5 to 1.5
- w_qkv: bfloat16 [3, 512, 512], P(None, 'seq', 'head'), may hold values from -0.25 to 0.25
- conv_taps: float32 [8, 33], P('head'), may hold values from -1 to 1
- w_out: bfloat16 [512, 512], P('head', 'seq'), may hold values from -0.25 to 0.25
- out_bias: float32 [512], replicated, may hold values from -1.5 to 1.5
- kernel7: float32 [7, 7, 512], replicated, may hold values from -0.875 to 0.875
- kernel5: float32 [5, 5, 512], replicated, may hold values from -1.25 to 1.25
- kernel3: float32 [3, 3, 512], replicated, may hold values from -2 to 2
- ppeg_bias: float32 [512], replicated, may hold values from -1.5 to 1.5
- cotangent: bfloat16 [2, 4096, 512], P(None, 'seq'), may hold values from -6 to 6
Outputs:
- output: bfloat16 [2, 4096, 512], P(None, 'seq')
- grad_tokens: float32 [2, 4096, 512], P(None, 'seq')
- grad_ln_gain: float32 [512], replicated
- grad_ln_bias: float32 [512], replicated
- grad_w_qkv: float32 [3, 512, 512], P(None, 'seq', 'head')
- grad_conv_taps: float32 [8, 33], P('head')
- grad_w_out: float32 [512, 512], P('head', 'seq')
- grad_out_bias: float32 [512], replicated
- grad_kernel7: float32 [7, 7, 512], replicated
- grad_kernel5: float32 [5, 5, 512], replicated
- grad_kernel3: float32 [3, 3, 512], replicated
- grad_ppeg_bias: float32 [512], replicated
Inputs may be any that keep to these rules, and one draw needn't show every extreme that they name: `counts`: one slide of every draw, which one drawn from the seed, fills all 4096 slots.
All inputs are finite; a program needn't handle non-finite values.
Results may differ from a plain program's by a relative error of at most 0.009.
Values may be sent and summed in bfloat16 or wider, within the bound.
A program may use at most 128 MiB of HBM per device.

v0:
```python
import jax
import jax.numpy as jnp
from jax import lax
from jax.sharding import PartitionSpec as P

LANDMARKS = 256
PINV_ITERS = 6
GRID_W = 64


EPSILON = 1e-05
FULL_PRECISION = lax.Precision.HIGHEST


def combined_all(part, axis, combine):
    gathered = jax.tree.map(lambda a: lax.all_gather(a, axis), part)

    def take(source):
        return jax.tree.map(lambda a: lax.dynamic_index_in_dim(a, source, 0, False), gathered)

    return lax.fori_loop(
        1, lax.axis_size(axis), lambda source, state: combine(state, take(source)), take(0)
    )


def padded_2(cells, sides, width):
    for axis, dim in sides:
        count = lax.axis_size(axis)
        ends = count - 1
        head = lax.slice_in_dim(cells, 0, width, axis=dim)
        tail = lax.slice_in_dim(cells, cells.shape[dim] - width, cells.shape[dim], axis=dim)
        cells = jnp.concatenate(
            [
                lax.ppermute(tail, axis, [(i, (i + 1) % count) for i in range(ends)]),
                cells,
                lax.ppermute(head, axis, [((i + 1) % count, i) for i in range(ends)]),
            ],
            axis=dim,
        )
    return cells


def batched_product(left_matrix, right_matrix):
    return jnp.einsum("hij,hjk->hik", left_matrix, right_matrix, precision=FULL_PRECISION)


def pseudo_inverse(matrix):
    column_sums = jnp.sum(matrix, axis=1)
    row_sums = jnp.sum(matrix, axis=2)
    scaling = jnp.max(column_sums, axis=-1) * jnp.max(row_sums, axis=-1)
    iterate = jnp.swapaxes(matrix, 1, 2) / scaling[:, None, None]
    identity = jnp.eye(matrix.shape[-1], dtype=matrix.dtype)
    for sweep in range(PINV_ITERS):
        product = batched_product(matrix, iterate)
        inner_term = 7.0 * identity - product
        inner_term = 15.0 * identity - batched_product(product, inner_term)
        inner_term = 13.0 * identity - batched_product(product, inner_term)
        iterate = 0.25 * batched_product(iterate, inner_term)
    return iterate


def chain_from_scores(mark_scores, value_landmarks):
    inverse = pseudo_inverse(jax.nn.softmax(mark_scores, axis=-1))
    return jnp.einsum("hij,jhd->ihd", inverse, value_landmarks, precision=FULL_PRECISION)


def grid_conv(padded, kernel_taps):
    convolved = lax.conv_general_dilated(
        padded[None],
        kernel_taps[:, :, None, :],
        (1, 1),
        "VALID",
        dimension_numbers=("NHWC", "HWIO", "NHWC"),
        feature_group_count=kernel_taps.shape[-1],
        precision=FULL_PRECISION,
    )
    return convolved[0]


def line_conv(extended, columns):
    convolved = lax.conv_general_dilated(
        extended[None],
        columns[:, None, :],
        (1,),
        "VALID",
        dimension_numbers=("NWC", "WIO", "NWC"),
        feature_group_count=columns.shape[-1],
        precision=FULL_PRECISION,
    )
    return convolved[0]


def combine_stats(former, second):
    top_score = jnp.maximum(former[0], second[0])
    total_sum = former[1] * jnp.exp(former[0] - top_score) + second[1] * jnp.exp(
        second[0] - top_score
    )
    return (top_score, total_sum)


def shard_grads(grad_in, grad_back):
    return (
        lax.psum_scatter(grad_in, "seq", scatter_dimension=1, tiled=True),
        lax.psum_scatter(grad_back, "seq", scatter_dimension=1, tiled=True),
    )


def shards(
    tokens,
    counts,
    ln_gain,
    ln_bias,
    w_qkv,
    conv_taps,
    w_out,
    out_bias,
    kernel7,
    kernel5,
    kernel3,
    ppeg_bias,
    cotangent,
):
    length_local = tokens.shape[1]
    model_width = tokens.shape[2]
    heads_local = conv_taps.shape[0]
    local_width = w_qkv.shape[2]
    head_width = local_width // heads_local
    tap_count = conv_taps.shape[1]
    margin = tap_count // 2
    grid_rows = length_local // GRID_W
    mark_count = LANDMARKS
    scores_scale_factor = head_width ** (-0.5)
    positions = lax.axis_index("seq") * length_local + jnp.arange(length_local, dtype=jnp.int32)
    slot_ids = jnp.arange(mark_count, dtype=jnp.int32)
    tap_columns = jnp.repeat(conv_taps.T, head_width, axis=1)
    taps_flipped = tap_columns[::-1]
    combined = (
        kernel7
        + jnp.pad(kernel5, ((1, 1), (1, 1), (0, 0)))
        + jnp.pad(kernel3, ((2, 2), (2, 2), (0, 0)))
    )
    flipped = combined[::-1, ::-1]

    def one_slide(running, slide_item):
        tokens_slide, cot_slide, count = slide_item
        w_in, w_back = (
            lax.all_gather(w_qkv, "seq", axis=1, tiled=True),
            lax.all_gather(w_out, "seq", axis=1, tiled=True),
        )
        is_valid = positions < count
        mask_float = is_valid.astype(jnp.float32)
        inputs = tokens_slide.astype(jnp.float32)
        centred = inputs - jnp.mean(inputs, axis=-1, keepdims=True)
        inv_std = lax.rsqrt(jnp.mean(centred * centred, axis=-1, keepdims=True) + EPSILON)
        standard = centred * inv_std
        normed = (standard * ln_gain + ln_bias).astype(jnp.bfloat16)
        projected = jnp.einsum(
            "ld,kdc->klc", normed, w_in, preferred_element_type=jnp.float32
        ).astype(jnp.bfloat16)
        query_row_block = projected[0].reshape(length_local, heads_local, head_width)
        key_row_block = projected[1].reshape(length_local, heads_local, head_width)
        value_rows = projected[2].reshape(length_local, heads_local, head_width)
        segment = jnp.where(is_valid, positions * mark_count // count, mark_count)
        member = (segment[None, :] == slot_ids[:, None]).astype(jnp.bfloat16)
        mark_sums = jnp.einsum(
            "ml,klc->kmc", member, projected[:2], preferred_element_type=jnp.float32
        )
        mark_sums = lax.psum(mark_sums, "seq")
        seg_upper = ((slot_ids + 1) * count + mark_count - 1) // mark_count
        seg_lower = (slot_ids * count + mark_count - 1) // mark_count
        seg_sizes = (seg_upper - seg_lower).astype(jnp.float32)
        mark_means = (mark_sums / seg_sizes[None, :, None]).astype(jnp.bfloat16)
        query_landmarks = mark_means[0].reshape(mark_count, heads_local, head_width)
        key_landmarks = mark_means[1].reshape(mark_count, heads_local, head_width)
        query_landmark_scores = scores_scale_factor * jnp.einsum(
            "wox,vox->owv", query_row_block, key_landmarks, preferred_element_type=jnp.float32
        )
        attention_query_side = jax.nn.softmax(query_landmark_scores, axis=-1)
        attention_landmark_rows = attention_query_side.astype(jnp.bfloat16)
        landmark_key_scores = scores_scale_factor * jnp.einsum(
            "oue,fue->uof", query_landmarks, key_row_block, preferred_element_type=jnp.float32
        )
        landmark_key_scores = jnp.where(is_valid[None, None, :], landmark_key_scores, -1e30)
        local_top = jnp.max(landmark_key_scores, axis=-1)
        local_total = jnp.sum(
            jnp.where(
                is_valid[None, None, :], jnp.exp(landmark_key_scores - local_top[..., None]), 0.0
            ),
            axis=-1,
        )
        top_score, total_sum = combined_all((local_top, local_total), "seq", combine_stats)
        attention_key_side = (
            jnp.where(
                is_valid[None, None, :], jnp.exp(landmark_key_scores - top_score[..., None]), 0.0
            )
            / total_sum[..., None]
        )
        key_side_inverse = attention_key_side.astype(jnp.bfloat16)
        value_rows_masked = value_rows * mask_float.astype(jnp.bfloat16)[:, None, None]
        value_part = jnp.einsum(
            "uqy,yut->qut", key_side_inverse, value_rows_masked, preferred_element_type=jnp.float32
        )
        exact_part = jnp.einsum(
            "uqy,yut->qut",
            attention_key_side,
            value_rows_masked.astype(jnp.float32),
            precision=FULL_PRECISION,
        )
        value_landmarks, exact_marks = lax.psum((value_part, exact_part), "seq")
        mark_scores = scores_scale_factor * jnp.einsum(
            "ihd,jhd->hij", query_landmarks, key_landmarks, preferred_element_type=jnp.float32
        )
        mixed_landmarks, chain_pull = jax.vjp(chain_from_scores, mark_scores, value_landmarks)
        mixed_landmark_inverse = mixed_landmarks.astype(jnp.bfloat16)
        flat_values = value_rows_masked.reshape(length_local, local_width)
        value_ext = padded_2(flat_values, (("seq", 0),), margin).astype(jnp.float32)
        attention_matrix = jnp.einsum(
            "kjo,okx->jkx",
            attention_landmark_rows,
            mixed_landmark_inverse,
            preferred_element_type=jnp.float32,
        ).reshape(length_local, local_width)
        attention_matrix = attention_matrix + line_conv(value_ext, tap_columns)
        attention_low = attention_matrix.astype(jnp.bfloat16)
        partial_out = jnp.dot(attention_low, w_back, preferred_element_type=jnp.float32)
        hidden = (
            inputs
            + lax.psum(partial_out.astype(jnp.bfloat16), "head").astype(jnp.float32)
            + out_bias
        )
        grid_cells = (hidden * mask_float[:, None]).reshape(grid_rows, GRID_W, model_width)
        grid_ext = padded_2(grid_cells.astype(jnp.bfloat16), (("seq", 0),), 3).astype(
            grid_cells.dtype
        )
        grid_pad = jnp.pad(grid_ext, ((0, 0), (3, 3), (0, 0)))
        result = (
            hidden + grid_conv(grid_pad, combined).reshape(length_local, model_width) + ppeg_bias
        )
        grad_out = cot_slide.astype(jnp.float32)
        cot_grid = cot_slide.reshape(grid_rows, GRID_W, model_width)
        cot_ext = padded_2(cot_grid, (("seq", 0),), 3)
        cot_pad = jnp.pad(cot_ext.astype(jnp.float32), ((0, 0), (3, 3), (0, 0)))
        grad_grid = grid_conv(cot_pad, flipped).reshape(length_local, model_width)
        unused_grid, kernel_pull = jax.vjp(
            lambda kernel_now: grid_conv(grid_pad, kernel_now), combined
        )
        grad_kernel = kernel_pull(grad_out.reshape(grid_rows, GRID_W, model_width))[0]
        grad_hidden = grad_out + grad_grid * mask_float[:, None]
        hidden_low = grad_hidden.astype(jnp.bfloat16)
        grad_back = jnp.einsum(
            "lc,ld->cd", attention_low, hidden_low, preferred_element_type=jnp.float32
        )
        grad_attention = jnp.einsum(
            "ld,cd->lc", hidden_low, w_back, preferred_element_type=jnp.float32
        ).astype(jnp.bfloat16)
        grad_ext = padded_2(grad_attention, (("seq", 0),), margin).astype(jnp.float32)
        conv_values = line_conv(grad_ext, taps_flipped)
        unused_line, tap_pull = jax.vjp(lambda columns: line_conv(value_ext, columns), tap_columns)
        grad_columns = tap_pull(grad_attention.astype(jnp.float32))[0]
        grad_taps = jnp.sum(grad_columns.reshape(tap_count, heads_local, head_width), axis=-1).T
        head_gradients = grad_attention.reshape(length_local, heads_local, head_width)
        grad_one = jnp.einsum(
            "wox,vox->owv",
            head_gradients,
            mixed_landmark_inverse,
            preferred_element_type=jnp.float32,
        )
        grad_mixed = jnp.einsum(
            "ufp,fua->pua",
            attention_landmark_rows,
            head_gradients,
            preferred_element_type=jnp.float32,
        )
        scores_grad = attention_query_side * (
            grad_one - jnp.sum(attention_query_side * grad_one, axis=-1, keepdims=True)
        )
        landmark_scores = scores_grad.astype(jnp.bfloat16)
        grad_query = scores_scale_factor * jnp.einsum(
            "kjo,okx->jkx", landmark_scores, key_landmarks, preferred_element_type=jnp.float32
        )
        key_mark_part = scores_scale_factor * jnp.einsum(
            "ufp,fua->pua", landmark_scores, query_row_block, preferred_element_type=jnp.float32
        )
        grad_mixed, key_mark_part = lax.psum((grad_mixed, key_mark_part), "seq")
        grad_mark_scores, grad_value_marks = chain_pull(grad_mixed)
        chain_query = scores_scale_factor * jnp.einsum(
            "hij,jhd->ihd",
            grad_mark_scores,
            key_landmarks.astype(jnp.float32),
            precision=FULL_PRECISION,
        )
        chain_key = scores_scale_factor * jnp.einsum(
            "hij,ihd->jhd",
            grad_mark_scores,
            query_landmarks.astype(jnp.float32),
            precision=FULL_PRECISION,
        )
        value_landmarks_inverse = grad_value_marks.astype(jnp.bfloat16)
        grad_three = jnp.einsum(
            "oue,fue->uof",
            value_landmarks_inverse,
            value_rows_masked,
            preferred_element_type=jnp.float32,
        )
        row_terms = jnp.einsum(
            "sjv,sjv->js",
            value_landmarks_inverse.astype(jnp.float32),
            exact_marks,
            precision=FULL_PRECISION,
        )
        three_grad = attention_key_side * (grad_three - row_terms[..., None])
        key_side_inverse_gradient = three_grad.astype(jnp.bfloat16)
        query_mark_part = scores_scale_factor * jnp.einsum(
            "uqy,yut->qut",
            key_side_inverse_gradient,
            key_row_block,
            preferred_element_type=jnp.float32,
        )
        grad_keys = scores_scale_factor * jnp.einsum(
            "kqy,qkx->ykx",
            key_side_inverse_gradient,
            query_landmarks,
            preferred_element_type=jnp.float32,
        )
        grad_values = (
            jnp.einsum(
                "kqy,qkx->ykx",
                key_side_inverse,
                value_landmarks_inverse,
                preferred_element_type=jnp.float32,
            ).reshape(length_local, local_width)
            + conv_values
        )
        query_mark_grad = lax.psum(query_mark_part, "seq") + chain_query
        key_mark_grad = key_mark_part + chain_key
        spread = (
            jnp.stack([query_mark_grad, key_mark_grad]).reshape(2, mark_count, local_width)
            / seg_sizes[None, :, None]
        )
        returned = jnp.einsum(
            "ml,kmc->klc", member.astype(jnp.float32), spread, precision=FULL_PRECISION
        )
        grad_projected = jnp.stack(
            [
                grad_query.reshape(length_local, local_width) + returned[0],
                grad_keys.reshape(length_local, local_width) + returned[1],
                grad_values * mask_float[:, None],
            ]
        ).astype(jnp.bfloat16)
        grad_normed = lax.psum(
            jnp.einsum(
                "klc,kdc->ld", grad_projected, w_in, preferred_element_type=jnp.float32
            ).astype(jnp.bfloat16),
            "head",
        ).astype(jnp.float32)
        grad_in = jnp.einsum(
            "ld,klc->kdc", normed, grad_projected, preferred_element_type=jnp.float32
        )
        grad_standard = grad_normed * ln_gain
        grad_inputs = (
            inv_std
            * (
                grad_standard
                - jnp.mean(grad_standard, axis=-1, keepdims=True)
                - standard * jnp.mean(grad_standard * standard, axis=-1, keepdims=True)
            )
            + grad_hidden
        )
        grad_in, grad_back = shard_grads(grad_in, grad_back)
        acc_in, acc_back, small_grads = running
        slide_small = (
            jnp.sum(grad_normed * standard, axis=0),
            jnp.sum(grad_normed, axis=0),
            grad_taps,
            jnp.sum(grad_hidden, axis=0),
            grad_kernel,
            jnp.sum(grad_out, axis=0),
        )
        small_grads = jax.tree.map(lambda former, latter: former + latter, small_grads, slide_small)
        running = (acc_in + grad_in, acc_back + grad_back, small_grads)
        return (running, (result.astype(jnp.bfloat16), grad_inputs))

    start_in = jnp.zeros(w_qkv.shape, jnp.float32)
    start_back = jnp.zeros(w_out.shape, jnp.float32)
    start_small = (
        jnp.zeros((model_width,), jnp.float32),
        jnp.zeros((model_width,), jnp.float32),
        jnp.zeros(conv_taps.shape, jnp.float32),
        jnp.zeros((model_width,), jnp.float32),
        jnp.zeros(combined.shape, jnp.float32),
        jnp.zeros((model_width,), jnp.float32),
    )
    final, stacked = lax.scan(
        one_slide, (start_in, start_back, start_small), (tokens, cotangent, counts)
    )
    acc_in, acc_back, small_grads = final
    grad_w_qkv, grad_w_out = (acc_in, acc_back)
    grad_gain, grad_bias, grad_taps, grad_obias, grad_kernel, grad_pbias = lax.psum(
        (
            small_grads[0],
            small_grads[1],
            small_grads[2],
            small_grads[3],
            small_grads[4],
            small_grads[5],
        ),
        "seq",
    )
    return (
        stacked[0],
        stacked[1],
        grad_gain,
        grad_bias,
        grad_w_qkv,
        grad_taps,
        grad_w_out,
        grad_obias,
        grad_kernel,
        grad_kernel[1:6, 1:6],
        grad_kernel[2:5, 2:5],
        grad_pbias,
    )


def solution(mesh):
    placed = (
        P(None, "seq", None),
        P(),
        P(),
        P(),
        P(None, "seq", "head"),
        P("head", None),
        P("head", "seq"),
        P(),
        P(),
        P(),
        P(),
        P(),
        P(None, "seq", None),
    )
    return jax.shard_map(
        shards,
        mesh=mesh,
        in_specs=placed,
        out_specs=(
            P(None, "seq", None),
            P(None, "seq", None),
            P(),
            P(),
            P(None, "seq", "head"),
            P("head", None),
            P("head", "seq"),
            P(),
            P(),
            P(),
            P(),
            P(),
        ),
        check_vma=False,
    )
```

profile of v0, /device:TPU:0, one launch (start us, length us, event | category | flops | bytes accessed | tf_op | source)
XLA Modules:
  0.0 1871.0 jit_solution(17815985552110019939)
XLA Ops:
  12.1 1737.6 %while.83 = (s32[]{:T(128)}, f32[3,32,256]{2,0,1:T(4,128)}, f32[256,32]{0,1:T(8,128)}, f32[512]{0:T(512)}, f32[512]{0:T(512)}, /*index=5*/f32[4,33]{0,1:T(8,128)...) while((s32[]{:T(128)}, f32[3,32,256]{2,0,1:T(4,128)}, ...), condition=%wide.region_37.38_spmd.clone.clone, body=%wide.region_0.37_spmd.clone.clone.sunk | while | flops 56492851200 | bytes 719289024 | solution.py:393
  15.3 6.2 collective-permute-start.1
  24.0 44.2 %all_gather.83 = bf16[3,512,256]{2,1,0:T(8,128)(2,1)S(1)} all-gather(bf16[3,32,256]{2,1,0:T(8,128)(2,1)} %get-tuple-element.1660), channel_id=1, replica_groups=mesh['seq'=16,'head'=2] {'seq'}, dimensions={1}, use_global_device_ids=true | all-gather | bytes 835584 | tf_op jit(solution)/shard_map/while/body/eval_jaxpr/all_gather | solution.py:147
  73.3 4.5 collective-permute-start.5
  78.7 37.4 %all_gather.82 = bf16[256,512]{0,1:T(8,128)(2,1)S(1)} all-gather(bf16[256,32]{0,1:T(8,128)(2,1)S(1)} %copy-done.137), channel_id=1, replica_groups=mesh['seq'=16,'head'=2] {'seq'}, dimensions={1}, use_global_device_ids=true | all-gather | bytes 278528 | tf_op jit(solution)/shard_map/while/body/eval_jaxpr/all_gather | solution.py:148
  131.3 4.5 collective-permute-start.3
  140.4 35.1 %all-reduce.26.cloned.1.call-done = f32[2,256,256]{1,2,0:T(8,128)} async-done(((f32[2,256,256]{1,2,0:T(8,128)}), f32[2,256,256]{1,2,0:T(8,128)}) %all-reduce.26.cloned.1.call-update) | async-done | bytes 524304 | tf_op jit(solution)/shard_map/while/body/eval_jaxpr/psum | solution.py:168
  177.1 39.0 %all-gather.8 = f32[16,4,256]{2,1,0:T(4,128)S(1)} all-gather(f32[1,4,256]{2,1,0:T(4,128)S(1)} %bitcast.910), channel_id=2, replica_groups=mesh['seq'=16,'head'=2] {'seq'}, dimensions={0}, use_global_device_ids=true | all-gather | bytes 69632 | tf_op jit(solution)/shard_map/while/body/eval_jaxpr/all_gather | solution.py:16
  216.5 36.1 %all-gather.9 = f32[16,4,256]{2,1,0:T(4,128)S(1)} all-gather(f32[1,4,256]{2,1,0:T(4,128)S(1)} %bitcast.912), channel_id=3, replica_groups=mesh['seq'=16,'head'=2] {'seq'}, dimensions={0}, use_global_device_ids=true | all-gather | bytes 69632 | tf_op jit(solution)/shard_map/while/body/eval_jaxpr/all_gather | solution.py:16
  264.9 4.6 online-softmax
  269.6 2.8 fusion.904
  274.6 3.1 convolution_multiply_fusion.27
  277.7 5.3 online-softmax.1
  290.2 4.6 online-softmax.2
  294.8 3.0 fusion.907
  302.1 4.6 online-softmax.3
  306.7 3.0 fusion.908
  314.1 4.8 online-softmax.4
  318.9 2.9 fusion.909
  326.2 4.6 online-softmax.5
  330.8 3.9 fusion.910
  339.1 3.0 convolution_subtract_fusion.18
  345.3 101.0 %all-reduce.28.cloned.1.call-done = (f32[4,64,256]{2,1,0:T(8,128)}, f32[256,4,64]{0,2,1:T(8,128)}, f32[256,4,64]{0,2,1:T(8,128)}) async-done(((f32[4,64,256]{2,1,0:T(8,128)}, f32[256,4,64]{0,2,1:T(8,128)}, f32[256,4,64]{0,2,1:T(8,128)}), (f32[4,64,256]{2,1,0:T(8,128)}, f32[256,4,64]{0,2,1:T(8,128)}, f32[256,4,64]{0,2,1:T(8,128)})) %all-reduce.28.cloned.1.call-update) | async-done | bytes 786448 | tf_op jit(solution)/shard_map/while/body/eval_jaxpr/psum | solution.py:284
  528.3 2.9 fusion.946
  540.5 3.0 fusion.947
  548.8 99.3 %all-reduce.30.cloned.1.call-done = (f32[256,4,64]{0,2,1:T(8,128)}, f32[256,4,64]{0,2,1:T(8,128)}) async-done(((f32[256,4,64]{0,2,1:T(8,128)}, f32[256,4,64]{0,2,1:T(8,128)}), (f32[256,4,64]{0,2,1:T(8,128)}, f32[256,4,64]{0,2,1:T(8,128)})) %all-reduce.30.cloned.1.call-update) | async-done | bytes 524304 | tf_op jit(solution)/shard_map/while/body/eval_jaxpr/psum | solution.py:284
  656.0 6.5 convolution_reduce_fusion.2
  665.3 6.3 all-reduce.34.cloned.1.call-done
  674.0 4.7 collective-permute-start.7
  678.7 73.4 %reduce-scatter.2.cloned.1.call-done = f32[256,32]{0,1:T(8,128)} async-done(((f32[256,512]{0,1:T(8,128)}), f32[256,32]{0,1:T(8,128)}) %reduce-scatter.2.cloned.1.call-update) | async-done | bytes 32784 | tf_op jit(solution)/shard_map/while/body/eval_jaxpr/reduce_scatter | solution.py:104
  755.5 21.1 %fusion.962 = f32[7,7,1,512]{3,2,1,0:T(1,128)S(1)} fusion(bf16[1,10,70,512]{3,2,1,0:T(8,128)(2,1)S(1)} %copy-done.105, bf16[1,4,64,512]{3,2,1,0:T(8,128)(2,1)S(1)} %bitcast.875), kind=kOutput, calls=%fused_computation.41.clone.1 | convolution fusion | flops 12845056 | bytes 1079296 | tf_op jit(solution)/shard_map/while/body/eval_jaxpr/transpose(jvp())/conv_general_dilated | solution.py:68
  781.6 98.2 %all-reduce.32.cloned.1.call-done = f32[3,512,256]{2,0,1:T(4,128)} async-done(((f32[3,512,256]{2,0,1:T(4,128)}), f32[3,512,256]{2,0,1:T(4,128)}) %all-reduce.32.cloned.1.call-update) | async-done | bytes 1572880 | tf_op jit(solution)/shard_map/while
  884.9 5.2 collective-permute-start.1
  892.7 42.7 %all_gather.83 = bf16[3,512,256]{2,1,0:T(8,128)(2,1)S(1)} all-gather(bf16[3,32,256]{2,1,0:T(8,128)(2,1)} %get-tuple-element.1660), channel_id=1, replica_groups=mesh['seq'=16,'head'=2] {'seq'}, dimensions={1}, use_global_device_ids=true | all-gather | bytes 835584 | tf_op jit(solution)/shard_map/while/body/eval_jaxpr/all_gather | solution.py:147
  940.5 4.5 collective-permute-start.5
  945.8 38.1 %all_gather.82 = bf16[256,512]{0,1:T(8,128)(2,1)S(1)} all-gather(bf16[256,32]{0,1:T(8,128)(2,1)S(1)} %copy-done.137), channel_id=1, replica_groups=mesh['seq'=16,'head'=2] {'seq'}, dimensions={1}, use_global_device_ids=true | all-gather | bytes 278528 | tf_op jit(solution)/shard_map/while/body/eval_jaxpr/all_gather | solution.py:148
  999.2 4.5 collective-permute-start.3
  1008.2 34.5 %all-reduce.26.cloned.1.call-done = f32[2,256,256]{1,2,0:T(8,128)} async-done(((f32[2,256,256]{1,2,0:T(8,128)}), f32[2,256,256]{1,2,0:T(8,128)}) %all-reduce.26.cloned.1.call-update) | async-done | bytes 524304 | tf_op jit(solution)/shard_map/while/body/eval_jaxpr/psum | solution.py:168
  1044.4 39.0 %all-gather.8 = f32[16,4,256]{2,1,0:T(4,128)S(1)} all-gather(f32[1,4,256]{2,1,0:T(4,128)S(1)} %bitcast.910), channel_id=2, replica_groups=mesh['seq'=16,'head'=2] {'seq'}, dimensions={0}, use_global_device_ids=true | all-gather | bytes 69632 | tf_op jit(solution)/shard_map/while/body/eval_jaxpr/all_gather | solution.py:16
  1083.8 36.0 %all-gather.9 = f32[16,4,256]{2,1,0:T(4,128)S(1)} all-gather(f32[1,4,256]{2,1,0:T(4,128)S(1)} %bitcast.912), channel_id=3, replica_groups=mesh['seq'=16,'head'=2] {'seq'}, dimensions={0}, use_global_device_ids=true | all-gather | bytes 69632 | tf_op jit(solution)/shard_map/while/body/eval_jaxpr/all_gather | solution.py:16
  1132.1 4.6 online-softmax
  1141.8 3.1 convolution_multiply_fusion.27
  1144.9 5.1 online-softmax.1
  1157.2 4.6 online-softmax.2
  1161.8 3.0 fusion.907
  1169.1 4.6 online-softmax.3
  1173.7 3.0 fusion.908
  1181.1 4.8 online-softmax.4
  1185.9 2.9 fusion.909
  1193.2 4.6 online-softmax.5
  1197.8 3.9 fusion.910
  1206.1 3.0 convolution_subtract_fusion.18
  1212.3 101.0 %all-reduce.28.cloned.1.call-done = (f32[4,64,256]{2,1,0:T(8,128)}, f32[256,4,64]{0,2,1:T(8,128)}, f32[256,4,64]{0,2,1:T(8,128)}) async-done(((f32[4,64,256]{2,1,0:T(8,128)}, f32[256,4,64]{0,2,1:T(8,128)}, f32[256,4,64]{0,2,1:T(8,128)}), (f32[4,64,256]{2,1,0:T(8,128)}, f32[256,4,64]{0,2,1:T(8,128)}, f32[256,4,64]{0,2,1:T(8,128)})) %all-reduce.28.cloned.1.call-update) | async-done | bytes 786448 | tf_op jit(solution)/shard_map/while/body/eval_jaxpr/psum | solution.py:284
  1395.3 2.9 fusion.946
  1407.5 3.0 fusion.947
  1415.8 99.2 %all-reduce.30.cloned.1.call-done = (f32[256,4,64]{0,2,1:T(8,128)}, f32[256,4,64]{0,2,1:T(8,128)}) async-done(((f32[256,4,64]{0,2,1:T(8,128)}, f32[256,4,64]{0,2,1:T(8,128)}), (f32[256,4,64]{0,2,1:T(8,128)}, f32[256,4,64]{0,2,1:T(8,128)})) %all-reduce.30.cloned.1.call-update) | async-done | bytes 524304 | tf_op jit(solution)/shard_map/while/body/eval_jaxpr/psum | solution.py:284
  1523.0 6.5 convolution_reduce_fusion.2
  1532.3 6.3 all-reduce.34.cloned.1.call-done
  1541.0 4.7 collective-permute-start.7
  1545.7 73.3 %reduce-scatter.2.cloned.1.call-done = f32[256,32]{0,1:T(8,128)} async-done(((f32[256,512]{0,1:T(8,128)}), f32[256,32]{0,1:T(8,128)}) %reduce-scatter.2.cloned.1.call-update) | async-done | bytes 32784 | tf_op jit(solution)/shard_map/while/body/eval_jaxpr/reduce_scatter | solution.py:104
  1622.4 21.1 %fusion.962 = f32[7,7,1,512]{3,2,1,0:T(1,128)S(1)} fusion(bf16[1,10,70,512]{3,2,1,0:T(8,128)(2,1)S(1)} %copy-done.105, bf16[1,4,64,512]{3,2,1,0:T(8,128)(2,1)S(1)} %bitcast.875), kind=kOutput, calls=%fused_computation.41.clone.1 | convolution fusion | flops 12845056 | bytes 1079296 | tf_op jit(solution)/shard_map/while/body/eval_jaxpr/transpose(jvp())/conv_general_dilated | solution.py:68
  1648.5 98.2 %all-reduce.32.cloned.1.call-done = f32[3,512,256]{2,0,1:T(4,128)} async-done(((f32[3,512,256]{2,0,1:T(4,128)}), f32[3,512,256]{2,0,1:T(4,128)}) %all-reduce.32.cloned.1.call-update) | async-done | bytes 1572880 | tf_op jit(solution)/shard_map/while
  1752.7 75.2 %all-reduce.8 = (f32[512]{0:T(512)}, f32[512]{0:T(512)}, f32[4,33]{1,0:T(4,128)}, f32[512]{0:T(512)}, f32[512]{0:T(512)}) all-reduce(f32[512]{0:T(512)} %get-tuple-element.886, f32[512]{0:T(512)} %get-tuple-element.887, f32[4,33]{1,0:T(4,128)S(1)} %copy.219, f32[512]{0:T(512)} %get-tuple-element.891, ...), channel_id=1, replica_groups=mesh['seq'=16,'head'=2] {'seq'}, use_global_device_ids=true, to_apply=%region_38.39 | all-reduce | flops 2180 | bytes 17440 | tf_op jit(solution)/shard_map/psum | solution.py:398
  1827.9 31.0 %all-reduce.24.cloned.1.call-done = f32[7,7,512]{2,1,0:T(8,128)} async-done(((f32[7,7,512]{2,1,0:T(8,128)}), f32[7,7,512]{2,1,0:T(8,128)}) %all-reduce.24.cloned.1.call-update) | async-done | bytes 100368 | tf_op jit(solution)/shard_map/psum | solution.py:398
  (1222 shorter events, 397.9 us)
Async XLA Ops:
  12.1 106.5 %copy-start.123 = (f32[33,4]{1,0:T(8,128)}, f32[33,4]{1,0:T(8,128)S(1)}, u32[]{:S(2)}) copy-start(f32[33,4]{1,0:T(8,128)S(1)} %get-tuple-element.1670) | copy-start | bytes 1588 | tf_op jit(solution)/shard_map/while
  12.1 56.2 %copy-start.57 = (bf16[2,256,512]{2,1,0:T(8,128)(2,1)S(1)}, bf16[2,256,512]{2,1,0:T(8,128)(2,1)}, u32[]{:S(2)}) copy-start(bf16[2,256,512]{2,1,0:T(8,128)(2,1)} %get-tuple-element.1657) | copy-start | bytes 1572868 | tf_op jit(solution)/shard_map/while
  12.1 57.3 %copy-start.132 = (f32[512]{0:T(512)S(1)}, f32[512]{0:T(512)}, u32[]{:S(2)}) copy-start(f32[512]{0:T(512)} %get-tuple-element.1658) | copy-start | bytes 6148 | tf_op jit(solution)/shard_map/while
  12.1 57.3 %copy-start.172 = (f32[512]{0:T(512)S(1)}, f32[512]{0:T(512)}, u32[]{:S(2)}) copy-start(f32[512]{0:T(512)} %get-tuple-element.1659) | copy-start | bytes 6148 | tf_op jit(solution)/shard_map/while
  12.1 163.4 %all-reduce.26.cloned.1.call-start = ((), (), s32[]{:S(2)}) async-start(), calls=%async_computation.2 | async-start | bytes 1048576 | tf_op jit(solution)/shard_map/while/body/eval_jaxpr/psum | solution.py:168
  14.0 107.7 %collective-permute-start = (bf16[3,64,512]{2,1,0:T(8,128)(2,1)}, bf16[3,64,512]{2,1,0:T(8,128)(2,1)}, u32[]{:S(2)}, u32[]{:S(2)}) collective-permute-start(bf16[3,64,512]{2,1,0:T(8,128)(2,1)} %bitcast.844), channel_id=1, source_target_pairs={{2,0},{4,2},{6,4},{8,6},{10,8},{12,10},{14,12},{16,14},{18,16},{20... | collective-permute-start | bytes 589832 | tf_op jit(solution)/shard_map/while/body/eval_jaxpr/ppermute | solution.py:36
  15.3 106.4 %collective-permute-start.1 = (bf16[3,64,512]{2,1,0:T(8,128)(2,1)}, bf16[3,64,512]{2,1,0:T(8,128)(2,1)}, u32[]{:S(2)}, u32[]{:S(2)}) collective-permute-start(bf16[3,64,512]{2,1,0:T(8,128)(2,1)} %bitcast.846), channel_id=1, source_target_pairs={{0,2},{2,4},{4,6},{6,8},{8,10},{10,12},{12,14},{14,16},{16,18},{18... | collective-permute-start | bytes 589832 | tf_op jit(solution)/shard_map/while/body/eval_jaxpr/ppermute | solution.py:34
  24.0 93.3 %copy-start.145 = (pred[256]{0:T(512)(128)(4,1)}, pred[256]{0:T(512)(128)(4,1)S(1)}, u32[]{:S(2)}) copy-start(pred[256]{0:T(512)(128)(4,1)S(1)} %get-tuple-element.1469) | copy-start | bytes 772 | tf_op jit(solution)/shard_map/while
  71.1 375.1 %all-reduce.28.cloned.1.call-start = ((), (), s32[]{:S(2)}) async-start(), calls=%async_computation.3 | async-start | bytes 1572864 | tf_op jit(solution)/shard_map/while/body/eval_jaxpr/psum | solution.py:284
  72.0 47.4 %collective-permute-start.4 = (bf16[16,256]{0,1:T(8,128)(2,1)S(1)}, bf16[16,256]{0,1:T(8,128)(2,1)S(1)}, u32[]{:S(2)}, u32[]{:S(2)}) collective-permute-start(bf16[16,256]{0,1:T(8,128)(2,1)S(1)} %bitcast.907), channel_id=1, source_target_pairs={{2,0},{4,2},{6,4},{8,6},{10,8},{12,10},{14,12},{16,14},{18,16},{20... | collective-permute-start | bytes 24584 | tf_op jit(solution)/shard_map/while/body/eval_jaxpr/ppermute | solution.py:36
  73.3 46.1 %collective-permute-start.5 = (bf16[16,256]{0,1:T(8,128)(2,1)S(1)}, bf16[16,256]{0,1:T(8,128)(2,1)S(1)}, u32[]{:S(2)}, u32[]{:S(2)}) collective-permute-start(bf16[16,256]{0,1:T(8,128)(2,1)S(1)} %bitcast.906), channel_id=1, source_target_pairs={{0,2},{2,4},{4,6},{6,8},{8,10},{10,12},{12,14},{14,16},{16,18},{18... | collective-permute-start | bytes 24584 | tf_op jit(solution)/shard_map/while/body/eval_jaxpr/ppermute | solution.py:34
  78.6 204.3 %copy-start.21 = (f32[256,256]{1,0:T(8,128)}, f32[256,256]{1,0:T(8,128)S(1)}, u32[]{:S(2)}) copy-start(f32[256,256]{1,0:T(8,128)S(1)} %fusion.903) | copy-start | bytes 786436 | tf_op jit(solution)/shard_map/while
  78.6 193.8 %copy-start.22 = (f32[256,256]{1,0:T(8,128)}, f32[256,256]{1,0:T(8,128)S(1)}, u32[]{:S(2)}) copy-start(f32[256,256]{1,0:T(8,128)S(1)} %fusion.905) | copy-start | bytes 786436 | tf_op jit(solution)/shard_map/while
  130.0 8.4 collective-permute-start.2
  131.3 7.1 collective-permute-start.3
  176.6 80.9 %copy-start.75 = (bf16[1,256,256]{1,2,0:T(8,128)(2,1)}, bf16[1,256,256]{1,2,0:T(8,128)(2,1)S(1)}, u32[]{:S(2)}) copy-start(bf16[1,256,256]{1,2,0:T(8,128)(2,1)S(1)} %get-tuple-element.1481) | copy-start | bytes 393220 | tf_op jit(solution)/shard_map/while
  176.6 76.7 %copy-start.107 = (bf16[256,4,64]{0,2,1:T(8,128)(2,1)S(1)}, bf16[256,4,64]{0,2,1:T(8,128)(2,1)}, u32[]{:S(2)}) copy-start(bf16[256,4,64]{0,2,1:T(8,128)(2,1)} %copy-done.106) | copy-start | bytes 393220 | tf_op jit(solution)/shard_map/while
  177.1 77.4 %copy-start.61 = (f32[4,256,256]{2,1,0:T(8,128)}, f32[4,256,256]{2,1,0:T(8,128)S(1)}, u32[]{:S(2)}) copy-start(f32[4,256,256]{2,1,0:T(8,128)S(1)} %get-tuple-element.1483) | copy-start | bytes 3145732 | tf_op jit(solution)/shard_map/while
  337.1 311.0 %all-reduce.30.cloned.1.call-start = ((), (), s32[]{:S(2)}) async-start(), calls=%async_computation.4 | async-start | bytes 1048576 | tf_op jit(solution)/shard_map/while/body/eval_jaxpr/psum | solution.py:284
  540.4 131.2 %all-reduce.34.cloned.1.call-start = ((), (), s32[]{:S(2)}) async-start(), calls=%async_computation.7 | async-start | bytes 1048576 | tf_op jit(solution)/shard_map/while/body/eval_jaxpr/psum | solution.py:350
  653.7 98.4 %reduce-scatter.2.cloned.1.call-start = ((), (), s32[]{:S(2)}) async-start(), calls=%async_computation.6 | async-start | bytes 557056 | tf_op jit(solution)/shard_map/while/body/eval_jaxpr/reduce_scatter | solution.py:104
  655.4 224.4 %all-reduce.32.cloned.1.call-start = ((), (), s32[]{:S(2)}) async-start(), calls=%async_computation.5 | async-start | bytes 4194304 | tf_op jit(solution)/shard_map/while
  665.3 86.9 %copy-start.126 = (f32[256,32]{0,1:T(8,128)S(1)}, f32[256,32]{0,1:T(8,128)}, u32[]{:S(2)}) copy-start(f32[256,32]{0,1:T(8,128)} %get-tuple-element.1610) | copy-start | bytes 98308 | tf_op jit(solution)/shard_map/while
  672.7 80.2 %collective-permute-start.6 = (bf16[3,64,512]{2,1,0:T(8,128)(2,1)S(1)}, bf16[3,64,512]{2,1,0:T(8,128)(2,1)S(1)}, u32[]{:S(2)}, u32[]{:S(2)}) collective-permute-start(bf16[3,64,512]{2,1,0:T(8,128)(2,1)S(1)} %bitcast.902), channel_id=1, source_target_pairs={{2,0},{4,2},{6,4},{8,6},{10,8},{12,10},{14,12},{16,14},{18,16},{20... | collective-permute-start | bytes 589832 | tf_op jit(solution)/shard_map/while/body/eval_jaxpr/ppermute | solution.py:36
  674.0 78.9 %collective-permute-start.7 = (bf16[3,64,512]{2,1,0:T(8,128)(2,1)S(1)}, bf16[3,64,512]{2,1,0:T(8,128)(2,1)S(1)}, u32[]{:S(2)}, u32[]{:S(2)}) collective-permute-start(bf16[3,64,512]{2,1,0:T(8,128)(2,1)S(1)} %bitcast.901), channel_id=1, source_target_pairs={{0,2},{2,4},{4,6},{6,8},{8,10},{10,12},{12,14},{14,16},{16,18},{18... | collective-permute-start | bytes 589832 | tf_op jit(solution)/shard_map/while/body/eval_jaxpr/ppermute | solution.py:34
  780.7 99.1 %copy-start.116 = (f32[3,32,256]{2,0,1:T(4,128)S(1)}, f32[3,32,256]{2,0,1:T(4,128)}, u32[]{:S(2)}) copy-start(f32[3,32,256]{2,0,1:T(4,128)} %get-tuple-element.1609) | copy-start | bytes 294916 | tf_op jit(solution)/shard_map/while
  780.7 100.8 %copy-start.124 = (f32[33,4]{1,0:T(8,128)S(1)}, f32[33,4]{1,0:T(8,128)}, u32[]{:S(2)}) copy-start(f32[33,4]{1,0:T(8,128)} %copy-done.123) | copy-start | bytes 1588 | tf_op jit(solution)/shard_map/while
  780.7 100.1 %copy-start.159 = (f32[512]{0:T(512)}, f32[512]{0:T(512)S(1)}, u32[]{:S(2)}) copy-start(f32[512]{0:T(512)S(1)} %get-tuple-element.1649) | copy-start | bytes 6148 | tf_op jit(solution)/shard_map/while
  780.8 100.1 %copy-start.161 = (f32[512]{0:T(512)}, f32[512]{0:T(512)S(1)}, u32[]{:S(2)}) copy-start(f32[512]{0:T(512)S(1)} %get-tuple-element.1650) | copy-start | bytes 6148 | tf_op jit(solution)/shard_map/while
  780.8 100.1 %copy-start.119 = (f32[7,7,512]{2,1,0:T(8,128)}, f32[7,7,512]{2,1,0:T(8,128)S(1)}, u32[]{:S(2)}) copy-start(f32[7,7,512]{2,1,0:T(8,128)S(1)} %bitcast_add_fusion.9) | copy-start | bytes 301060 | tf_op jit(solution)/shard_map/while
  780.9 100.0 %copy-start.180 = (bf16[2,256,512]{2,1,0:T(8,128)(2,1)}, bf16[2,256,512]{2,1,0:T(8,128)(2,1)S(1)}, u32[]{:S(2)}) copy-start(bf16[2,256,512]{2,1,0:T(8,128)(2,1)S(1)} %bitcast_dynamic-update-slice_fusion.2) | copy-start | bytes 1572868 | tf_op jit(solution)/shard_map/while
  781.6 99.3 %copy-start.178 = (f32[2,256,512]{2,1,0:T(8,128)}, f32[2,256,512]{2,1,0:T(8,128)S(1)}, u32[]{:S(2)}) copy-start(f32[2,256,512]{2,1,0:T(8,128)S(1)} %fusion.963) | copy-start | bytes 3145732 | tf_op jit(solution)/shard_map/while
  881.7 104.8 %copy-start.123 = (f32[33,4]{1,0:T(8,128)}, f32[33,4]{1,0:T(8,128)S(1)}, u32[]{:S(2)}) copy-start(f32[33,4]{1,0:T(8,128)S(1)} %get-tuple-element.1670) | copy-start | bytes 1588 | tf_op jit(solution)/shard_map/while
  881.7 54.8 %copy-start.132 = (f32[512]{0:T(512)S(1)}, f32[512]{0:T(512)}, u32[]{:S(2)}) copy-start(f32[512]{0:T(512)} %get-tuple-element.1658) | copy-start | bytes 6148 | tf_op jit(solution)/shard_map/while
  881.7 54.8 %copy-start.172 = (f32[512]{0:T(512)S(1)}, f32[512]{0:T(512)}, u32[]{:S(2)}) copy-start(f32[512]{0:T(512)} %get-tuple-element.1659) | copy-start | bytes 6148 | tf_op jit(solution)/shard_map/while
  881.7 161.1 %all-reduce.26.cloned.1.call-start = ((), (), s32[]{:S(2)}) async-start(), calls=%async_computation.2 | async-start | bytes 1048576 | tf_op jit(solution)/shard_map/while/body/eval_jaxpr/psum | solution.py:168
  883.6 106.0 %collective-permute-start = (bf16[3,64,512]{2,1,0:T(8,128)(2,1)}, bf16[3,64,512]{2,1,0:T(8,128)(2,1)}, u32[]{:S(2)}, u32[]{:S(2)}) collective-permute-start(bf16[3,64,512]{2,1,0:T(8,128)(2,1)} %bitcast.844), channel_id=1, source_target_pairs={{2,0},{4,2},{6,4},{8,6},{10,8},{12,10},{14,12},{16,14},{18,16},{20... | collective-permute-start | bytes 589832 | tf_op jit(solution)/shard_map/while/body/eval_jaxpr/ppermute | solution.py:36
  884.9 104.7 %collective-permute-start.1 = (bf16[3,64,512]{2,1,0:T(8,128)(2,1)}, bf16[3,64,512]{2,1,0:T(8,128)(2,1)}, u32[]{:S(2)}, u32[]{:S(2)}) collective-permute-start(bf16[3,64,512]{2,1,0:T(8,128)(2,1)} %bitcast.846), channel_id=1, source_target_pairs={{0,2},{2,4},{4,6},{6,8},{8,10},{10,12},{12,14},{14,16},{16,18},{18... | collective-permute-start | bytes 589832 | tf_op jit(solution)/shard_map/while/body/eval_jaxpr/ppermute | solution.py:34
  892.7 92.5 %copy-start.145 = (pred[256]{0:T(512)(128)(4,1)}, pred[256]{0:T(512)(128)(4,1)S(1)}, u32[]{:S(2)}) copy-start(pred[256]{0:T(512)(128)(4,1)S(1)} %get-tuple-element.1469) | copy-start | bytes 772 | tf_op jit(solution)/shard_map/while
  938.3 375.0 %all-reduce.28.cloned.1.call-start = ((), (), s32[]{:S(2)}) async-start(), calls=%async_computation.3 | async-start | bytes 1572864 | tf_op jit(solution)/shard_map/while/body/eval_jaxpr/psum | solution.py:284
  939.2 48.1 %collective-permute-start.4 = (bf16[16,256]{0,1:T(8,128)(2,1)S(1)}, bf16[16,256]{0,1:T(8,128)(2,1)S(1)}, u32[]{:S(2)}, u32[]{:S(2)}) collective-permute-start(bf16[16,256]{0,1:T(8,128)(2,1)S(1)} %bitcast.907), channel_id=1, source_target_pairs={{2,0},{4,2},{6,4},{8,6},{10,8},{12,10},{14,12},{16,14},{18,16},{20... | collective-permute-start | bytes 24584 | tf_op jit(solution)/shard_map/while/body/eval_jaxpr/ppermute | solution.py:36
  940.5 46.8 %collective-permute-start.5 = (bf16[16,256]{0,1:T(8,128)(2,1)S(1)}, bf16[16,256]{0,1:T(8,128)(2,1)S(1)}, u32[]{:S(2)}, u32[]{:S(2)}) collective-permute-start(bf16[16,256]{0,1:T(8,128)(2,1)S(1)} %bitcast.906), channel_id=1, source_target_pairs={{0,2},{2,4},{4,6},{6,8},{8,10},{10,12},{12,14},{14,16},{16,18},{18... | collective-permute-start | bytes 24584 | tf_op jit(solution)/shard_map/while/body/eval_jaxpr/ppermute | solution.py:34
  945.7 204.2 %copy-start.21 = (f32[256,256]{1,0:T(8,128)}, f32[256,256]{1,0:T(8,128)S(1)}, u32[]{:S(2)}) copy-start(f32[256,256]{1,0:T(8,128)S(1)} %fusion.903) | copy-start | bytes 786436 | tf_op jit(solution)/shard_map/while
  945.8 193.8 %copy-start.22 = (f32[256,256]{1,0:T(8,128)}, f32[256,256]{1,0:T(8,128)S(1)}, u32[]{:S(2)}) copy-start(f32[256,256]{1,0:T(8,128)S(1)} %fusion.905) | copy-start | bytes 786436 | tf_op jit(solution)/shard_map/while
  997.9 8.4 collective-permute-start.2
  999.2 7.1 collective-permute-start.3
  1043.9 80.7 %copy-start.75 = (bf16[1,256,256]{1,2,0:T(8,128)(2,1)}, bf16[1,256,256]{1,2,0:T(8,128)(2,1)S(1)}, u32[]{:S(2)}) copy-start(bf16[1,256,256]{1,2,0:T(8,128)(2,1)S(1)} %get-tuple-element.1481) | copy-start | bytes 393220 | tf_op jit(solution)/shard_map/while
  1043.9 76.6 %copy-start.107 = (bf16[256,4,64]{0,2,1:T(8,128)(2,1)S(1)}, bf16[256,4,64]{0,2,1:T(8,128)(2,1)}, u32[]{:S(2)}) copy-start(bf16[256,4,64]{0,2,1:T(8,128)(2,1)} %copy-done.106) | copy-start | bytes 393220 | tf_op jit(solution)/shard_map/while
  1044.4 77.3 %copy-start.61 = (f32[4,256,256]{2,1,0:T(8,128)}, f32[4,256,256]{2,1,0:T(8,128)S(1)}, u32[]{:S(2)}) copy-start(f32[4,256,256]{2,1,0:T(8,128)S(1)} %get-tuple-element.1483) | copy-start | bytes 3145732 | tf_op jit(solution)/shard_map/while
  1204.1 310.9 %all-reduce.30.cloned.1.call-start = ((), (), s32[]{:S(2)}) async-start(), calls=%async_computation.4 | async-start | bytes 1048576 | tf_op jit(solution)/shard_map/while/body/eval_jaxpr/psum | solution.py:284
  1407.3 131.2 %all-reduce.34.cloned.1.call-start = ((), (), s32[]{:S(2)}) async-start(), calls=%async_computation.7 | async-start | bytes 1048576 | tf_op jit(solution)/shard_map/while/body/eval_jaxpr/psum | solution.py:350
  1520.7 98.3 %reduce-scatter.2.cloned.1.call-start = ((), (), s32[]{:S(2)}) async-start(), calls=%async_computation.6 | async-start | bytes 557056 | tf_op jit(solution)/shard_map/while/body/eval_jaxpr/reduce_scatter | solution.py:104
  1522.4 224.3 %all-reduce.32.cloned.1.call-start = ((), (), s32[]{:S(2)}) async-start(), calls=%async_computation.5 | async-start | bytes 4194304 | tf_op jit(solution)/shard_map/while
  1532.2 86.8 %copy-start.126 = (f32[256,32]{0,1:T(8,128)S(1)}, f32[256,32]{0,1:T(8,128)}, u32[]{:S(2)}) copy-start(f32[256,32]{0,1:T(8,128)} %get-tuple-element.1610) | copy-start | bytes 98308 | tf_op jit(solution)/shard_map/while
  1539.7 80.1 %collective-permute-start.6 = (bf16[3,64,512]{2,1,0:T(8,128)(2,1)S(1)}, bf16[3,64,512]{2,1,0:T(8,128)(2,1)S(1)}, u32[]{:S(2)}, u32[]{:S(2)}) collective-permute-start(bf16[3,64,512]{2,1,0:T(8,128)(2,1)S(1)} %bitcast.902), channel_id=1, source_target_pairs={{2,0},{4,2},{6,4},{8,6},{10,8},{12,10},{14,12},{16,14},{18,16},{20... | collective-permute-start | bytes 589832 | tf_op jit(solution)/shard_map/while/body/eval_jaxpr/ppermute | solution.py:36
  1541.0 78.8 %collective-permute-start.7 = (bf16[3,64,512]{2,1,0:T(8,128)(2,1)S(1)}, bf16[3,64,512]{2,1,0:T(8,128)(2,1)S(1)}, u32[]{:S(2)}, u32[]{:S(2)}) collective-permute-start(bf16[3,64,512]{2,1,0:T(8,128)(2,1)S(1)} %bitcast.901), channel_id=1, source_target_pairs={{0,2},{2,4},{4,6},{6,8},{8,10},{10,12},{12,14},{14,16},{16,18},{18... | collective-permute-start | bytes 589832 | tf_op jit(solution)/shard_map/while/body/eval_jaxpr/ppermute | solution.py:34
  1647.5 99.1 %copy-start.116 = (f32[3,32,256]{2,0,1:T(4,128)S(1)}, f32[3,32,256]{2,0,1:T(4,128)}, u32[]{:S(2)}) copy-start(f32[3,32,256]{2,0,1:T(4,128)} %get-tuple-element.1609) | copy-start | bytes 294916 | tf_op jit(solution)/shard_map/while
  1647.6 100.8 %copy-start.124 = (f32[33,4]{1,0:T(8,128)S(1)}, f32[33,4]{1,0:T(8,128)}, u32[]{:S(2)}) copy-start(f32[33,4]{1,0:T(8,128)} %copy-done.123) | copy-start | bytes 1588 | tf_op jit(solution)/shard_map/while
  1647.6 100.1 %copy-start.159 = (f32[512]{0:T(512)}, f32[512]{0:T(512)S(1)}, u32[]{:S(2)}) copy-start(f32[512]{0:T(512)S(1)} %get-tuple-element.1649) | copy-start | bytes 6148 | tf_op jit(solution)/shard_map/while
  1647.6 100.1 %copy-start.161 = (f32[512]{0:T(512)}, f32[512]{0:T(512)S(1)}, u32[]{:S(2)}) copy-start(f32[512]{0:T(512)S(1)} %get-tuple-element.1650) | copy-start | bytes 6148 | tf_op jit(solution)/shard_map/while
  1647.7 100.0 %copy-start.119 = (f32[7,7,512]{2,1,0:T(8,128)}, f32[7,7,512]{2,1,0:T(8,128)S(1)}, u32[]{:S(2)}) copy-start(f32[7,7,512]{2,1,0:T(8,128)S(1)} %bitcast_add_fusion.9) | copy-start | bytes 301060 | tf_op jit(solution)/shard_map/while
  1647.8 100.0 %copy-start.180 = (bf16[2,256,512]{2,1,0:T(8,128)(2,1)}, bf16[2,256,512]{2,1,0:T(8,128)(2,1)S(1)}, u32[]{:S(2)}) copy-start(bf16[2,256,512]{2,1,0:T(8,128)(2,1)S(1)} %bitcast_dynamic-update-slice_fusion.2) | copy-start | bytes 1572868 | tf_op jit(solution)/shard_map/while
  1648.5 99.3 %copy-start.178 = (f32[2,256,512]{2,1,0:T(8,128)}, f32[2,256,512]{2,1,0:T(8,128)S(1)}, u32[]{:S(2)}) copy-start(f32[2,256,512]{2,1,0:T(8,128)S(1)} %fusion.963) | copy-start | bytes 3145732 | tf_op jit(solution)/shard_map/while
  1749.7 109.2 %all-reduce.24.cloned.1.call-start = ((), (), s32[]{:S(2)}) async-start(), calls=%async_computation.1 | async-start | bytes 229376 | tf_op jit(solution)/shard_map/psum | solution.py:398
  (338 other events, 1629.4 us)
Sparse Core Ops, SparseCore 0:
  71.2 104.2 all-reduce.25
  337.3 108.9 all-reduce.27
  540.5 107.5 all-reduce.29
  653.8 17.7 all-reduce.33
  673.8 78.2 reduce-scatter.1
  757.5 122.3 all-reduce.31
  938.4 104.3 all-reduce.25
  1204.2 108.9 all-reduce.27
  1407.5 107.5 all-reduce.29
  1520.8 17.7 all-reduce.33
  1540.9 78.0 reduce-scatter.1
  1624.3 122.2 all-reduce.31
Sparse Core Ops, SparseCore 1:
  1756.2 102.6 all-reduce.23
where the time goes:
time: 1880 us; the launch traced here: 1870 us
  waiting for transfers between devices  858 us (46%)
  blocking collectives  388 us (21%)
  matrix products  379 us (20%)
  local copies, waits for them, and re-layouts  73.8 us (4%)
  Pallas kernels  57 us (3%)
  starting transfers between devices  50.7 us (3%)
  other arithmetic  38.4 us (2%)
    psum x4, waiting for transfers between devices, one_slide(): grad_mixed, key_mark_part = lax.psum((grad_mixed, key_mark_part), 'seq')  401 us
    dot_general x132, matrix products, batched_product(): jnp.einsum('hij,hjk->hik', left_matrix, right_matrix, precision=FULL_PREC...  249 us
    while x14, waiting for transfers between devices  197 us
    all_gather x4, blocking collectives, combined_all(): gathered = jax.tree.map(lambda a: lax.all_gather(a, axis), part)  150 us
    reduce_scatter x2, waiting for transfers between devices, shard_grads(): lax.psum_scatter(grad_back, 'seq', scatter_dimension=1, tiled=True)  147 us
    all_gather x2, blocking collectives, one_slide(): lax.all_gather(w_qkv, 'seq', axis=1, tiled=True)  86.9 us
    all_gather x2, blocking collectives, one_slide(): lax.all_gather(w_out, 'seq', axis=1, tiled=True)  75.5 us
    psum x1, blocking collectives, shards(): lax.psum((small_grads[0], small_grads[1], small_grads[2], small_grads[3],...  75.2 us
  transfers between devices with their start and end apart: 29, of which 13 were waited for; matrix products, arithmetic and copies ran while one was open for 8% of the time, Pallas kernels for 0%

commit v1 on v0

v1 whole, which is shorter than its diff:
```python
import functools

import jax
import jax.numpy as jnp
from jax import lax
from jax.experimental import pallas as pl
from jax.experimental.pallas import tpu as pltpu
from jax.sharding import PartitionSpec as P

MESH = pl.DeviceIdType.MESH
GRID_W = 64
MARKS = 256
SWEEPS = 6
EPSILON = 1e-05
f32, bf16 = jnp.float32, jnp.bfloat16
VMEM = pl.BlockSpec(memory_space=pltpu.VMEM)
SMEM = pl.BlockSpec(memory_space=pltpu.SMEM)
DMA = pltpu.SemaphoreType.DMA
BLK = 144


def sds(shape, dtype=f32):
    return jax.ShapeDtypeStruct(shape, dtype)


def call(kernel, outs, specs, scratch=(), cid=None, vmem=56):
    extra = {} if cid is None else dict(collective_id=cid, has_side_effects=True)
    return pl.pallas_call(
        kernel,
        out_shape=outs,
        in_specs=specs,
        out_specs=jax.tree.map(lambda _: VMEM, outs),
        scratch_shapes=list(scratch),
        compiler_params=pltpu.CompilerParams(vmem_limit_bytes=vmem * 2**20, **extra),
    )


def mm(left, right, cl=1, cr=0):
    return lax.dot_general(left, right, (((cl,), (cr,)), ((), ())), preferred_element_type=f32)


def split(value):
    high = value.astype(bf16)
    return high, (value - high.astype(f32)).astype(bf16)


def split3(row):
    high = row.astype(bf16).astype(f32)
    rest = row - high
    mid = rest.astype(bf16).astype(f32)
    return [high, mid, rest - mid]


def mm3(left, right, cl=1, cr=0):
    (lh, ll), (rh, rl) = left, right
    return mm(lh, rh, cl, cr) + (mm(lh, rl, cl, cr) + mm(ll, rh, cl, cr))


def iota(shape, dim):
    return lax.broadcasted_iota(jnp.int32, shape, dim)


def edges(count, marks):
    return (marks * count + (MARKS - 1)) >> 8, ((marks + 1) * count + (MARKS - 1)) >> 8


def member(count, start, rows):
    low, high = edges(count, iota((MARKS, rows), 0))
    slot = iota((MARKS, rows), 1) + start
    return jnp.where((slot >= low) & (slot < high), 1.0, 0.0).astype(bf16)


def owner_of(pair):
    return (pair // 2) * 4 + (pair % 2) * 3


def pair_of(me):
    z = lax.rem(me, 16) // 4
    return 2 * z + jnp.where(lax.rem(me, 4) == 3, 1, 0)


def is_owner(me):
    return (me < 16) & ((lax.rem(me, 4) == 0) | (lax.rem(me, 4) == 3))


def norm_kernel(rows, cnt, tok, gain, bias, normed, xpart):
    me, hd = lax.axis_index("seq"), lax.axis_index("head")
    for s in range(2):
        x = tok[s].astype(f32)
        xc = x - jnp.mean(x, axis=-1, keepdims=True)
        inv = lax.rsqrt(jnp.mean(xc * xc, axis=-1, keepdims=True) + EPSILON)
        normed[s] = (xc * inv * gain[...] + bias[...]).astype(bf16)
        mem = member(cnt[s], me * rows, rows)
        xpart[s] = mm(mem, normed[s, :, pl.ds(hd * 256, 256)]).astype(bf16)


def greet(n, pair=True):
    me, hd = lax.axis_index("seq"), lax.axis_index("head")
    sem = pltpu.get_barrier_semaphore()
    for i in range(1, n):
        pl.semaphore_signal(sem, inc=1, device_id={"seq": lax.rem(me + i, n)}, device_id_type=MESH)
    if pair:
        pl.semaphore_signal(sem, inc=1, device_id={"head": 1 - hd}, device_id_type=MESH)
    pl.semaphore_wait(sem, n - 1 + (1 if pair else 0))


def remote(src, dst, send, recv, **where):
    return pltpu.make_async_remote_copy(
        src_ref=src, dst_ref=dst, send_sem=send, recv_sem=recv, device_id=where, device_id_type=MESH
    )


def start_kernel(n, cnt, xpart, wts, cot, xbar, wall, halo, xr, xm, sx, rx, sw, rw, sh, rh, sp, rp, sg, rg):
    me, hd = lax.axis_index("seq"), lax.axis_index("head")
    mb = MARKS // n
    wr = wts.shape[1]
    rows = cot.shape[1]
    mine = pl.ds(pl.multiple_of(hd * 256, 256), 256)
    greet(n)
    peers = [lax.rem(me + i, n) for i in range(n)]
    cx, cw, cg = [], [], []
    for i in range(1, n):
        cx.append(
            remote(xpart.at[:, pl.ds(pl.multiple_of(peers[i] * mb, mb), mb)], xr.at[me], sx.at[i], rx.at[i], seq=peers[i])
        )
        cx[-1].start()
    ch = [
        remote(cot.at[:, pl.ds(rows - 192, 192), mine], halo.at[0], sh.at[0], rh.at[0], seq=peers[1]),
        remote(cot.at[:, pl.ds(0, 192), mine], halo.at[1], sh.at[1], rh.at[1], seq=peers[n - 1]),
    ]
    for c in ch:
        c.start()
    wrow = pl.ds(pl.multiple_of(me * wr, wr), wr)
    for i in range(1, n):
        cw.append(remote(wts, wall.at[:, wrow], sw.at[i], rw.at[i], seq=peers[i]))
        cw[-1].start()
    wall[:, wrow] = wts[...]
    row = pl.ds(pl.multiple_of(me * mb, mb), mb)
    xr[pl.ds(me, 1)] = xpart[:, row][None]
    for c in cx:
        c.wait_recv()
    total = xr[0].astype(f32)
    for d in range(1, n):
        total = total + xr[d].astype(f32)
    for s in range(2):
        low, high = edges(cnt[s], iota((mb, 256), 0) + me * mb)
        xm[s] = (total[s] / (high - low).astype(f32)).astype(bf16)
    xbar[:, row, mine] = xm[...]
    for i in range(1, n):
        cg.append(remote(xm, xbar.at[:, row, mine], sg.at[i], rg.at[i], seq=peers[i]))
        cg[-1].start()
    for c in cg:
        c.wait_recv()
    cp = remote(xbar.at[:, :, mine], xbar.at[:, :, mine], sp, rp, head=1 - hd)
    cp.start()
    for c in ch + cw:
        c.wait_recv()
    cp.wait_recv()
    for c in cx + ch + cw + cg + [cp]:
        c.wait_send()


def fill_kernel(half, full, ss, rs):
    hd = lax.axis_index("head")
    sem = pltpu.get_barrier_semaphore()
    pl.semaphore_signal(sem, inc=1, device_id={"head": 1 - hd}, device_id_type=MESH)
    pl.semaphore_wait(sem, 1)
    mine = pl.ds(pl.multiple_of(hd * 256, 256), 256)
    c = remote(half, full.at[:, :, mine], ss, rs, head=1 - hd)
    c.start()
    full[:, :, mine] = half[...]
    c.wait()


def reduce_kernel(n, blk, hal, recv, hrecv, ss, rs, sh, rh):
    me = lax.axis_index("seq")
    greet(n, False)
    right, left = lax.rem(me + 1, n), lax.rem(me + n - 1, n)
    ch = [
        remote(hal.at[1], hrecv.at[0], sh.at[0], rh.at[0], seq=right),
        remote(hal.at[0], hrecv.at[1], sh.at[1], rh.at[1], seq=left),
    ]
    for p in range(8):
        o = owner_of(p)

        @pl.when(me != o)
        def _():
            remote(blk.at[p], recv.at[me], ss.at[p], rs.at[me], seq=o).start()

        @pl.when(me == o)
        def _():
            recv[pl.ds(me, 1)] = blk[pl.ds(p, 1)]

    for c in ch:
        c.start()
    for c in ch:
        c.wait()
    for p in range(8):
        o = owner_of(p)

        @pl.when(me != o)
        def _():
            remote(blk.at[p], recv.at[me], ss.at[p], rs.at[me], seq=o).wait_send()

        @pl.when(me == o)
        def _():
            for d in range(n):
                if d != o:
                    remote(blk.at[p], recv.at[d], ss.at[p], rs.at[d], seq=o).wait_recv()


def spread_kernel(n, res, out, ss, rs):
    me = lax.axis_index("seq")
    greet(n, False)
    for p in range(8):
        o = owner_of(p)

        @pl.when(me == o)
        def _():
            for i in range(1, n):
                remote(res, out.at[p], ss.at[i], rs.at[p], seq=lax.rem(me + i, n)).start()
            out[p] = res[...]

    for p in range(8):
        o = owner_of(p)

        @pl.when(me != o)
        def _():
            remote(res, out.at[p], ss.at[0], rs.at[p], seq=o).wait_recv()

        @pl.when(me == o)
        def _():
            for i in range(1, n):
                remote(res, out.at[p], ss.at[i], rs.at[p], seq=lax.rem(me + i, n)).wait_send()


def late_kernel(n, cnt, tok, obias, po, ep, dn, wpart, hid, dnr, eall, gw, zhalo,
                por, er, es, erv, em, wrv, zs, *sems):
    (sp, rp, se, re, sa, ra, sw, rw, sz, rz, sf, rf) = sems
    me, hd = lax.axis_index("seq"), lax.axis_index("head")
    mb = MARKS // n
    wr = wpart.shape[1] // n
    rows = tok.shape[1]
    mine = pl.ds(pl.multiple_of(hd * 256, 256), 256)
    other = pl.ds(pl.multiple_of((1 - hd) * 256, 256), 256)
    peers = [lax.rem(me + i, n) for i in range(n)]
    greet(n)
    cp = [
        remote(ep.at[:, :, other], er, sp.at[0], rp.at[0], head=1 - hd),
        remote(po.at[:, :, other], por, sp.at[1], rp.at[1], head=1 - hd),
        remote(dn, dnr, sp.at[2], rp.at[2], head=1 - hd),
    ]
    for c in cp:
        c.start()
    cp[0].wait_recv()
    es[...] = (ep[:, :, mine].astype(f32) + er[...].astype(f32)).astype(bf16)
    row = pl.ds(pl.multiple_of(me * mb, mb), mb)
    ce, ca, cw = [], [], []
    for i in range(1, n):
        ce.append(remote(es.at[:, pl.ds(pl.multiple_of(peers[i] * mb, mb), mb)], erv.at[me], se.at[i], re.at[i], seq=peers[i]))
        ce[-1].start()
    cp[1].wait_recv()
    for s in range(2):
        h = tok[s, :, mine].astype(f32) + (po[s, :, mine].astype(f32) + por[s].astype(f32)) + obias[:, mine]
        hid[s] = h
        slot = iota((rows, 256), 0) + me * rows
        zs[s] = jnp.where(slot < cnt[s], h, 0.0).astype(bf16)
    cz = [
        remote(zs.at[:, pl.ds(rows - 192, 192)], zhalo.at[0], sz.at[0], rz.at[0], seq=peers[1]),
        remote(zs.at[:, pl.ds(0, 192)], zhalo.at[1], sz.at[1], rz.at[1], seq=peers[n - 1]),
    ]
    for c in cz:
        c.start()
    for i in range(1, n):
        cw.append(remote(wpart.at[:, pl.ds(pl.multiple_of(peers[i] * wr, wr), wr)], wrv.at[me], sw.at[i], rw.at[i], seq=peers[i]))
        cw[-1].start()
    erv[pl.ds(me, 1)] = es[:, row][None]
    wrv[pl.ds(me, 1)] = wpart[:, pl.ds(pl.multiple_of(me * wr, wr), wr)][None]
    for c in ce:
        c.wait_recv()
    total = erv[0].astype(f32)
    for d in range(1, n):
        total = total + erv[d].astype(f32)
    em[...] = total.astype(bf16)
    eall[:, row, mine] = em[...]
    for i in range(1, n):
        ca.append(remote(em, eall.at[:, row, mine], sa.at[i], ra.at[i], seq=peers[i]))
        ca[-1].start()
    for c in ca:
        c.wait_recv()
    cf = remote(eall.at[:, :, mine], eall.at[:, :, mine], sf, rf, head=1 - hd)
    cf.start()
    for c in cw:
        c.wait_recv()
    total = wrv[0].astype(f32)
    for d in range(1, n):
        total = total + wrv[d].astype(f32)
    gw[...] = total
    cf.wait_recv()
    cp[2].wait_recv()
    for c in cz:
        c.wait_recv()
    for c in cp + ce + ca + cw + cz + [cf]:
        c.wait_send()


def last_kernel(n, outh, gk, small, out, gkall, ssum, gkr, gkm, smr, *sems):
    (so, ro, sk, rk, sa, ra, sp, rp, ss, rs) = sems
    me, hd = lax.axis_index("seq"), lax.axis_index("head")
    mine = pl.ds(pl.multiple_of(hd * 256, 256), 256)
    peers = [lax.rem(me + i, n) for i in range(n)]
    greet(n)
    co = remote(outh, out.at[:, :, mine], so, ro, head=1 - hd)
    co.start()
    cs = []
    for i in range(1, n):
        cs.append(remote(small, smr.at[me], ss.at[i], rs.at[i], seq=peers[i]))
        cs[-1].start()
    nb = gk.shape[0] // 8

    def to(b):
        return remote(gk.at[pl.ds(8 * b, 8)], gkr.at[me], sk.at[b], rk.at[me], seq=b)

    def back(b, i):
        return remote(gkm, gkall.at[pl.ds(8 * b, 8), mine], sa.at[i], ra.at[b], seq=peers[i])

    for b in range(nb):

        @pl.when(me != b)
        def _():
            to(b).start()

    out[:, :, mine] = outh[...]
    smr[pl.ds(me, 1)] = small[...][None]
    for b in range(nb):

        @pl.when(me == b)
        def _():
            gkr[pl.ds(me, 1)] = gk[pl.ds(8 * b, 8)][None]
            for d in range(n):
                if d != b:
                    remote(gk.at[pl.ds(8 * b, 8)], gkr.at[d], sk.at[b], rk.at[d], seq=b).wait_recv()
            total = gkr[0]
            for d in range(1, n):
                total = total + gkr[d]
            gkm[...] = total
            gkall[pl.ds(8 * b, 8), mine] = total
            for i in range(1, n):
                back(b, i).start()

    for c in cs:
        c.wait_recv()
    total = smr[0]
    for d in range(1, n):
        total = total + smr[d]
    ssum[...] = total
    for b in range(nb):

        @pl.when(me != b)
        def _():
            back(b, 0).wait_recv()
            to(b).wait_send()

        @pl.when(me == b)
        def _():
            for i in range(1, n):
                back(b, i).wait_send()

    cg = remote(gkall.at[:, mine], gkall.at[:, mine], sp, rp, head=1 - hd)
    cg.start()
    cg.wait()
    co.wait()
    for c in cs:
        c.wait_send()


def load_grid(zs, pad, body, top, bottom):
    grid = body.shape[0] // GRID_W
    pad[...] = jnp.zeros_like(pad)
    pad[0:3, 8:8 + GRID_W] = top.reshape(3, GRID_W, 256)
    pad[3:3 + grid, 8:8 + GRID_W] = body.reshape(grid, GRID_W, 256)
    pad[3 + grid:6 + grid, 8:8 + GRID_W] = bottom.reshape(3, GRID_W, 256)
    for b in range(7):
        zs[b] = pad[:, 5 + b:5 + b + GRID_W, :]


def conv_row(zs, taps, i, flip):
    acc = jnp.zeros((GRID_W, 256), f32)
    for a in range(7):
        for b in range(7):
            t = 48 - (a * 7 + b) if flip else a * 7 + b
            acc = acc + taps[t:t + 1, :] * zs[b, i + a]
    return acc


def ends(me, n, top, bottom):
    top = jnp.where(me > 0, top.astype(f32), 0.0)
    bottom = jnp.where(me < n - 1, bottom.astype(f32), 0.0)
    return top, bottom


def back_conv_kernel(n, cnt, cot, halo, taps, dh, zs, pad):
    me, hd = lax.axis_index("seq"), lax.axis_index("head")
    rows = cot.shape[1]
    mine = pl.ds(pl.multiple_of(hd * 256, 256), 256)
    for s in range(2):
        top, bottom = ends(me, n, halo[0, s], halo[1, s])
        load_grid(zs, pad, cot[s, :, mine].astype(f32), top, bottom)

        @pl.loop(0, rows // GRID_W)
        def _(i):
            acc = conv_row(zs, taps, i, True)
            here = pl.ds(pl.multiple_of(i * GRID_W, GRID_W), GRID_W)
            slot = iota((GRID_W, 256), 0) + (me * rows + i * GRID_W)
            dh[s, here] = cot[s, here, mine].astype(f32) + jnp.where(slot < cnt[s], acc, 0.0)


def scores_kernel(cnt, normed, xbar, wall, dh, qt, kt, vt, qlt, klt, dot, wback, a1, e3, blk, hal):
    me = lax.axis_index("seq")
    rows = normed.shape[1]
    scale = 64 ** -0.5
    wback[...] = wall[3].astype(f32).T.astype(bf16)
    for s in range(2):
        nr = normed[s]
        qt[s] = mm(wall[0], nr, 0, 1).astype(bf16)
        kt[s] = mm(wall[1], nr, 0, 1).astype(bf16)
        slots = iota((256, rows), 1) + me * rows
        vt[s] = jnp.where(slots < cnt[s], mm(wall[2], nr, 0, 1), 0.0).astype(bf16)
        qlt[s] = mm(wall[0], xbar[s], 0, 1).astype(bf16)
        klt[s] = mm(wall[1], xbar[s], 0, 1).astype(bf16)
        dhr = dh[s].astype(bf16)
        dot[s] = mm(wback[...], dhr, 1, 1).astype(bf16)
        for side, first in ((0, 0), (1, rows - 16)):
            slot = iota((16, 256), 0) + (me * rows + first)
            v = mm(normed[s, first:first + 16], wall[2])
            hal[side, s, 0] = jnp.where(slot < cnt[s], v, 0.0).astype(bf16)
            hal[side, s, 1] = mm(dhr[first:first + 16], wback[...], 1, 1).astype(bf16)

    @pl.loop(0, 8)
    def _(p):
        s, h = p // 4, lax.rem(p, 4)
        here = pl.ds(pl.multiple_of(h * 64, 64), 64)
        count = cnt[s]
        s1 = mm(klt[s, here] * scale, qt[s, here], 0, 0)
        e1 = jnp.exp(s1 - jnp.max(s1, axis=0, keepdims=True))
        a = (e1 / jnp.sum(e1, axis=0, keepdims=True)).astype(bf16)
        a1[p] = a
        blk[p, 64:128] = mm(dot[s, here], a, 1, 1).astype(bf16)
        s3 = mm(kt[s, here] * scale, qlt[s, here], 0, 0)
        ok = iota((rows, MARKS), 0) + me * rows < count
        s3 = jnp.where(ok, s3, -1e30)
        top = jnp.max(s3, axis=0, keepdims=True)
        e = jnp.where(ok, jnp.exp(s3 - top), 0.0)
        total = jnp.sum(e, axis=0, keepdims=True)
        er = e.astype(bf16)
        e3[p] = er
        blk[p, 0:64] = mm(vt[s, here], er).astype(bf16)
        stat = jnp.concatenate(split3(top) + split3(total) + [jnp.zeros((10, MARKS), f32)], axis=0)
        blk[p, 128:144] = stat.astype(bf16)


def three(stat, first):
    return (stat[first:first + 1] + stat[first + 1:first + 2]) + stat[first + 2:first + 3]


def chain_kernel(recv, qlt, klt, res, dqz, ps, ts, xs):
    me = lax.axis_index("seq")
    pair = pair_of(me)
    s, h = pair // 4, lax.rem(pair, 4)
    here = pl.ds(pl.multiple_of(h * 64, 64), 64)
    scale = 64 ** -0.5
    parts = recv.shape[0]
    dqz[...] = jnp.zeros_like(dqz)

    @pl.when(is_owner(me))
    def _():
        tops = [three(recv[d, 128:144].astype(f32), 0) for d in range(parts)]
        top = functools.reduce(jnp.maximum, tops)
        total, value, dct = 0.0, 0.0, 0.0
        for d in range(parts):
            w = jnp.exp(tops[d] - top)
            total = total + three(recv[d, 128:144].astype(f32), 3) * w
            value = value + recv[d, 0:64].astype(f32) * w
            dct = dct + recv[d, 64:128].astype(f32)
        value = value / total
        ql, kl = qlt[s, here], klt[s, here]
        s2 = mm(ql * scale, kl, 0, 0)
        e2 = jnp.exp(s2 - jnp.max(s2, axis=1, keepdims=True))
        a = e2 / jnp.sum(e2, axis=1, keepdims=True)
        asp = split(a)
        cs, rs = jnp.sum(a, axis=0, keepdims=True), jnp.sum(a, axis=1, keepdims=True)
        cm, rm = jnp.max(cs, axis=1, keepdims=True), jnp.max(rs, axis=0, keepdims=True)
        inv = 1.0 / (cm * rm)
        p = mm3(asp, asp, 1, 1) * inv
        x = value
        for k in range(SWEEPS):
            psp = split(p)
            t = mm3(psp, psp)
            tsp = split(t)
            ps[k, 0], ps[k, 1] = psp
            ts[k, 0], ts[k, 1] = tsp
            xs[k] = x
            if k < SWEEPS - 1:
                p = 0.25 * (13.0 * p - 15.0 * t + mm3(tsp, split(7.0 * p - t)))
            xt = mm3(split(x), tsp)
            x = 0.25 * (13.0 * x + 7.0 * xt - mm3(split(15.0 * x + xt), psp))
        ct = mm3(split(x), asp) * inv
        res[0:64] = ct.astype(bf16)
        dcs = split(dct)
        y = mm3(dcs, asp, 1, 1) * inv
        da = mm3(split(x), dcs, 0, 0) * inv
        ds = -jnp.sum(jnp.sum(dct * ct, axis=0, keepdims=True), axis=1, keepdims=True) * inv * (cm * rm) * inv
        e = None
        for k in range(SWEEPS - 1, -1, -1):
            psp = (ps[k, 0], ps[k, 1])
            tsp = (ts[k, 0], ts[k, 1])
            outer = mm3(split(y), split(xs[k]), 0, 0) * 0.125
            d = outer + outer.T
            pd = mm3(psp, split(d))
            if e is None:
                v = 7.0 * pd
                w = -d
                new = -15.0 * d + mm3(split(-pd), psp)
                half = mm3(tsp, split(w))
            else:
                eq = 0.25 * e
                pe = mm3(psp, split(eq))
                v = 7.0 * pd - 15.0 * pe
                new = 13.0 * eq - 15.0 * d + mm3(split(7.0 * pe - pd), psp)
                half = mm3(tsp, split(7.0 * eq - d - (pe + pe.T)))
            half = half + v
            e = new + (half + half.T)
            yt = mm3(split(y), tsp)
            y = 0.25 * (13.0 * y + 7.0 * yt - mm3(split(15.0 * y + yt), psp))
        dbr = y.astype(bf16)
        res[64:128] = dbr
        rt = jnp.sum(dbr.astype(f32) * value, axis=0, keepdims=True)
        stat = jnp.concatenate(split3(top) + split3(total) + split3(rt) + [jnp.zeros((7, MARKS), f32)], axis=0)
        res[128:144] = stat.astype(bf16)
        da = da + mm3(split(e), asp) * (2.0 * inv)
        p0 = ps[0, 0].astype(f32) + ps[0, 1].astype(f32)
        ds = ds - jnp.sum(jnp.sum(e * p0, axis=0, keepdims=True), axis=1, keepdims=True) * inv
        eqc, eqr = jnp.where(cs == cm, 1.0, 0.0), jnp.where(rs == rm, 1.0, 0.0)
        da = da + (ds * rm) * (eqc / jnp.sum(eqc, axis=1, keepdims=True))
        da = da + (ds * cm) * (eqr / jnp.sum(eqr, axis=0, keepdims=True))
        dsc = a * (da - jnp.sum(a * da, axis=1, keepdims=True)) * scale
        dh, dl = split(dsc)
        dqz[0] = mm(kl, dh, 1, 1) + mm(kl, dl, 1, 1)
        dqz[1] = mm(ql, dh) + mm(ql, dl)


def band(base, shift, rows):
    wide = jnp.broadcast_to(base, (rows, 256))
    return pltpu.roll(wide, shift, 1, stride=1, stride_axis=0)


def diagonals(g, shift):
    return jnp.sum(pltpu.roll(g, shift, 1, stride=1, stride_axis=0), axis=0, keepdims=True)


def grads_kernel(n, cnt, normed, xbar, wall, wback, dh, qt, kt, vt, qlt, klt, dot, a1, e3, blk, res, hrecv, base, dqz,
                 po, dn, ep, wpart, gtaps, att, dp, dlm, gsum, tm, th, ht, vr):
    me = lax.axis_index("seq")
    rows = normed.shape[1]
    scale = 64 ** -0.5
    pi, pj = iota((rows, rows), 0), iota((rows, rows), 1)
    inside = (pi - pj <= 16) & (pj - pi <= 16)
    hi, hj = iota((32, rows), 0), iota((32, rows), 1)
    far = jnp.where(hi < 16, hi - hj, hj - hi - (rows - 32)) >= 0
    for f in range(2):
        for h in range(4):
            line = base[4 * f + h:4 * f + h + 1, :]
            full = jnp.where(inside, band(line, 0, rows), 0.0)
            tm[f, h, 0], tm[f, h, 1] = split(full)
            both = jnp.concatenate([band(line, 240, 16), band(line, 0, 16)], axis=0)
            th[f, h, 0], th[f, h, 1] = split(jnp.where(far, both, 0.0))
    gsum[...] = jnp.zeros_like(gsum)
    mirror = jnp.where(pi + pj == rows - 1, 1.0, 0.0).astype(bf16)
    si, sj = iota((32, 32), 0), iota((32, 32), 1)
    mirror32 = jnp.where(si + sj == jnp.where(si < 16, 15, 47), 1.0, 0.0).astype(bf16)
    for s in range(2):
        for k in range(2):
            top, bottom = ends(me, n, hrecv[0, s, k], hrecv[1, s, k])
            ht[k, s] = jnp.concatenate([top, bottom], axis=0).T.astype(bf16)
        vr[s] = mm(vt[s], mirror).astype(bf16)
        ht[2, s] = mm(ht[0, s], mirror32).astype(bf16)
    mine = pair_of(me)
    use = jnp.where(is_owner(me), 1.0, 0.0)

    @pl.loop(0, 8)
    def _(p):
        s, h = p // 4, lax.rem(p, 4)
        here = pl.ds(pl.multiple_of(h * 64, 64), 64)
        ct, dbt = res[p, 0:64], res[p, 64:128]
        stat = res[p, 128:144].astype(f32)
        own = three(blk[p, 128:144].astype(f32), 0)
        factor = jnp.exp(own - three(stat, 0)) / three(stat, 3)
        rt = three(stat, 6)
        do, v, vh, doh = dot[s, here], vt[s, here], ht[0, s, here], ht[1, s, here]
        conv = mm(v, tm[0, h, 0]) + mm(v, tm[0, h, 1]) + mm(vh, th[0, h, 0]) + mm(vh, th[0, h, 1])
        dconv = mm(do, tm[1, h, 0]) + mm(do, tm[1, h, 1]) + mm(doh, th[1, h, 0]) + mm(doh, th[1, h, 1])
        gsum[h, 0:rows] = gsum[h, 0:rows] + mm(vr[s, here], do, 0, 0)
        gsum[h, rows:rows + 32] = gsum[h, rows:rows + 32] + mm(ht[2, s, here], do, 0, 0)
        a = a1[p]
        af = a.astype(f32)
        att[s, here] = (mm(ct, a) + conv).astype(bf16)
        da = mm(ct, do, 0, 0)
        d1 = (af * (da - jnp.sum(af * da, axis=0, keepdims=True))).astype(bf16)
        dp[0, s, here] = mm(klt[s, here] * scale, d1).astype(bf16)
        own_chain = jnp.where(p == mine, use, 0.0)
        dlm[1, s, here] = (mm(qt[s, here] * scale, d1, 1, 1) + own_chain * dqz[1]).astype(bf16)
        a3 = e3[p].astype(f32) * factor
        d3 = (a3 * (mm(v, dbt, 0, 0) - rt)).astype(bf16)
        dlm[0, s, here] = (mm(kt[s, here] * scale, d3) + own_chain * dqz[0]).astype(bf16)
        dp[1, s, here] = mm(qlt[s, here] * scale, d3, 1, 1).astype(bf16)
        dv = mm(dbt, a3.astype(bf16), 1, 1) + dconv
        slot = iota((64, rows), 1) + me * rows
        dp[2, s, here] = jnp.where(slot < cnt[s], dv, 0.0).astype(bf16)

    near = (pi + pj >= rows - 17) & (pi + pj <= rows + 15)
    beyond = jnp.where(hi < 16, 15 - hi - hj, hi + hj - (rows + 15)) >= 0
    for h in range(4):
        g = jnp.where(near, gsum[h, 0:rows], 0.0)
        gh = jnp.where(beyond, gsum[h, rows:rows + 32], 0.0)
        gtaps[h:h + 1, :] = diagonals(g, 1) + diagonals(gh[0:16], 1) + diagonals(gh[16:32], 241)
    gtaps[4:8, :] = jnp.zeros((4, 256), f32)
    for j in range(3):
        g = mm(dp[j, 0], normed[0]) + mm(dp[j, 1], normed[1])
        if j < 2:
            g = g + (mm(dlm[j, 0], xbar[0]) + mm(dlm[j, 1], xbar[1]))
        wpart[j] = g.T.astype(bf16)
    g = mm(att[0], dh[0].astype(bf16)) + mm(att[1], dh[1].astype(bf16))
    wpart[3] = g.T.astype(bf16)
    for s in range(2):
        po[s] = mm(att[s], wback[...], 0, 0).astype(bf16)
        d = mm(wall[0], dp[0, s]) + mm(wall[1], dp[1, s]) + mm(wall[2], dp[2, s])
        dn[s] = d.T.astype(bf16)
        e = mm(wall[0], dlm[0, s]) + mm(wall[1], dlm[1, s])
        ep[s] = e.T.astype(bf16)


def final_kernel(n, cnt, hid, zhalo, cot, taps, pbias, tok, dh, dn, dnr, eall, gain, gtaps, outh, gx, gk, small, zs, pad, gacc):
    me, hd = lax.axis_index("seq"), lax.axis_index("head")
    rows = tok.shape[1]
    mine = pl.ds(pl.multiple_of(hd * 256, 256), 256)
    gacc[...] = jnp.zeros_like(gacc)
    small[...] = jnp.zeros_like(small)
    small[4:8, 0:256] = gtaps[0:4, :]
    for s in range(2):
        count = cnt[s]
        slot = iota((rows, 256), 0) + me * rows
        top, bottom = ends(me, n, zhalo[0, s], zhalo[1, s])
        load_grid(zs, pad, jnp.where(slot < count, hid[s], 0.0), top, bottom)

        @pl.loop(0, rows // GRID_W)
        def _(i):
            here = pl.ds(pl.multiple_of(i * GRID_W, GRID_W), GRID_W)
            acc = conv_row(zs, taps, i, False)
            outh[s, here] = (hid[s, here] + acc + pbias[:, mine]).astype(bf16)
            g = cot[s, here, mine].astype(f32)
            for a in range(7):
                for b in range(7):
                    t = a * 7 + b
                    part = (g * zs[b, i + a]).reshape(GRID_W // 8, 8, 256)
                    gacc[t] = gacc[t] + jnp.sum(part, axis=0)

        low, high = edges(count, iota((MARKS, 512), 0))
        e = (eall[s].astype(f32) / (high - low).astype(f32)).astype(bf16)
        mem = member(count, me * rows, rows)
        total = (dn[s].astype(f32) + dnr[s].astype(f32)) + mm(mem, e, 0, 0)
        x = tok[s].astype(f32)
        xc = x - jnp.mean(x, axis=-1, keepdims=True)
        inv = lax.rsqrt(jnp.mean(xc * xc, axis=-1, keepdims=True) + EPSILON)
        xh = xc * inv
        dg = total * gain[...]
        m1 = jnp.mean(dg, axis=-1, keepdims=True)
        m2 = jnp.mean(dg * xh, axis=-1, keepdims=True)
        gx[s] = dh[s] + (dg - m1 - xh * m2) * inv
        small[0:1] = small[0:1] + jnp.sum(total * xh, axis=0, keepdims=True)
        small[1:2] = small[1:2] + jnp.sum(total, axis=0, keepdims=True)
        small[2:3] = small[2:3] + jnp.sum(dh[s], axis=0, keepdims=True)
        small[3:4] = small[3:4] + jnp.sum(cot[s].astype(f32), axis=0, keepdims=True)
    for t in range(49):
        gk[t:t + 1] = jnp.sum(gacc[t], axis=0, keepdims=True)
    gk[49:56] = jnp.zeros((7, 256), f32)


def ring(rows_up, rows_down):
    count = lax.axis_size("seq")
    up = lax.ppermute(rows_up, "seq", [(i, (i + 1) % count) for i in range(count)])
    down = lax.ppermute(rows_down, "seq", [((i + 1) % count, i) for i in range(count)])
    return jnp.stack([up, down])


def half_of(full, axis):
    return lax.dynamic_slice_in_dim(full, lax.axis_index("head") * 256, 256, axis)


def start_plain(counts, xpart, wts, cot):
    low, high = edges(counts[:, None], jnp.arange(MARKS, dtype=jnp.int32)[None])
    xs = lax.psum(xpart.astype(f32), "seq") / (high - low).astype(f32)[..., None]
    xbar = lax.all_gather(xs.astype(bf16), "head", axis=2, tiled=True)
    wall = lax.all_gather(wts, "seq", axis=1, tiled=True)
    mine = half_of(cot, 2)
    return xbar, wall, ring(mine[:, -192:], mine[:, :192])


def reduce_plain(blk, hal):
    hrecv = ring(hal[1], hal[0])
    stat = blk[:, 128:].astype(f32)
    top, total = three_rows(stat, 0), three_rows(stat, 3)
    best = lax.pmax(top, "seq")
    w = jnp.exp(top - best)
    total, value, dct = lax.psum(
        (total * w, blk[:, 0:64].astype(f32) * w, blk[:, 64:128].astype(f32)), "seq"
    )
    rows = [jnp.concatenate([r[p] for p in range(8)], 0) for r in split3(best) + split3(total)]
    stat = jnp.stack(rows + [jnp.zeros_like(rows[0])] * 10, axis=1)
    whole = jnp.concatenate([value, dct, stat], axis=1).astype(bf16)
    return lax.dynamic_slice_in_dim(whole, pair_of(lax.axis_index("seq")), 1, 0), hrecv


def three_rows(stat, first):
    return (stat[:, first:first + 1] + stat[:, first + 1:first + 2]) + stat[:, first + 2:first + 3]


def spread_plain(res):
    me = lax.axis_index("seq")
    held = jnp.where((jnp.arange(8) == pair_of(me)) & is_owner(me), 1, 0)[:, None, None] == 1
    return lax.psum(jnp.where(held, res[None].astype(f32), 0.0), "seq").astype(bf16)


def late_plain(counts, tok, obias, po, ep, dn, wpart):
    rows = tok.shape[1]
    both = lax.psum(po.astype(f32), "head")
    hid = half_of(tok.astype(f32) + both + obias, 2)
    slots = lax.axis_index("seq") * rows + jnp.arange(rows)
    z = jnp.where((slots[None] < counts[:, None])[..., None], hid, 0.0).astype(bf16)
    zhalo = ring(z[:, -192:], z[:, :192])
    dnr = lax.ppermute(dn, "head", [(0, 1), (1, 0)])
    eall = lax.psum(ep.astype(f32), ("seq", "head")).astype(bf16)
    gw = lax.psum_scatter(wpart.astype(f32), "seq", scatter_dimension=1, tiled=True)
    return hid, dnr, eall, gw, zhalo


def last_plain(outh, gk, small):
    out = lax.all_gather(outh, "head", axis=2, tiled=True)
    gkall = lax.all_gather(lax.psum(gk, "seq"), "head", axis=1, tiled=True)
    return out, gkall, lax.psum(small, "seq")


def shards(n, tokens, counts, ln_gain, ln_bias, w_qkv, conv_taps, w_out, out_bias, kernel7, kernel5, kernel3, ppeg_bias, cotangent):
    rows = tokens.shape[1]
    direct = n == 16
    grid = rows // GRID_W
    mb, wr = MARKS // n, w_qkv.shape[1]
    gain, bias, obias, pbias = (v[None, :] for v in (ln_gain, ln_bias, out_bias, ppeg_bias))
    taps = kernel7 + jnp.pad(kernel5, ((1, 1), (1, 1), (0, 0))) + jnp.pad(kernel3, ((2, 2), (2, 2), (0, 0)))
    taps = half_of(taps.reshape(49, -1), 1)
    lines = jnp.concatenate([conv_taps, conv_taps[:, ::-1]], axis=0)
    base = jnp.concatenate([lines[:, 16::-1], jnp.zeros((8, 223), f32), lines[:, :16:-1]], axis=1)
    wts = jnp.concatenate([w_qkv, w_out.T[None]], axis=0)
    me_arg = counts

    normed, xpart = call(
        functools.partial(norm_kernel, rows),
        [sds((2, rows, 512), bf16), sds((2, MARKS, 256), bf16)],
        [SMEM, VMEM, VMEM, VMEM],
    )(me_arg, tokens, gain, bias)

    if direct:
        xbar, wall, halo = call(
            functools.partial(start_kernel, n),
            [sds((2, MARKS, 512), bf16), sds((4, 512, 256), bf16), sds((2, 2, 192, 256), bf16)],
            [SMEM, VMEM, VMEM, VMEM],
            [pltpu.VMEM((n, 2, mb, 256), bf16), pltpu.VMEM((2, mb, 256), bf16)]
            + [DMA((n,)), DMA((n,)), DMA((n,)), DMA((n,)), DMA((2,)), DMA((2,)), DMA, DMA, DMA((n,)), DMA((n,))],
            cid=0,
        )(counts, xpart, wts, cotangent)
    else:
        xbar, wall, halo = start_plain(counts, xpart, wts, cotangent)

    conv_scratch = [pltpu.VMEM((7, grid + 6, GRID_W, 256), f32), pltpu.VMEM((grid + 6, GRID_W + 16, 256), f32)]
    dhh = call(
        functools.partial(back_conv_kernel, n), sds((2, rows, 256)), [SMEM, VMEM, VMEM, VMEM], conv_scratch
    )(counts, cotangent, halo, taps)
    if direct:
        dh = call(fill_kernel, sds((2, rows, 512)), [VMEM], [DMA, DMA], cid=1)(dhh)
    else:
        dh = lax.all_gather(dhh, "head", axis=2, tiled=True)

    t2 = sds((2, 256, rows), bf16)
    m2 = sds((2, 256, MARKS), bf16)
    qt, kt, vt, qlt, klt, dot, wback, a1, e3, blk, hal = call(
        scores_kernel,
        [t2, t2, t2, m2, m2, t2, sds((256, 512), bf16), sds((8, MARKS, rows), bf16), sds((8, rows, MARKS), bf16),
         sds((8, BLK, MARKS), bf16), sds((2, 2, 2, 16, 256), bf16)],
        [SMEM, VMEM, VMEM, VMEM, VMEM],
    )(counts, normed, xbar, wall, dh)

    if direct:
        recv, hrecv = call(
            functools.partial(reduce_kernel, n),
            [sds((n, BLK, MARKS), bf16), sds(hal.shape, bf16)],
            [VMEM, VMEM],
            [DMA((8,)), DMA((n,)), DMA((2,)), DMA((2,))],
            cid=2,
        )(blk, hal)
    else:
        recv, hrecv = reduce_plain(blk, hal)

    square = pltpu.VMEM((SWEEPS, 2, 256, 256), bf16)
    res, dqz = call(
        chain_kernel,
        [sds((BLK, MARKS), bf16), sds((2, 64, MARKS))],
        [VMEM, VMEM, VMEM],
        [square, square, pltpu.VMEM((SWEEPS, 64, 256), f32)],
    )(recv, qlt, klt)

    if direct:
        res = call(
            functools.partial(spread_kernel, n), sds((8, BLK, MARKS), bf16), [VMEM], [DMA((n,)), DMA((8,))], cid=3
        )(res)
    else:
        res = spread_plain(res)

    po, dn, ep, wpart, gtaps = call(
        functools.partial(grads_kernel, n),
        [sds((2, rows, 512), bf16), sds((2, rows, 512), bf16), sds((2, MARKS, 512), bf16), sds((4, 512, 256), bf16),
         sds((8, 256))],
        [SMEM] + [VMEM] * 18,
        [pltpu.VMEM((2, 256, rows), bf16), pltpu.VMEM((3, 2, 256, rows), bf16), pltpu.VMEM((2, 2, 256, MARKS), bf16),
         pltpu.VMEM((4, rows + 32, rows), f32), pltpu.VMEM((2, 4, 2, rows, rows), bf16), pltpu.VMEM((2, 4, 2, 32, rows), bf16),
         pltpu.VMEM((3, 2, 256, 32), bf16), pltpu.VMEM((2, 256, rows), bf16)],
    )(counts, normed, xbar, wall, wback, dh, qt, kt, vt, qlt, klt, dot, a1, e3, blk, res, hrecv, base, dqz)

    if direct:
        hid, dnr, eall, gw, zhalo = call(
            functools.partial(late_kernel, n),
            [sds((2, rows, 256)), sds((2, rows, 512), bf16), sds((2, MARKS, 512), bf16), sds((4, wr, 256)),
             sds((2, 2, 192, 256), bf16)],
            [SMEM] + [VMEM] * 6,
            [pltpu.VMEM((2, rows, 256), bf16), pltpu.VMEM((2, MARKS, 256), bf16), pltpu.VMEM((2, MARKS, 256), bf16),
             pltpu.VMEM((n, 2, mb, 256), bf16), pltpu.VMEM((2, mb, 256), bf16), pltpu.VMEM((n, 4, wr, 256), bf16),
             pltpu.VMEM((2, rows, 256), bf16)]
            + [DMA((3,)), DMA((3,))] + [DMA((n,))] * 6 + [DMA((2,)), DMA((2,)), DMA, DMA],
            cid=4,
        )(counts, tokens, obias, po, ep, dn, wpart)
    else:
        hid, dnr, eall, gw, zhalo = late_plain(counts, tokens, obias, po, ep, dn, wpart)

    outh, gx, gk, small = call(
        functools.partial(final_kernel, n),
        [sds((2, rows, 256), bf16), sds((2, rows, 512)), sds((56, 256)), sds((8, 512))],
        [SMEM] + [VMEM] * 12,
        conv_scratch + [pltpu.VMEM((49, 8, 256), f32)],
    )(counts, hid, zhalo, cotangent, taps, pbias, tokens, dh, dn, dnr, eall, gain, gtaps)

    if direct:
        out, gk, small = call(
            functools.partial(last_kernel, n),
            [sds((2, rows, 512), bf16), sds((56, 512)), sds((8, 512))],
            [VMEM] * 3,
            [pltpu.VMEM((n, 8, 256), f32), pltpu.VMEM((8, 256), f32), pltpu.VMEM((n, 8, 512), f32),
             DMA, DMA, DMA((7,)), DMA((n,)), DMA((n,)), DMA((7,)), DMA, DMA, DMA((n,)), DMA((n,))],
            cid=5,
        )(outh, gk, small)
    else:
        out, gk, small = last_plain(outh, gk, small)

    gk = gk[:49].reshape(7, 7, 512)
    gtaps = jnp.concatenate([small[4:8, 16::-1][:, :17], small[4:8, 255:239:-1]], axis=1)
    return (
        out, gx, small[0], small[1], gw[0:3], gtaps, gw[3].T, small[2], gk, gk[1:6, 1:6], gk[2:5, 2:5], small[3],
    )


def solution(mesh):
    rows, cols = P(None, "seq", None), P(None, "seq", "head")
    return jax.shard_map(
        functools.partial(shards, mesh.shape["seq"]),
        mesh=mesh,
        in_specs=(rows, P(), P(), P(), cols, P("head", None), P("head", "seq"), P(), P(), P(), P(), P(), rows),
        out_specs=(rows, rows, P(), P(), cols, P("head", None), P("head", "seq"), P(), P(), P(), P(), P()),
        check_vma=False,
    )
```

time: 1880 us -> 252 us (0.13)
  waiting for transfers between devices: 858 us -> 0 us
  blocking collectives: 388 us -> 0 us
  matrix products: 379 us -> 0 us
  Pallas kernels: 57 us -> 236 us
  local copies, waits for them, and re-layouts: 73.8 us -> 10.1 us
  starting transfers between devices: 50.7 us -> 0 us
  other arithmetic: 38.4 us -> 4.46 us
    psum x9 -> x0, waiting for transfers between devices: 514 us -> none  [the longest x4 401 us: one_slide(): grad_mixed, key_mark_part = lax.psum((grad_mixed, key_mark_part), 'seq')]
    all_gather x8 -> x0, blocking collectives: 313 us -> none  [the longest x4 150 us: combined_all(): gathered = jax.tree.map(lambda a: lax.all_gather(a, axis), part)]
    dot_general x184 -> x0, matrix products: 306 us -> none  [the longest x132 249 us: batched_product(): jnp.einsum('hij,hjk->hik', left_matrix, right_matrix, precision=FULL_PREC...]
    pallas_call x0 -> x12, Pallas kernels: none -> 236 us  [the longest x1 57.3 us: shards(): call(functools.partial(late_kernel, n), [sds((2, rows, 256)), sds((2, row...]
    while x14 -> x0, waiting for transfers between devices: 197 us -> none
    reduce_scatter x2 -> x0, waiting for transfers between devices: 147 us -> none  [shard_grads(): lax.psum_scatter(grad_back, 'seq', scatter_dimension=1, tiled=True)]
    psum x1 -> x0, blocking collectives: 75.2 us -> none  [shards(): lax.psum((small_grads[0], small_grads[1], small_grads[2], small_grads[3],...]
    conv_general_dilated x12 -> x0, matrix products: 67.6 us -> none  [the longest x6 51.7 us: grid_conv(): lax.conv_general_dilated(padded[None], kernel_taps[:, :, None, :], (1, 1)...]
  transfers between devices with their start and end apart: 29 -> 0, of which waited for: 13 -> 0; matrix products, arithmetic and copies ran while one was open for 8% -> 0% of each run, Pallas kernels for 0% -> 0%
where the time goes in v1:
time: 252 us
  Pallas kernels  236 us (94%)
  local copies, waits for them, and re-layouts  10.1 us (4%)
  other arithmetic  4.46 us (2%)
    pallas_call x1, Pallas kernels, shards(): call(functools.partial(late_kernel, n), [sds((2, rows, 256)), sds((2, row...  57.3 us
    pallas_call x1, Pallas kernels, shards(): call(functools.partial(start_kernel, n), [sds((2, MARKS, 512), bf16), sds...  49.3 us
    pallas_call x1, Pallas kernels, shards(): call(functools.partial(spread_kernel, n), sds((8, BLK, MARKS), bf16), [VM...  26 us
    pallas_call x1, Pallas kernels, shards(): call(functools.partial(reduce_kernel, n), [sds((n, BLK, MARKS), bf16), sd...  22.6 us
    pallas_call x1, Pallas kernels, shards(): call(functools.partial(last_kernel, n), [sds((2, rows, 512), bf16), sds((...  20.2 us
    pallas_call x1, Pallas kernels, shards(): call(chain_kernel, [sds((BLK, MARKS), bf16), sds((2, 64, MARKS))], [VMEM,...  15.8 us
    pallas_call x1, Pallas kernels, shards(): call(functools.partial(grads_kernel, n), [sds((2, rows, 512), bf16), sds(...  13.7 us
    pallas_call x1, Pallas kernels, shards(): call(functools.partial(final_kernel, n), [sds((2, rows, 256), bf16), sds(...  10.1 us

profile of v1, /device:TPU:0, one launch (start us, length us, event | category | flops | bytes accessed | tf_op | source)
XLA Modules:
  0.0 251.5 jit_solution(13650368817588426116)
XLA Ops:
  0.7 0.1 pad.13.clone
  0.7 0.8 rev.15
  1.5 0.7 pad_maximum_fusion.2
  2.2 0.1 rev.16
  2.3 0.1 slice.40
  2.3 0.1 rev.17
  2.4 0.7 pad_maximum_fusion.1.base
  3.1 1.5 pad_maximum_fusion.wts
  4.5 1.0 pad_add_fusion
  5.6 0.6 constant_dynamic-slice_fusion.taps
  6.2 2.5 shard_map.220
  8.6 49.3 %shard_map.221 = (bf16[2,256,512]{2,1,0:T(8,128)(2,1)}, bf16[4,512,256]{2,1,0:T(8,128)(2,1)}, bf16[2,2,192,256]{3,2,1,0:T(8,128)(2,1)}) custom-call(s32[2]{0:T(128)} %cnt.13, bf16[2,256,256]{2,1,0:T(8,128)(2,1)} %get-tuple-element.50.xpart, bf16[4,32,256]{2,1,0:T(8,128)(2,1)} %pad_maximum_fusion.wts, bf16[2,256,512]{2,1,0:T(8,128)(2,1)} %cot.5), custom_call_target="tpu_custom_call" | custom-call | tf_op jit(solution)/shard_map/pallas_call | solution.py:772
  57.9 5.1 %shard_map.222.half = f32[2,256,256]{2,1,0:T(8,128)} custom-call(s32[2]{0:T(128)} %cnt.13, bf16[2,256,512]{2,1,0:T(8,128)(2,1)} %cot.5, bf16[2,2,192,256]{3,2,1,0:T(8,128)(2,1)} %get-tuple-element.53.halo, f32[49,256]{1,0:T(8,128)} %constant_dynamic-slice_fusion.taps), custom_call_target="tpu_custom_call" | custom-call | tf_op jit(solution)/shard_map/pallas_call | solution.py:784
  63.1 4.0 %shard_map.223.dh = f32[2,256,512]{2,1,0:T(8,128)} custom-call(f32[2,256,256]{2,1,0:T(8,128)} %shard_map.222.half), custom_call_target="tpu_custom_call" | custom-call | tf_op jit(solution)/shard_map/pallas_call | solution.py:788
  67.1 9.6 %shard_map.224 = (bf16[2,256,256]{2,1,0:T(8,128)(2,1)}, bf16[2,256,256]{2,1,0:T(8,128)(2,1)}, bf16[2,256,256]{2,1,0:T(8,128)(2,1)}, bf16[2,256,256]{2,1,0:T(8,12...) custom-call(s32[2]{0:T(128)} %cnt.13, ...), custom_call_target="tpu_custom_call" | custom-call | tf_op jit(solution)/shard_map/pallas_call | solution.py:794
  76.7 22.6 %shard_map.225 = (bf16[16,144,256]{2,1,0:T(8,128)(2,1)}, bf16[2,2,2,16,256]{4,3,2,1,0:T(8,128)(2,1)}) custom-call(bf16[8,144,256]{2,1,0:T(8,128)(2,1)} %get-tuple-element.63.blk, bf16[2,2,2,16,256]{4,3,2,1,0:T(8,128)(2,1)} %get-tuple-element.64.hal), custom_call_target="tpu_custom_call" | custom-call | tf_op jit(solution)/shard_map/pallas_call | solution.py:802
  99.3 15.8 %shard_map.226 = (bf16[144,256]{1,0:T(8,128)(2,1)}, f32[2,64,256]{2,1,0:T(8,128)}) custom-call(bf16[16,144,256]{2,1,0:T(8,128)(2,1)} %get-tuple-element.65.recv, bf16[2,256,256]{2,1,0:T(8,128)(2,1)} %get-tuple-element.58.qlt, bf16[2,256,256]{2,1,0:T(8,128)(2,1)} %get-tuple-element.59.klt), custom_call_target="tpu_custom_call" | custom-call | tf_op jit(solution)/shard_map/pallas_call | solution.py:813
  115.2 26.0 %shard_map.227.res = bf16[8,144,256]{2,1,0:T(8,128)(2,1)} custom-call(bf16[144,256]{1,0:T(8,128)(2,1)} %get-tuple-element.66.res), custom_call_target="tpu_custom_call" | custom-call | tf_op jit(solution)/shard_map/pallas_call | solution.py:821
  141.2 13.7 %shard_map.228 = (bf16[2,256,512]{2,1,0:T(8,128)(2,1)}, bf16[2,256,512]{2,1,0:T(8,128)(2,1)}, bf16[2,256,512]{2,1,0:T(8,128)(2,1)}, bf16[4,512,256]{2,1,0:T(8,128)(2,1)}, f32[8,256]{1,0:T(8,128)}) custom-call(s32[2]{0:T(128)} %cnt.13, bf16[2,256,512]{2,1,0:T(8,128)(2,1)} %get-tuple-element.49.normed, bf16[2,256,512]{2,1,0:T(8,128)(2,1)} %get-tuple-element.51.xbar, ...), custom_call_target="tpu_custom_call" | custom-call | tf_op jit(solution)/shard_map/pallas_call | solution.py:827
  154.8 57.3 %shard_map.229 = (f32[2,256,256]{2,1,0:T(8,128)}, bf16[2,256,512]{2,1,0:T(8,128)(2,1)}, bf16[2,256,512]{2,1,0:T(8,128)(2,1)}, f32[4,32,256]{2,1,0:T(8,128)}, bf16[2,2,192,256]{3,2,1,0:T(8,128)(2,1)}) custom-call(s32[2]{0:T(128)} %cnt.13, bf16[2,256,512]{2,1,0:T(8,128)(2,1)} %tok.5, f32[1,512]{1,0:T(1,128)} %bitcast.23, ...), custom_call_target="tpu_custom_call" | custom-call | tf_op jit(solution)/shard_map/pallas_call | solution.py:838
  212.1 0.0 copy-start.1
  212.1 10.1 %shard_map.230 = (bf16[2,256,256]{2,1,0:T(8,128)(2,1)}, f32[2,256,512]{2,1,0:T(8,128)}, f32[56,256]{1,0:T(8,128)}, f32[8,512]{1,0:T(8,128)}) custom-call(s32[2]{0:T(128)} %cnt.13, f32[2,256,256]{2,1,0:T(8,128)} %get-tuple-element.73.hid, bf16[2,2,192,256]{3,2,1,0:T(8,128)(2,1)} %get-tuple-element.74.zhalo, bf16[2,256,512]{2,1,0:T(8,128)(2,1)} %cot.5, ...), custom_call_target="tpu_custom_call" | custom-call | tf_op jit(solution)/shard_map/pallas_call | solution.py:852
  222.2 0.0 copy-done.1
  222.2 0.6 slice_bitcast_fusion
  222.9 0.6 slice.43
  223.5 20.2 %shard_map.231 = (bf16[2,256,512]{2,1,0:T(8,128)(2,1)}, f32[56,512]{1,0:T(8,128)}, f32[8,512]{1,0:T(8,128)}) custom-call(bf16[2,256,256]{2,1,0:T(8,128)(2,1)} %get-tuple-element.78.outh, f32[56,256]{1,0:T(8,128)} %get-tuple-element.79.gk, f32[8,512]{1,0:T(8,128)} %get-tuple-element.80.small), custom_call_target="tpu_custom_call" | custom-call | tf_op jit(solution)/shard_map/pallas_call | solution.py:860
  243.7 0.9 reshape.31
  244.7 0.0 copy-start
  244.7 0.7 slice.44
  245.3 0.1 rev.18
  245.4 0.7 slice.45
  246.2 1.5 fusion
  247.6 0.1 rev.19
  247.7 0.7 pad_maximum_fusion.3
  248.4 0.6 slice.53
  249.0 0.6 slice.52
  249.7 1.9 copy.26
  251.5 0.0 copy-done
  (2 shorter events, 0.0 us)
Async XLA Ops:
  212.1 10.1 %copy-start.1 = (f32[4,32,256]{2,1,0:T(8,128)S(1)}, f32[4,32,256]{2,1,0:T(8,128)}, u32[]{:S(2)}) copy-start(f32[4,32,256]{2,1,0:T(8,128)} %get-tuple-element.84) | copy-start | bytes 393220
  244.7 6.9 %copy-start = (f32[7,7,512]{2,1,0:T(8,128)}, f32[7,7,512]{2,1,0:T(8,128)S(1)}, u32[]{:S(2)}) copy-start(f32[7,7,512]{2,1,0:T(8,128)S(1)} %reshape.31) | copy-start | bytes 301060

commit v2 on v1

v2 whole, which is shorter than its diff:
```python
import functools

import jax
import jax.numpy as jnp
from jax import lax
from jax.experimental import pallas as pl
from jax.experimental.pallas import tpu as pltpu
from jax.sharding import PartitionSpec as P

MESH = pl.DeviceIdType.MESH
GRID_W = 64
MARKS = 256
SWEEPS = 6
EPSILON = 1e-05
f32, bf16 = jnp.float32, jnp.bfloat16
VMEM = pl.BlockSpec(memory_space=pltpu.VMEM)
SMEM = pl.BlockSpec(memory_space=pltpu.SMEM)
DMA = pltpu.SemaphoreType.DMA
BLK = 144


def sds(shape, dtype=f32):
    return jax.ShapeDtypeStruct(shape, dtype)


def call(kernel, outs, specs, scratch=(), cid=None, vmem=56):
    extra = {} if cid is None else dict(collective_id=cid, has_side_effects=True)
    return pl.pallas_call(
        kernel,
        out_shape=outs,
        in_specs=specs,
        out_specs=jax.tree.map(lambda _: VMEM, outs),
        scratch_shapes=list(scratch),
        compiler_params=pltpu.CompilerParams(vmem_limit_bytes=vmem * 2**20, **extra),
    )


def mm(left, right, cl=1, cr=0):
    return lax.dot_general(left, right, (((cl,), (cr,)), ((), ())), preferred_element_type=f32)


def split(value):
    high = value.astype(bf16)
    return high, (value - high.astype(f32)).astype(bf16)


def split3(row):
    high = row.astype(bf16).astype(f32)
    rest = row - high
    mid = rest.astype(bf16).astype(f32)
    return [high, mid, rest - mid]


def mm3(left, right, cl=1, cr=0):
    (lh, ll), (rh, rl) = left, right
    return mm(lh, rh, cl, cr) + (mm(lh, rl, cl, cr) + mm(ll, rh, cl, cr))


def iota(shape, dim):
    return lax.broadcasted_iota(jnp.int32, shape, dim)


def edges(count, marks):
    return (marks * count + (MARKS - 1)) >> 8, ((marks + 1) * count + (MARKS - 1)) >> 8


def member(count, start, rows):
    low, high = edges(count, iota((MARKS, rows), 0))
    slot = iota((MARKS, rows), 1) + start
    return jnp.where((slot >= low) & (slot < high), 1.0, 0.0).astype(bf16)

OWNERS = (0, 3, 5, 6)


def place(n):
    me = lax.axis_index("seq")
    return me // (n // 2), lax.rem(me, n // 2), lax.rem(me + n // 2, n)


def head_of(g):
    return jnp.where(g == 0, 0, jnp.where(g == 3, 1, jnp.where(g == 5, 2, 3)))


def is_owner(g):
    return (g == 0) | (g == 3) | (g == 5) | (g == 6)


def my_half():
    return pl.ds(pl.multiple_of(lax.axis_index("head") * 256, 256), 256)


def block_start(n, g, b, rows):
    return (g + b * (n // 2)) * rows


def places(n, g, rows, shape, dim):
    at = iota(shape, dim)
    return at + g * rows + jnp.where(at >= rows, (n // 2 - 1) * rows, 0)


def norm_rows(x, gain, bias):
    x = x.astype(f32)
    xc = x - jnp.mean(x, axis=-1, keepdims=True)
    inv = lax.rsqrt(jnp.mean(xc * xc, axis=-1, keepdims=True) + EPSILON)
    return (xc * inv * gain + bias).astype(bf16)


def segment_sums(n, g, count, normed):
    rows = normed.shape[1]
    mine = my_half()
    return sum(mm(member(count, block_start(n, g, b, rows), rows), normed[b, :, mine]) for b in range(2))


def join_taps(kc, k7, k5, k3):
    mine = my_half()
    kc[...] = jnp.zeros_like(kc)
    for a in range(7):
        kc[a, 0:7] = k7[a, :, mine]
    for a in range(5):
        kc[a + 1, 1:6] = kc[a + 1, 1:6] + k5[a, :, mine]
    for a in range(3):
        kc[a + 2, 2:5] = kc[a + 2, 2:5] + k3[a, :, mine]


def load_grid(zs, pad, body, top, bottom):
    grid = body.shape[0] // GRID_W
    pad[...] = jnp.zeros_like(pad)
    pad[0:3, 8:8 + GRID_W] = top.reshape(3, GRID_W, 256)
    pad[3:3 + grid, 8:8 + GRID_W] = body.reshape(grid, GRID_W, 256)
    pad[3 + grid:6 + grid, 8:8 + GRID_W] = bottom.reshape(3, GRID_W, 256)
    for b in range(7):
        zs[b] = pad[:, 5 + b:5 + b + GRID_W, :]


def conv_row(zs, kc, i, flip):
    acc = jnp.zeros((GRID_W, 256), f32)
    for a in range(7):
        for b in range(7):
            ka, kb = (6 - a, 6 - b) if flip else (a, b)
            acc = acc + kc[ka, kb:kb + 1, :] * zs[b, i + a]
    return acc


def ends(n, top, bottom):
    me = lax.axis_index("seq")
    return jnp.where(me > 0, top.astype(f32), 0.0), jnp.where(me < n - 1, bottom.astype(f32), 0.0)


def back_conv(n, count, s, cot, halo, kc, dh, zs, pad):
    me = lax.axis_index("seq")
    rows = cot.shape[1]
    mine = my_half()
    top, bottom = ends(n, halo[0, s], halo[1, s])
    load_grid(zs, pad, cot[s, :, mine].astype(f32), top, bottom)

    @pl.loop(0, rows // GRID_W)
    def _(i):
        acc = conv_row(zs, kc, i, True)
        here = pl.ds(pl.multiple_of(i * GRID_W, GRID_W), GRID_W)
        slot = iota((GRID_W, 256), 0) + (me * rows + i * GRID_W)
        dh[s, here] = cot[s, here, mine].astype(f32) + jnp.where(slot < count, acc, 0.0)


def hidden_rows(count, s, tok, obias, part, hid):
    rows = tok.shape[1]
    mine = my_half()
    hid[s] = tok[s, :, mine].astype(f32) + part.astype(f32) + obias[:, mine]
    slot = iota((rows, 256), 0) + lax.axis_index("seq") * rows
    return jnp.where(slot < count, hid[s], 0.0)


def grid_forward(n, count, s, hid, halo, cot, kc, pbias, outh, zs, pad, gacc):
    rows = hid.shape[1]
    mine = my_half()
    slot = iota((rows, 256), 0) + lax.axis_index("seq") * rows
    top, bottom = ends(n, halo[0, s], halo[1, s])
    load_grid(zs, pad, jnp.where(slot < count, hid[s], 0.0), top, bottom)

    @pl.loop(0, rows // GRID_W)
    def _(i):
        here = pl.ds(pl.multiple_of(i * GRID_W, GRID_W), GRID_W)
        acc = conv_row(zs, kc, i, False)
        outh[s, here] = (hid[s, here] + acc + pbias[:, mine]).astype(bf16)
        g = cot[s, here, mine].astype(f32)
        for a in range(7):
            for b in range(7):
                part = (g * zs[b, i + a]).reshape(GRID_W // 8, 8, 256)
                gacc[a * 7 + b] = gacc[a * 7 + b] + jnp.sum(part, axis=0)


def grid_sums(gacc, dh, cot, gtaps, gk):
    mine = my_half()
    for t in range(49):
        gk[t:t + 1] = jnp.sum(gacc[t], axis=0, keepdims=True)
    gk[49:50] = jnp.sum(dh[0], axis=0, keepdims=True) + jnp.sum(dh[1], axis=0, keepdims=True)
    g = cot[0, :, mine].astype(f32) + cot[1, :, mine].astype(f32)
    gk[50:51] = jnp.sum(g, axis=0, keepdims=True)
    gk[51:55] = gtaps[0:4]
    gk[55:56] = jnp.zeros((1, 256), f32)


def norm_back(n, g, count, b, x, dn, dnr, eall, gain, small):
    rows = x.shape[1]
    low, high = edges(count, iota((MARKS, 512), 0))
    e = (eall[...].astype(f32) / (high - low).astype(f32)).astype(bf16)
    mem = member(count, block_start(n, g, b, rows), rows)
    total = (dn[b].astype(f32) + dnr[b].astype(f32)) + mm(mem, e, 0, 0)
    x = x[b].astype(f32)
    xc = x - jnp.mean(x, axis=-1, keepdims=True)
    inv = lax.rsqrt(jnp.mean(xc * xc, axis=-1, keepdims=True) + EPSILON)
    xh = xc * inv
    dg = total * gain[...]
    m1 = jnp.mean(dg, axis=-1, keepdims=True)
    m2 = jnp.mean(dg * xh, axis=-1, keepdims=True)
    small[0:1] = small[0:1] + jnp.sum(total * xh, axis=0, keepdims=True)
    small[1:2] = small[1:2] + jnp.sum(total, axis=0, keepdims=True)
    return (dg - m1 - xh * m2) * inv


def spill_kernels(gkall, k7o, k5o, k3o):
    for a in range(7):
        k7o[a] = gkall[7 * a:7 * a + 7]
    for a in range(5):
        k5o[a] = gkall[7 * a + 8:7 * a + 13]
    for a in range(3):
        k3o[a] = gkall[7 * a + 16:7 * a + 19]


def greet(peers, pair=True):
    sem = pltpu.get_barrier_semaphore()
    for peer in peers:
        pl.semaphore_signal(sem, inc=1, device_id={"seq": peer}, device_id_type=MESH)
    if pair:
        hd = lax.axis_index("head")
        pl.semaphore_signal(sem, inc=1, device_id={"head": 1 - hd}, device_id_type=MESH)
    pl.semaphore_wait(sem, len(peers) + (1 if pair else 0))


def everyone(n):
    me = lax.axis_index("seq")
    return [lax.rem(me + i, n) for i in range(n)]


def cube(n):
    half, g, _ = place(n)
    return [half * (n // 2) + lax.rem(g + i, n // 2) for i in range(n // 2)]


def remote(src, dst, sems, i, **where):
    return pltpu.make_async_remote_copy(
        src_ref=src, dst_ref=dst, send_sem=sems.at[0, i], recv_sem=sems.at[1, i], device_id=where, device_id_type=MESH
    )


def go(copies):
    for c in copies:
        c.start()
    return copies


def got(copies):
    for c in copies:
        c.wait_recv()


def sent(copies):
    for c in copies:
        c.wait_send()


def start_kernel(n, cnt, tok, cot, gain, bias, wqkv, wout, k7, k5, k3,
                 xblk, normed, xbar, wall, dh, dhrb,
                 wts, halo, xp, xr, xm, kc, zs, pad, dhs, s_w, s_t, s_h, s_v, s_x, s_g, s_p, s_d):
    half, g, partner = place(n)
    me = lax.axis_index("seq")
    other = 1 - half
    size = n // 2
    rows = tok.shape[1]
    mb, wr = MARKS // size, wts.shape[1]
    hd = lax.axis_index("head")
    mine = my_half()
    count = cnt[half]
    near, far = cube(n), everyone(n)
    wts[0:3] = wqkv[...]
    wts[3] = wout[...].astype(f32).T.astype(bf16)

    def wrow(device):
        return pl.ds(pl.multiple_of(device * wr, wr), wr)

    greet(far[1:])
    c_w = go([remote(wts, wall.at[:, wrow(me)], s_w, 0, seq=partner)])
    c_t = go([remote(tok.at[other, :, mine], xblk.at[half, :, mine], s_t, 0, seq=partner)])
    c_h = go([
        remote(cot.at[:, pl.ds(rows - 192, 192), mine], halo.at[0], s_h, 0, seq=far[1]),
        remote(cot.at[:, pl.ds(0, 192), mine], halo.at[1], s_h, 1, seq=far[n - 1]),
    ])
    wall[:, wrow(me)] = wts[...]
    xblk[half] = tok[half]
    normed[half] = norm_rows(tok[half], gain[...], bias[...])
    join_taps(kc, k7, k5, k3)
    got(c_w)
    c_v = []
    for i in range(1, size):
        c_v += go([remote(wts, wall.at[:, wrow(me)], s_v, 2 * i, seq=near[i])])
        c_v += go([remote(wall.at[:, wrow(partner)], wall.at[:, wrow(partner)], s_v, 2 * i + 1, seq=near[i])])
    got(c_t)
    c_p = go([remote(xblk.at[other, :, mine], xblk.at[other, :, mine], s_p, 0, head=1 - hd)])
    got(c_p)
    normed[other] = norm_rows(xblk[other], gain[...], bias[...])
    xp[...] = segment_sums(n, g, count, normed).astype(bf16)
    c_x = []
    for i in range(1, size):
        at = pl.ds(pl.multiple_of(lax.rem(g + i, size) * mb, mb), mb)
        c_x += go([remote(xp.at[at], xr.at[g], s_x, i, seq=near[i])])
    row = pl.ds(pl.multiple_of(g * mb, mb), mb)
    xr[pl.ds(g, 1)] = xp[row][None]
    got(c_h)
    back_conv(n, cnt[other], other, cot, halo, kc, dh, zs, pad)
    dhs[...] = dh[other].astype(bf16)
    c_d = go([remote(dhs, dhrb.at[half, :, mine], s_d, 0, seq=partner)])
    got(c_x)
    total = xr[0].astype(f32)
    for d in range(1, size):
        total = total + xr[d].astype(f32)
    low, high = edges(count, iota((mb, 256), 0) + g * mb)
    xm[...] = (total / (high - low).astype(f32)).astype(bf16)
    xbar[row, mine] = xm[...]
    c_g = go([remote(xm, xbar.at[row, mine], s_g, i, seq=near[i]) for i in range(1, size)])
    back_conv(n, cnt[half], half, cot, halo, kc, dh, zs, pad)
    dhrb[half, :, mine] = dh[half].astype(bf16)
    got(c_g)
    c_p += go([remote(xbar.at[:, mine], xbar.at[:, mine], s_p, 1, head=1 - hd)])
    got(c_d)
    c_p += go([remote(dhrb.at[:, :, mine], dhrb.at[:, :, mine], s_p, 2, head=1 - hd)])
    got(c_v)
    got(c_p[1:])
    sent(c_w + c_t + c_h + c_v + c_x + c_d + c_g + c_p)


def reduce_kernel(n, blk, hal, recv, hrecv, s_b, s_h):
    half, g, _ = place(n)
    size = n // 2
    near = cube(n)
    greet(near[1:], False)

    def to(h, d):
        return pltpu.make_async_remote_copy(
            src_ref=blk.at[h], dst_ref=recv.at[d], send_sem=s_b.at[0, h], recv_sem=s_b.at[1, d],
            device_id={"seq": half * size + OWNERS[h]}, device_id_type=MESH,
        )

    for h, o in enumerate(OWNERS):

        @pl.when(g != o)
        def _():
            to(h, g).start()

        @pl.when(g == o)
        def _():
            recv[pl.ds(g, 1)] = blk[h:h + 1]

    c_h = go([
        remote(hal.at[1], hrecv.at[0], s_h, 0, seq=near[1]),
        remote(hal.at[0], hrecv.at[1], s_h, 1, seq=near[size - 1]),
    ])
    for c in c_h:
        c.wait()
    for h, o in enumerate(OWNERS):

        @pl.when(g != o)
        def _():
            to(h, g).wait_send()

        @pl.when(g == o)
        def _():
            for d in range(size):
                if d != o:
                    to(h, d).wait_recv()


def spread_kernel(n, res, out, s_r):
    half, g, _ = place(n)
    size = n // 2
    near = cube(n)
    greet(near[1:], False)

    def to(h, i):
        return pltpu.make_async_remote_copy(
            src_ref=res, dst_ref=out.at[h], send_sem=s_r.at[0, i], recv_sem=s_r.at[1, h],
            device_id={"seq": near[i]}, device_id_type=MESH,
        )

    for h, o in enumerate(OWNERS):

        @pl.when(g == o)
        def _():
            for i in range(1, size):
                to(h, i).start()
            out[h] = res[...]

    for h, o in enumerate(OWNERS):

        @pl.when(g != o)
        def _():
            to(h, 1).wait_recv()

        @pl.when(g == o)
        def _():
            for i in range(1, size):
                to(h, i).wait_send()


def late_kernel(n, cnt, tok, cot, xblk, dh, po, ep, dn, wpart, gtaps, gain, obias, pbias, k7, k5, k3,
                out, gx, gwqkv, gwout, sums, gkall, k7o, k5o, k3o,
                er, es, erv, em, eall, por, ps, psr, dnr, dhr, hid, z, halo, lnb, lnr, lns, wrv, wsum, wone,
                kc, zs, pad, gacc, outh, gk, gkr, gkm, small, smr, smx,
                s_a, s_e, s_g, s_o, s_z, s_l, s_w, s_v, s_k, s_b, s_s):
    half, g, partner = place(n)
    me = lax.axis_index("seq")
    other = 1 - half
    size = n // 2
    rows = tok.shape[1]
    mb, wr = MARKS // size, wone.shape[1]
    hd = lax.axis_index("head")
    mine = my_half()
    theirs = pl.ds(pl.multiple_of((1 - hd) * 256, 256), 256)
    count = cnt[half]
    near, far = cube(n), everyone(n)
    greet(far[1:])
    c_a = go([
        remote(ep.at[:, theirs], er, s_a, 0, head=1 - hd),
        remote(po.at[:, :, theirs], por, s_a, 1, head=1 - hd),
        remote(dn, dnr, s_a, 2, head=1 - hd),
        remote(dh, dhr, s_a, 3, head=1 - hd),
    ])
    got(c_a[0:1])
    es[...] = (ep[:, mine].astype(f32) + er[...].astype(f32)).astype(bf16)
    c_e = []
    for i in range(1, size):
        at = pl.ds(pl.multiple_of(lax.rem(g + i, size) * mb, mb), mb)
        c_e += go([remote(es.at[at], erv.at[g], s_e, i, seq=near[i])])
    row = pl.ds(pl.multiple_of(g * mb, mb), mb)
    erv[pl.ds(g, 1)] = es[row][None]
    got(c_a[1:2])
    ps[...] = (po[:, :, mine].astype(f32) + por[...].astype(f32)).astype(bf16)
    c_o = go([remote(ps.at[other], psr, s_o, 0, seq=partner)])
    join_taps(kc, k7, k5, k3)
    small[...] = jnp.zeros_like(small)
    gacc[...] = jnp.zeros_like(gacc)
    got(c_e)
    total = erv[0].astype(f32)
    for d in range(1, size):
        total = total + erv[d].astype(f32)
    em[...] = total.astype(bf16)
    eall[row, mine] = em[...]
    c_g = go([remote(em, eall.at[row, mine], s_g, i, seq=near[i]) for i in range(1, size)])

    def wrow(device):
        return pl.ds(pl.multiple_of(device * wr, wr), wr)

    c_w = []
    for i in range(1, size):
        for k, device in enumerate((near[i], lax.rem(near[i] + size, n))):
            c_w += go([remote(wpart.at[:, wrow(device)], wrv.at[g, k], s_w, 2 * i + k, seq=near[i])])
    wrv[pl.ds(g, 1), 0] = wpart[:, wrow(me)][None]
    wrv[pl.ds(g, 1), 1] = wpart[:, wrow(partner)][None]
    z[half] = hidden_rows(count, half, tok, obias, ps[half], hid).astype(bf16)
    got(c_o)
    z[other] = hidden_rows(cnt[other], other, tok, obias, psr[...], hid).astype(bf16)
    c_z = go([
        remote(z.at[:, pl.ds(rows - 192, 192)], halo.at[0], s_z, 0, seq=far[1]),
        remote(z.at[:, pl.ds(0, 192)], halo.at[1], s_z, 1, seq=far[n - 1]),
    ])
    got(c_g)
    c_a += go([remote(eall.at[:, mine], eall.at[:, mine], s_a, 4, head=1 - hd)])
    got(c_a[2:5])
    lnb[...] = norm_back(n, g, count, other, xblk, dn, dnr, eall, gain, small)
    lns[...] = lnb[:, mine].astype(bf16)
    c_l = go([remote(lns, lnr.at[:, mine], s_l, 0, seq=partner)])
    lnb[...] = norm_back(n, g, count, half, xblk, dn, dnr, eall, gain, small)
    gx[half, :, mine] = dh[half] + lnb[:, mine]
    gx[half, :, theirs] = dhr[half] + lnb[:, theirs]
    for a in range(2):
        for b in range(4):
            smx[4 * a + b:4 * a + b + 1] = small[a:a + 1, 128 * b:128 * b + 128]
    c_s = go([remote(smx, smr.at[me], s_s, i, seq=far[i]) for i in range(1, n)])
    smr[pl.ds(me, 1)] = smx[...][None]
    got(c_l)
    c_l += go([remote(lnr.at[:, mine], lnr.at[:, mine], s_l, 1, head=1 - hd)])
    got(c_z)
    for s in range(2):
        grid_forward(n, cnt[s], s, hid, halo, cot, kc, pbias, outh, zs, pad, gacc)
    c_l += go([remote(outh, out.at[:, :, mine], s_l, 2, head=1 - hd)])
    out[:, :, mine] = outh[...]
    grid_sums(gacc, dh, cot, gtaps, gk)
    blocks = gk.shape[0] // 8

    def to(b, d):
        return pltpu.make_async_remote_copy(
            src_ref=gk.at[pl.ds(8 * b, 8)], dst_ref=gkr.at[d], send_sem=s_k.at[0, b], recv_sem=s_k.at[1, d],
            device_id={"seq": b}, device_id_type=MESH,
        )

    def back(b, i):
        return pltpu.make_async_remote_copy(
            src_ref=gkm, dst_ref=gkall.at[pl.ds(8 * b, 8), mine], send_sem=s_b.at[0, i], recv_sem=s_b.at[1, b],
            device_id={"seq": far[i]}, device_id_type=MESH,
        )

    for b in range(blocks):

        @pl.when(me != b)
        def _():
            to(b, me).start()

    got(c_w)
    for k in (1, 0):
        total = wrv[0, k].astype(f32)
        for d in range(1, size):
            total = total + wrv[d, k].astype(f32)
        if k == 1:
            wsum[...] = total.astype(bf16)
            c_v = go([remote(wsum, wone, s_v, 0, seq=partner)])
    for b in range(blocks):

        @pl.when(me == b)
        def _():
            gkr[pl.ds(me, 1)] = gk[pl.ds(8 * b, 8)][None]
            for d in range(n):
                if d != b:
                    to(b, d).wait_recv()
            gsum = gkr[0]
            for d in range(1, n):
                gsum = gsum + gkr[d]
            gkm[...] = gsum
            gkall[pl.ds(8 * b, 8), mine] = gsum
            for i in range(1, n):
                back(b, i).start()

    got(c_l[1:2])
    gx[other, :, mine] = dh[other] + lnr[:, mine].astype(f32)
    gx[other, :, theirs] = dhr[other] + lnr[:, theirs].astype(f32)
    got(c_s)
    acc = smr[0]
    for d in range(1, n):
        acc = acc + smr[d]
    sums[...] = acc
    got(c_v)
    total = total + wone[...].astype(f32)
    gwqkv[...] = total[0:3]
    gwout[...] = total[3].T
    for b in range(blocks):

        @pl.when(me != b)
        def _():
            back(b, 0).wait_recv()
            to(b, me).wait_send()

        @pl.when(me == b)
        def _():
            for i in range(1, n):
                back(b, i).wait_send()

    c_k = go([remote(gkall.at[:, mine], gkall.at[:, mine], s_l, 3, head=1 - hd)])
    got(c_k)
    spill_kernels(gkall, k7o, k5o, k3o)
    got(c_l[2:])
    sent(c_a + c_e + c_o + c_g + c_w + c_z + c_l + c_s + c_v + c_k)


def scores_kernel(n, cnt, normed, xbar, wall, dhrb, qt, kt, vt, qlt, klt, dot, wback, a1, e3, blk, hal):
    half, g, _ = place(n)
    rows = normed.shape[1]
    wide = 2 * rows
    count = cnt[half]
    scale = 64 ** -0.5
    wback[...] = wall[3].astype(f32).T.astype(bf16)
    nr = normed[...].reshape(wide, 512)
    dhr = dhrb[...].reshape(wide, 512)
    qt[...] = mm(wall[0], nr, 0, 1).astype(bf16)
    kt[...] = mm(wall[1], nr, 0, 1).astype(bf16)
    slots = places(n, g, rows, (256, wide), 1)
    vt[...] = jnp.where(slots < count, mm(wall[2], nr, 0, 1), 0.0).astype(bf16)
    qlt[...] = mm(wall[0], xbar[...], 0, 1).astype(bf16)
    klt[...] = mm(wall[1], xbar[...], 0, 1).astype(bf16)
    dot[...] = mm(wback[...], dhr, 1, 1).astype(bf16)
    for b in range(2):
        for side, first in ((0, 0), (1, rows - 16)):
            slot = iota((16, 256), 0) + (block_start(n, g, b, rows) + first)
            v = mm(normed[b, first:first + 16], wall[2])
            hal[side, b, 0] = jnp.where(slot < count, v, 0.0).astype(bf16)
            hal[side, b, 1] = mm(dhrb[b, first:first + 16], wback[...], 1, 1).astype(bf16)
    ok = places(n, g, rows, (wide, MARKS), 0) < count

    @pl.loop(0, 4)
    def _(h):
        here = pl.ds(pl.multiple_of(h * 64, 64), 64)
        s1 = mm(klt[here] * scale, qt[here], 0, 0)
        e1 = jnp.exp(s1 - jnp.max(s1, axis=0, keepdims=True))
        a = (e1 / jnp.sum(e1, axis=0, keepdims=True)).astype(bf16)
        a1[h] = a
        blk[h, 64:128] = mm(dot[here], a, 1, 1).astype(bf16)
        s3 = jnp.where(ok, mm(kt[here] * scale, qlt[here], 0, 0), -1e30)
        top = jnp.max(s3, axis=0, keepdims=True)
        e = jnp.where(ok, jnp.exp(s3 - top), 0.0)
        total = jnp.sum(e, axis=0, keepdims=True)
        er = e.astype(bf16)
        e3[h] = er
        blk[h, 0:64] = mm(vt[here], er).astype(bf16)
        stat = jnp.concatenate(split3(top) + split3(total) + [jnp.zeros((10, MARKS), f32)], axis=0)
        blk[h, 128:144] = stat.astype(bf16)


def three(stat, first):
    return (stat[first:first + 1] + stat[first + 1:first + 2]) + stat[first + 2:first + 3]


def chain_kernel(n, recv, qlt, klt, res, dqz, ps, ts, xs):
    _, g, _ = place(n)
    h = head_of(g)
    here = pl.ds(pl.multiple_of(h * 64, 64), 64)
    scale = 64 ** -0.5
    parts = recv.shape[0]
    dqz[...] = jnp.zeros_like(dqz)

    @pl.when(is_owner(g))
    def _():
        tops = [three(recv[d, 128:144].astype(f32), 0) for d in range(parts)]
        top = functools.reduce(jnp.maximum, tops)
        total, value, dct = 0.0, 0.0, 0.0
        for d in range(parts):
            w = jnp.exp(tops[d] - top)
            total = total + three(recv[d, 128:144].astype(f32), 3) * w
            value = value + recv[d, 0:64].astype(f32) * w
            dct = dct + recv[d, 64:128].astype(f32)
        value = value / total
        ql, kl = qlt[here], klt[here]
        s2 = mm(ql * scale, kl, 0, 0)
        e2 = jnp.exp(s2 - jnp.max(s2, axis=1, keepdims=True))
        a = e2 / jnp.sum(e2, axis=1, keepdims=True)
        asp = split(a)
        cs, rs = jnp.sum(a, axis=0, keepdims=True), jnp.sum(a, axis=1, keepdims=True)
        cm, rm = jnp.max(cs, axis=1, keepdims=True), jnp.max(rs, axis=0, keepdims=True)
        inv = 1.0 / (cm * rm)
        p = mm3(asp, asp, 1, 1) * inv
        x = value
        for k in range(SWEEPS):
            psp = split(p)
            t = mm3(psp, psp)
            tsp = split(t)
            ps[k, 0], ps[k, 1] = psp
            ts[k, 0], ts[k, 1] = tsp
            xs[k] = x
            if k < SWEEPS - 1:
                p = 0.25 * (13.0 * p - 15.0 * t + mm3(tsp, split(7.0 * p - t)))
            xt = mm3(split(x), tsp)
            x = 0.25 * (13.0 * x + 7.0 * xt - mm3(split(15.0 * x + xt), psp))
        ct = mm3(split(x), asp) * inv
        res[0:64] = ct.astype(bf16)
        dcs = split(dct)
        y = mm3(dcs, asp, 1, 1) * inv
        da = mm3(split(x), dcs, 0, 0) * inv
        ds = -jnp.sum(jnp.sum(dct * ct, axis=0, keepdims=True), axis=1, keepdims=True) * inv * (cm * rm) * inv
        e = None
        for k in range(SWEEPS - 1, -1, -1):
            psp = (ps[k, 0], ps[k, 1])
            tsp = (ts[k, 0], ts[k, 1])
            outer = mm3(split(y), split(xs[k]), 0, 0) * 0.125
            d = outer + outer.T
            pd = mm3(psp, split(d))
            if e is None:
                v = 7.0 * pd
                w = -d
                new = -15.0 * d + mm3(split(-pd), psp)
                half = mm3(tsp, split(w))
            else:
                eq = 0.25 * e
                pe = mm3(psp, split(eq))
                v = 7.0 * pd - 15.0 * pe
                new = 13.0 * eq - 15.0 * d + mm3(split(7.0 * pe - pd), psp)
                half = mm3(tsp, split(7.0 * eq - d - (pe + pe.T)))
            half = half + v
            e = new + (half + half.T)
            yt = mm3(split(y), tsp)
            y = 0.25 * (13.0 * y + 7.0 * yt - mm3(split(15.0 * y + yt), psp))
        dbr = y.astype(bf16)
        res[64:128] = dbr
        rt = jnp.sum(dbr.astype(f32) * value, axis=0, keepdims=True)
        stat = jnp.concatenate(split3(top) + split3(total) + split3(rt) + [jnp.zeros((7, MARKS), f32)], axis=0)
        res[128:144] = stat.astype(bf16)
        da = da + mm3(split(e), asp) * (2.0 * inv)
        p0 = ps[0, 0].astype(f32) + ps[0, 1].astype(f32)
        ds = ds - jnp.sum(jnp.sum(e * p0, axis=0, keepdims=True), axis=1, keepdims=True) * inv
        eqc, eqr = jnp.where(cs == cm, 1.0, 0.0), jnp.where(rs == rm, 1.0, 0.0)
        da = da + (ds * rm) * (eqc / jnp.sum(eqc, axis=1, keepdims=True))
        da = da + (ds * cm) * (eqr / jnp.sum(eqr, axis=0, keepdims=True))
        dsc = a * (da - jnp.sum(a * da, axis=1, keepdims=True)) * scale
        dh, dl = split(dsc)
        dqz[0] = mm(kl, dh, 1, 1) + mm(kl, dl, 1, 1)
        dqz[1] = mm(ql, dh) + mm(ql, dl)


def band(base, shift, rows):
    wide = jnp.broadcast_to(base, (rows, 256))
    return pltpu.roll(wide, shift, 1, stride=1, stride_axis=0)


def diagonals(g, shift):
    return jnp.sum(pltpu.roll(g, shift, 1, stride=1, stride_axis=0), axis=0, keepdims=True)


def ring_ends(n, g, b, hrecv, k):
    top = jnp.where(g > 0, hrecv[0, b, k].astype(f32), hrecv[0, 0, k].astype(f32) if b else 0.0)
    bottom = jnp.where(g < n // 2 - 1, hrecv[1, b, k].astype(f32), 0.0 if b else hrecv[1, 1, k].astype(f32))
    return top, bottom


def grads_kernel(n, cnt, normed, xbar, wall, wback, dhrb, qt, kt, vt, qlt, klt, dot, a1, e3, blk, res, hrecv, taps, dqz,
                 po, dn, ep, wpart, gtaps, att, dp, dlm, gsum, tm, th, ht, vr):
    half, g, _ = place(n)
    rows = normed.shape[1]
    wide = 2 * rows
    count = cnt[half]
    scale = 64 ** -0.5
    pi, pj = iota((rows, rows), 0), iota((rows, rows), 1)
    inside = (pi - pj <= 16) & (pj - pi <= 16)
    hi, hj = iota((32, rows), 0), iota((32, rows), 1)
    far = jnp.where(hi < 16, hi - hj, hj - hi - (rows - 32)) >= 0
    ti, tl = iota((33, 256), 0), iota((33, 256), 1)
    spots = [jnp.where(((ti + tl if f == 0 else tl - ti + 32) & 255) == 16, 1.0, 0.0).astype(bf16) for f in range(2)]
    pieces = [piece.astype(bf16) for piece in split3(taps[...])]
    for f in range(2):
        lines = mm(pieces[0], spots[f]) + mm(pieces[1], spots[f]) + mm(pieces[2], spots[f])
        for h in range(4):
            line = lines[h:h + 1, :]
            full = jnp.where(inside, band(line, 0, rows), 0.0)
            tm[f, h, 0], tm[f, h, 1] = split(full)
            both = jnp.concatenate([band(line, 240, 16), band(line, 0, 16)], axis=0)
            th[f, h, 0], th[f, h, 1] = split(jnp.where(far, both, 0.0))
    gsum[...] = jnp.zeros_like(gsum)
    mirror = jnp.where(pi + pj == rows - 1, 1.0, 0.0).astype(bf16)
    si, sj = iota((32, 32), 0), iota((32, 32), 1)
    mirror32 = jnp.where(si + sj == jnp.where(si < 16, 15, 47), 1.0, 0.0).astype(bf16)
    for b in range(2):
        for k in range(2):
            top, bottom = ring_ends(n, g, b, hrecv, k)
            ht[k, b] = jnp.concatenate([top, bottom], axis=0).T.astype(bf16)
        vr[b] = mm(vt[:, b * rows:(b + 1) * rows], mirror).astype(bf16)
        ht[2, b] = mm(ht[0, b], mirror32).astype(bf16)
    mine = head_of(g)
    use = jnp.where(is_owner(g), 1.0, 0.0)
    slots = places(n, g, rows, (64, wide), 1)

    @pl.loop(0, 4)
    def _(h):
        here = pl.ds(pl.multiple_of(h * 64, 64), 64)
        ct, dbt = res[h, 0:64], res[h, 64:128]
        stat = res[h, 128:144].astype(f32)
        own = three(blk[h, 128:144].astype(f32), 0)
        factor = jnp.exp(own - three(stat, 0)) / three(stat, 3)
        rt = three(stat, 6)
        do, v = dot[here], vt[here]
        conv, dconv = [], []
        for b in range(2):
            part = slice(b * rows, (b + 1) * rows)
            vb, db, vh, dh = v[:, part], do[:, part], ht[0, b, here], ht[1, b, here]
            conv.append(mm(vb, tm[0, h, 0]) + mm(vb, tm[0, h, 1]) + mm(vh, th[0, h, 0]) + mm(vh, th[0, h, 1]))
            dconv.append(mm(db, tm[1, h, 0]) + mm(db, tm[1, h, 1]) + mm(dh, th[1, h, 0]) + mm(dh, th[1, h, 1]))
            gsum[h, 0:rows] = gsum[h, 0:rows] + mm(vr[b, here], db, 0, 0)
            gsum[h, rows:rows + 32] = gsum[h, rows:rows + 32] + mm(ht[2, b, here], db, 0, 0)
        a = a1[h]
        af = a.astype(f32)
        att[here] = (mm(ct, a) + jnp.concatenate(conv, axis=1)).astype(bf16)
        da = mm(ct, do, 0, 0)
        d1 = (af * (da - jnp.sum(af * da, axis=0, keepdims=True))).astype(bf16)
        dp[0, here] = mm(klt[here] * scale, d1).astype(bf16)
        own_chain = jnp.where(h == mine, use, 0.0)
        dlm[1, here] = (mm(qt[here] * scale, d1, 1, 1) + own_chain * dqz[1]).astype(bf16)
        a3 = e3[h].astype(f32) * factor
        d3 = (a3 * (mm(v, dbt, 0, 0) - rt)).astype(bf16)
        dlm[0, here] = (mm(kt[here] * scale, d3) + own_chain * dqz[0]).astype(bf16)
        dp[1, here] = mm(qlt[here] * scale, d3, 1, 1).astype(bf16)
        dv = mm(dbt, a3.astype(bf16), 1, 1) + jnp.concatenate(dconv, axis=1)
        dp[2, here] = jnp.where(slots < count, dv, 0.0).astype(bf16)

    ep[...] = (mm(wall[0], dlm[0]) + mm(wall[1], dlm[1])).T.astype(bf16)
    po[...] = mm(att[...], wback[...], 0, 0).astype(bf16).reshape(2, rows, 512)
    d = mm(wall[0], dp[0]) + mm(wall[1], dp[1]) + mm(wall[2], dp[2])
    dn[...] = d.T.astype(bf16).reshape(2, rows, 512)
    nr = normed[...].reshape(wide, 512)
    for j in range(3):
        grad = mm(dp[j], nr)
        if j < 2:
            grad = grad + mm(dlm[j], xbar[...])
        wpart[j] = grad.T.astype(bf16)
    wpart[3] = mm(att[...], dhrb[...].reshape(wide, 512)).T.astype(bf16)
    near = (pi + pj >= rows - 17) & (pi + pj <= rows + 15)
    beyond = jnp.where(hi < 16, 15 - hi - hj, hi + hj - (rows + 15)) >= 0
    for h in range(4):
        s = jnp.where(near, gsum[h, 0:rows], 0.0)
        sh = jnp.where(beyond, gsum[h, rows:rows + 32], 0.0)
        gtaps[h:h + 1, :] = diagonals(s, 1) + diagonals(sh[0:16], 1) + diagonals(sh[16:32], 241)
    gtaps[4:8, :] = jnp.zeros((4, 256), f32)


def ring(rows_up, rows_down):
    count = lax.axis_size("seq")
    up = lax.ppermute(rows_up, "seq", [(i, (i + 1) % count) for i in range(count)])
    down = lax.ppermute(rows_down, "seq", [((i + 1) % count, i) for i in range(count)])
    return jnp.stack([up, down])


def half_of(full, axis):
    return lax.dynamic_slice_in_dim(full, lax.axis_index("head") * 256, 256, axis)


def swap(n, blocks):
    half, _, _ = place(n)
    theirs = lax.ppermute(jnp.where(half == 0, blocks[1], blocks[0]), "seq", [(i, (i + n // 2) % n) for i in range(n)])
    own = jnp.where(half == 0, blocks[0], blocks[1])
    return jnp.where(half == 0, jnp.stack([own, theirs]), jnp.stack([theirs, own]))


def half_sum(n, value):
    half, _, _ = place(n)
    pair = lax.psum(jnp.stack([jnp.where(half == s, value, 0.0) for s in range(2)]), "seq")
    return jnp.where(half == 0, pair[0], pair[1])


def half_max(n, value):
    half, _, _ = place(n)
    pair = lax.pmax(jnp.stack([jnp.where(half == s, value, -jnp.inf) for s in range(2)]), "seq")
    return jnp.where(half == 0, pair[0], pair[1])


def norm_kernel(n, cnt, xblk, gain, bias, normed, xp):
    half, g, _ = place(n)
    for b in range(2):
        normed[b] = norm_rows(xblk[b], gain[...], bias[...])
    xp[...] = segment_sums(n, g, cnt[half], normed)


def back_conv_kernel(n, cnt, cot, halo, k7, k5, k3, dh, kc, zs, pad):
    join_taps(kc, k7, k5, k3)
    for s in range(2):
        back_conv(n, cnt[s], s, cot, halo, kc, dh, zs, pad)


def start_plain(n, counts, tok, cot, gain, bias, wqkv, wout, k7, k5, k3, scratch):
    half, _, _ = place(n)
    rows = tok.shape[1]
    count = counts[half]
    xblk = swap(n, tok)
    normed, xp = call(
        functools.partial(norm_kernel, n), [sds((2, rows, 512), bf16), sds((MARKS, 256))], [SMEM] + [VMEM] * 3
    )(counts, xblk, gain, bias)
    low, high = edges(count, jnp.arange(MARKS, dtype=jnp.int32))
    xbar = (half_sum(n, xp) / (high - low).astype(f32)[:, None]).astype(bf16)
    xbar = lax.all_gather(xbar, "head", axis=1, tiled=True)
    wts = jnp.concatenate([wqkv, wout.T[None]], axis=0)
    wall = lax.all_gather(wts, "seq", axis=1, tiled=True)
    mine = half_of(cot, 2)
    dh = call(functools.partial(back_conv_kernel, n), sds((2, rows, 256)), [SMEM] + [VMEM] * 5, scratch)(
        counts, cot, ring(mine[:, -192:], mine[:, :192]), k7, k5, k3
    )
    dhrb = swap(n, lax.all_gather(dh.astype(bf16), "head", axis=2, tiled=True))
    return xblk, normed, xbar, wall, dh, dhrb


def half_ring(n, hal):
    size = n // 2
    up = [(i, i // size * size + (i + 1) % size) for i in range(n)]
    return jnp.stack([lax.ppermute(hal[1], "seq", up), lax.ppermute(hal[0], "seq", [(j, i) for i, j in up])])


def three_rows(stat, first):
    return (stat[:, first:first + 1] + stat[:, first + 1:first + 2]) + stat[:, first + 2:first + 3]


def reduce_plain(n, blk, hal):
    _, g, _ = place(n)
    stat = blk[:, 128:].astype(f32)
    top, total = three_rows(stat, 0), three_rows(stat, 3)
    best = half_max(n, top)
    w = jnp.exp(top - best)
    total = half_sum(n, total * w)
    value = half_sum(n, blk[:, 0:64].astype(f32) * w)
    dct = half_sum(n, blk[:, 64:128].astype(f32))
    stat = jnp.concatenate(split3(best) + split3(total) + [jnp.zeros((4, 10, MARKS), f32)], axis=1)
    whole = jnp.concatenate([value, dct, stat], axis=1).astype(bf16)
    return lax.dynamic_slice_in_dim(whole, head_of(g), 1, 0), half_ring(n, hal)


def spread_plain(n, res):
    _, g, _ = place(n)
    held = ((jnp.arange(4) == head_of(g)) & is_owner(g))[:, None, None]
    return half_sum(n, jnp.where(held, res[None].astype(f32), 0.0)).astype(bf16)


def hidden_kernel(cnt, tok, obias, part, hid, z):
    for s in range(2):
        z[s] = hidden_rows(cnt[s], s, tok, obias, part[s], hid).astype(bf16)


def final_kernel(n, cnt, hid, halo, cot, k7, k5, k3, pbias, xblk, dn, dnr, eall, gain, dh, gtaps,
                 outh, lnb, gk, small, kc, zs, pad, gacc):
    half, g, _ = place(n)
    join_taps(kc, k7, k5, k3)
    gacc[...] = jnp.zeros_like(gacc)
    small[...] = jnp.zeros_like(small)
    for s in range(2):
        grid_forward(n, cnt[s], s, hid, halo, cot, kc, pbias, outh, zs, pad, gacc)
    grid_sums(gacc, dh, cot, gtaps, gk)
    for b in range(2):
        lnb[b] = norm_back(n, g, cnt[half], b, xblk, dn, dnr, eall, gain, small)


def late_plain(n, counts, tok, cot, xblk, dh, po, ep, dn, wpart, gtaps, gain, obias, pbias, k7, k5, k3, scratch):
    rows = tok.shape[1]
    part = half_of(swap(n, lax.psum(po.astype(f32), "head").astype(bf16)), 2)
    hid, z = call(hidden_kernel, [sds((2, rows, 256)), sds((2, rows, 256), bf16)], [SMEM] + [VMEM] * 3)(
        counts, tok, obias, part
    )
    dnr = lax.ppermute(dn, "head", [(0, 1), (1, 0)])
    eall = half_sum(n, lax.psum(ep.astype(f32), "head")).astype(bf16)
    outh, lnb, gk, small = call(
        functools.partial(final_kernel, n),
        [sds((2, rows, 256), bf16), sds((2, rows, 512)), sds((56, 256)), sds((8, 512))],
        [SMEM] + [VMEM] * 14,
        scratch + [pltpu.VMEM((49, 8, 256), f32)],
    )(counts, hid, ring(z[:, -192:], z[:, :192]), cot, k7, k5, k3, pbias, xblk, dn, dnr, eall, gain, dh, gtaps)
    out = lax.all_gather(outh, "head", axis=2, tiled=True)
    gx = lax.all_gather(dh, "head", axis=2, tiled=True) + swap(n, lnb)
    gw = lax.psum_scatter(wpart.astype(f32), "seq", scatter_dimension=1, tiled=True)
    gk, small = lax.psum((gk, small), "seq")
    gkall = lax.all_gather(gk, "head", axis=1, tiled=True)
    k7o = gkall[:49].reshape(7, 7, 512)
    return out, gx, gw[0:3], gw[3].T, small[0:2].reshape(8, 128), gkall, k7o, k7o[1:6, 1:6], k7o[2:5, 2:5]


def sem(count):
    return DMA((2, count))


def shards(n, tokens, counts, ln_gain, ln_bias, w_qkv, conv_taps, w_out, out_bias, kernel7, kernel5, kernel3, ppeg_bias, cotangent):
    rows = tokens.shape[1]
    direct = n == 16
    size = n // 2
    grid = rows // GRID_W
    wide = 2 * rows
    mb, wr = MARKS // size, w_qkv.shape[1]
    gain, bias, obias, pbias = (v[None, :] for v in (ln_gain, ln_bias, out_bias, ppeg_bias))
    kernels = (kernel7, kernel5, kernel3)
    scratch = [
        pltpu.VMEM((7, 8, 256), f32),
        pltpu.VMEM((7, grid + 6, GRID_W, 256), f32),
        pltpu.VMEM((grid + 6, GRID_W + 16, 256), f32),
    ]
    blocks = sds((2, rows, 512), bf16)

    if direct:
        xblk, normed, xbar, wall, dh, dhrb = call(
            functools.partial(start_kernel, n),
            [blocks, blocks, sds((MARKS, 512), bf16), sds((4, 512, 256), bf16), sds((2, rows, 256)), blocks],
            [SMEM] + [VMEM] * 9,
            [pltpu.VMEM((4, wr, 256), bf16), pltpu.VMEM((2, 2, 192, 256), bf16), pltpu.VMEM((MARKS, 256), bf16),
             pltpu.VMEM((size, mb, 256), bf16), pltpu.VMEM((mb, 256), bf16)] + scratch
            + [pltpu.VMEM((rows, 256), bf16)]
            + [sem(1), sem(1), sem(2), sem(2 * size), sem(size), sem(size), sem(3), sem(1)],
            cid=0,
        )(counts, tokens, cotangent, gain, bias, w_qkv, w_out, *kernels)
    else:
        xblk, normed, xbar, wall, dh, dhrb = start_plain(
            n, counts, tokens, cotangent, gain, bias, w_qkv, w_out, *kernels, scratch
        )

    t2, m2 = sds((256, wide), bf16), sds((256, MARKS), bf16)
    qt, kt, vt, qlt, klt, dot, wback, a1, e3, blk, hal = call(
        functools.partial(scores_kernel, n),
        [t2, t2, t2, m2, m2, t2, sds((256, 512), bf16), sds((4, MARKS, wide), bf16), sds((4, wide, MARKS), bf16),
         sds((4, BLK, MARKS), bf16), sds((2, 2, 2, 16, 256), bf16)],
        [SMEM, VMEM, VMEM, VMEM, VMEM],
    )(counts, normed, xbar, wall, dhrb)

    if direct:
        recv, hrecv = call(
            functools.partial(reduce_kernel, n),
            [sds((size, BLK, MARKS), bf16), sds(hal.shape, bf16)],
            [VMEM, VMEM],
            [sem(size), sem(2)],
            cid=1,
        )(blk, hal)
    else:
        recv, hrecv = reduce_plain(n, blk, hal)

    square = pltpu.VMEM((SWEEPS, 2, 256, 256), bf16)
    res, dqz = call(
        functools.partial(chain_kernel, n),
        [sds((BLK, MARKS), bf16), sds((2, 64, MARKS))],
        [VMEM, VMEM, VMEM],
        [square, square, pltpu.VMEM((SWEEPS, 64, 256), f32)],
    )(recv, qlt, klt)

    if direct:
        res = call(functools.partial(spread_kernel, n), sds((4, BLK, MARKS), bf16), [VMEM], [sem(size)], cid=2)(res)
    else:
        res = spread_plain(n, res)

    po, dn, ep, wpart, gtaps = call(
        functools.partial(grads_kernel, n),
        [blocks, blocks, sds((MARKS, 512), bf16), sds((4, 512, 256), bf16), sds((8, 256))],
        [SMEM] + [VMEM] * 18,
        [pltpu.VMEM((256, wide), bf16), pltpu.VMEM((3, 256, wide), bf16), pltpu.VMEM((2, 256, MARKS), bf16),
         pltpu.VMEM((4, rows + 32, rows), f32), pltpu.VMEM((2, 4, 2, rows, rows), bf16), pltpu.VMEM((2, 4, 2, 32, rows), bf16),
         pltpu.VMEM((3, 2, 256, 32), bf16), pltpu.VMEM((2, 256, rows), bf16)],
    )(counts, normed, xbar, wall, wback, dhrb, qt, kt, vt, qlt, klt, dot, a1, e3, blk, res, hrecv, conv_taps, dqz)

    late = (counts, tokens, cotangent, xblk, dh, po, ep, dn, wpart, gtaps, gain, obias, pbias, *kernels)
    if direct:
        halfb = (2, rows, 256)
        out, gx, gwqkv, gwout, sums, gkall, k7o, k5o, k3o = call(
            functools.partial(late_kernel, n),
            [blocks, sds((2, rows, 512)), sds((3, wr, 256)), sds((256, wr)), sds((8, 128)), sds((56, 512)),
             sds((7, 7, 512)), sds((5, 5, 512)), sds((3, 3, 512))],
            [SMEM] + [VMEM] * 15,
            [pltpu.VMEM((MARKS, 256), bf16), pltpu.VMEM((MARKS, 256), bf16), pltpu.VMEM((size, mb, 256), bf16),
             pltpu.VMEM((mb, 256), bf16), pltpu.VMEM((MARKS, 512), bf16), pltpu.VMEM(halfb, bf16), pltpu.VMEM(halfb, bf16),
             pltpu.VMEM((rows, 256), bf16), pltpu.VMEM((2, rows, 512), bf16), pltpu.VMEM(halfb, f32), pltpu.VMEM(halfb, f32),
             pltpu.VMEM(halfb, bf16), pltpu.VMEM((2, 2, 192, 256), bf16), pltpu.VMEM((rows, 512), f32),
             pltpu.VMEM((rows, 512), bf16), pltpu.VMEM((rows, 256), bf16), pltpu.VMEM((size, 2, 4, wr, 256), bf16),
             pltpu.VMEM((4, wr, 256), bf16), pltpu.VMEM((4, wr, 256), bf16)] + scratch
            + [pltpu.VMEM((49, 8, 256), f32), pltpu.VMEM(halfb, bf16), pltpu.VMEM((56, 256), f32),
               pltpu.VMEM((n, 8, 256), f32), pltpu.VMEM((8, 256), f32), pltpu.VMEM((8, 512), f32),
               pltpu.VMEM((n, 8, 128), f32), pltpu.VMEM((8, 128), f32)]
            + [sem(5), sem(size), sem(size), sem(1), sem(2), sem(4), sem(2 * size), sem(1), sem(n), sem(n), sem(n)],
            cid=3,
        )(*late)
    else:
        out, gx, gwqkv, gwout, sums, gkall, k7o, k5o, k3o = late_plain(n, *late, scratch)

    sums = sums.reshape(2, 512)
    gtaps = half_of(gkall[51:55], 1)
    gtaps = jnp.concatenate([gtaps[:, 16::-1], gtaps[:, 255:239:-1]], axis=1)
    return out, gx, sums[0], sums[1], gwqkv, gtaps, gwout, gkall[49], k7o, k5o, k3o, gkall[50]


def solution(mesh):
    rows, cols = P(None, "seq", None), P(None, "seq", "head")
    return jax.shard_map(
        functools.partial(shards, mesh.shape["seq"]),
        mesh=mesh,
        in_specs=(rows, P(), P(), P(), cols, P("head", None), P("head", "seq"), P(), P(), P(), P(), P(), rows),
        out_specs=(rows, rows, P(), P(), cols, P("head", None), P("head", "seq"), P(), P(), P(), P(), P()),
        check_vma=False,
    )
```

time: 252 us -> 174 us (0.69)
  Pallas kernels: 236 us -> 159 us
  other arithmetic: 4.46 us -> 0.65 us
  local copies, waits for them, and re-layouts: 10.1 us -> 12.9 us
    pallas_call x12 -> x7, Pallas kernels: 236 us -> 159 us  [the longest x1 60.1 us: shards(): call(functools.partial(late_kernel, n), [blocks, sds((2, rows, 512)), sds...]
    unnamed x5 -> x18, local copies, waits for them, and re-layouts: 1.88 us -> 9.09 us
    concatenate x4 -> x1, other arithmetic: 3.47 us -> 0.65 us  [shards(): gtaps = jnp.concatenate([gtaps[:, 16::-1], gtaps[:, 255:239:-1]], axis=1)]
    slice x7 -> x4, local copies, waits for them, and re-layouts: 4.86 us -> 2.24 us  [the longest x1 1.38 us: shards(): gkall[50]]
where the time goes in v2:
time: 174 us
  Pallas kernels  159 us (91%)
  local copies, waits for them, and re-layouts  12.9 us (7%)
    pallas_call x1, Pallas kernels, shards(): call(functools.partial(late_kernel, n), [blocks, sds((2, rows, 512)), sds...  60.1 us
    pallas_call x1, Pallas kernels, shards(): call(functools.partial(start_kernel, n), [blocks, blocks, sds((MARKS, 512...  42.5 us
    pallas_call x1, Pallas kernels, shards(): call(functools.partial(chain_kernel, n), [sds((BLK, MARKS), bf16), sds((2...  15.5 us
    pallas_call x1, Pallas kernels, shards(): call(functools.partial(reduce_kernel, n), [sds((size, BLK, MARKS), bf16),...  13.8 us
    pallas_call x1, Pallas kernels, shards(): call(functools.partial(grads_kernel, n), [blocks, blocks, sds((MARKS, 512...  10.9 us
    pallas_call x1, Pallas kernels, shards(): call(functools.partial(spread_kernel, n), sds((4, BLK, MARKS), bf16), [VM...  9.15 us
    unnamed x18, local copies, waits for them, and re-layouts  9.09 us
    pallas_call x1, Pallas kernels, shards(): call(functools.partial(scores_kernel, n), [t2, t2, t2, m2, m2, t2, sds((2...  7.47 us

profile of v2, /device:TPU:0, one launch (start us, length us, event | category | flops | bytes accessed | tf_op | source)
XLA Modules:
  0.0 173.7 jit_solution(11786656299361430893)
XLA Ops:
  0.6 1.5 copy.25.wout
  2.1 42.5 %shard_map.220 = (bf16[2,256,512]{2,1,0:T(8,128)(2,1)}, bf16[2,256,512]{2,1,0:T(8,128)(2,1)}, bf16[256,512]{1,0:T(8,128)(2,1)}, bf16[4,512,256]{2,1,0:T(8,128)(2...) custom-call(s32[2]{0:T(128)} %cnt.7, bf16[2,256,512]{2,1,0:T(8,128)(2,1)} %tok.3, bf16[2,256,512]{2,1,0:T(8,128)(2,1)} %cot.3, ...), custom_call_target="tpu_custom_call" | custom-call | tf_op jit(solution)/shard_map/pallas_call | solution.py:962
  44.6 7.5 %shard_map.221 = (bf16[256,512]{1,0:T(8,128)(2,1)}, bf16[256,512]{1,0:T(8,128)(2,1)}, bf16[256,512]{1,0:T(8,128)(2,1)}, bf16[256,256]{1,0:T(8,128)(2,1)}, bf16[2...) custom-call(s32[2]{0:T(128)} %cnt.7, ...), custom_call_target="tpu_custom_call" | custom-call | tf_op jit(solution)/shard_map/pallas_call | solution.py:978
  52.1 13.8 %shard_map.222 = (bf16[8,144,256]{2,1,0:T(8,128)(2,1)}, bf16[2,2,2,16,256]{4,3,2,1,0:T(8,128)(2,1)}) custom-call(bf16[4,144,256]{2,1,0:T(8,128)(2,1)} %get-tuple-element.62.blk, bf16[2,2,2,16,256]{4,3,2,1,0:T(8,128)(2,1)} %get-tuple-element.63.hal), custom_call_target="tpu_custom_call" | custom-call | tf_op jit(solution)/shard_map/pallas_call | solution.py:986
  65.9 15.5 %shard_map.223 = (bf16[144,256]{1,0:T(8,128)(2,1)}, f32[2,64,256]{2,1,0:T(8,128)}) custom-call(bf16[8,144,256]{2,1,0:T(8,128)(2,1)} %get-tuple-element.64.recv, bf16[256,256]{1,0:T(8,128)(2,1)} %get-tuple-element.57.qlt, bf16[256,256]{1,0:T(8,128)(2,1)} %get-tuple-element.58.klt), custom_call_target="tpu_custom_call" | custom-call | tf_op jit(solution)/shard_map/pallas_call | solution.py:997
  81.4 9.2 %shard_map.224.res = bf16[4,144,256]{2,1,0:T(8,128)(2,1)} custom-call(bf16[144,256]{1,0:T(8,128)(2,1)} %get-tuple-element.65.res), custom_call_target="tpu_custom_call" | custom-call | tf_op jit(solution)/shard_map/pallas_call | solution.py:1005
  90.6 10.9 %shard_map.225 = (bf16[2,256,512]{2,1,0:T(8,128)(2,1)}, bf16[2,256,512]{2,1,0:T(8,128)(2,1)}, bf16[256,512]{1,0:T(8,128)(2,1)}, bf16[4,512,256]{2,1,0:T(8,128)(2,1)}, f32[8,256]{1,0:T(8,128)}) custom-call(s32[2]{0:T(128)} %cnt.7, bf16[2,256,512]{2,1,0:T(8,128)(2,1)} %get-tuple-element.49.normed, bf16[256,512]{1,0:T(8,128)(2,1)} %get-tuple-element.50.xbar, ...), custom_call_target="tpu_custom_call" | custom-call | tf_op jit(solution)/shard_map/pallas_call | solution.py:1009
  101.5 60.1 %shard_map.226 = (bf16[2,256,512]{2,1,0:T(8,128)(2,1)}, f32[2,256,512]{2,1,0:T(8,128)}, f32[3,32,256]{2,1,0:T(8,128)}, f32[256,32]{1,0:T(8,128)}, f32[8,128]{1,0...) custom-call(s32[2]{0:T(128)} %cnt.7, ...), custom_call_target="tpu_custom_call" | custom-call | tf_op jit(solution)/shard_map/pallas_call | solution.py:1021
  161.6 0.0 copy-start
  161.6 1.4 slice_bitcast_fusion
  163.0 0.7 slice.25
  163.7 0.1 constant_dynamic-slice_fusion.1
  163.8 0.1 rev.7
  163.9 0.1 constant_dynamic-slice_fusion
  163.9 0.1 rev.6
  164.0 0.7 pad_maximum_fusion
  164.7 1.6 copy.26
  166.3 1.4 fusion
  167.7 1.9 %copy.33 = bf16[2,256,512]{2,1,0:T(8,128)(2,1)} copy(bf16[2,256,512]{2,1,0:T(8,128)(2,1)} %get-tuple-element.110) | data formatting | bytes 1048576
  169.5 0.0 copy-done
  169.5 0.0 copy-start.2
  169.5 1.0 copy.34
  170.5 0.0 copy-done.2
  170.5 0.0 copy-start.1
  170.5 0.6 copy.35
  171.2 0.3 copy-done.1
  171.4 0.0 copy-start.3
  171.4 0.6 copy.36
  172.1 0.3 copy-done.3
  172.4 0.0 copy-start.4
  172.4 0.6 copy.37
  173.0 0.1 copy-done.4
  173.1 0.6 copy.38
Async XLA Ops:
  161.6 7.9 %copy-start = (f32[2,256,512]{2,1,0:T(8,128)S(1)}, f32[2,256,512]{2,1,0:T(8,128)}, u32[]{:S(2)}) copy-start(f32[2,256,512]{2,1,0:T(8,128)} %get-tuple-element.111) | copy-start | bytes 3145732
  169.5 1.0 copy-start.2
  170.5 0.9 copy-start.1
  171.4 0.9 copy-start.3
  172.4 0.7 copy-start.4

commit v3 on v2

v3 whole, which is shorter than its diff:
```python
import functools

import jax
import jax.numpy as jnp
from jax import lax
from jax.experimental import pallas as pl
from jax.experimental.pallas import tpu as pltpu
from jax.sharding import PartitionSpec as P

MESH = pl.DeviceIdType.MESH
GRID_W = 64
MARKS = 256
SWEEPS = 6
EPSILON = 1e-05
f32, bf16 = jnp.float32, jnp.bfloat16
VMEM = pl.BlockSpec(memory_space=pltpu.VMEM)
SMEM = pl.BlockSpec(memory_space=pltpu.SMEM)
DMA = pltpu.SemaphoreType.DMA
SCALE = 64 ** -0.5
BLK = 144
PART = 80


def sds(shape, dtype=f32):
    return jax.ShapeDtypeStruct(shape, dtype)


def call(kernel, outs, specs, scratch=(), cid=None, vmem=56):
    extra = {} if cid is None else dict(collective_id=cid, has_side_effects=True)
    return pl.pallas_call(
        kernel,
        out_shape=outs,
        in_specs=specs,
        out_specs=jax.tree.map(lambda _: VMEM, outs),
        scratch_shapes=list(scratch),
        compiler_params=pltpu.CompilerParams(vmem_limit_bytes=vmem * 2**20, **extra),
    )


def mm(left, right, cl=1, cr=0):
    return lax.dot_general(left, right, (((cl,), (cr,)), ((), ())), preferred_element_type=f32)


def split(value):
    high = value.astype(bf16)
    return high, (value - high.astype(f32)).astype(bf16)


def split3(row):
    high = row.astype(bf16).astype(f32)
    rest = row - high
    mid = rest.astype(bf16).astype(f32)
    return [high, mid, rest - mid]


def mm3(left, right, cl=1, cr=0):
    (lh, ll), (rh, rl) = left, right
    return mm(lh, rh, cl, cr) + (mm(lh, rl, cl, cr) + mm(ll, rh, cl, cr))


def iota(shape, dim):
    return lax.broadcasted_iota(jnp.int32, shape, dim)


def edges(count, marks):
    return (marks * count + (MARKS - 1)) >> 8, ((marks + 1) * count + (MARKS - 1)) >> 8


def member(count, start, rows):
    low, high = edges(count, iota((MARKS, rows), 0))
    slot = iota((MARKS, rows), 1) + start
    return jnp.where((slot >= low) & (slot < high), 1.0, 0.0).astype(bf16)

OWNERS = (0, 3, 5, 6)


def place(n):
    me = lax.axis_index("seq")
    return me // (n // 2), lax.rem(me, n // 2), lax.rem(me + n // 2, n)


def head_of(g):
    return jnp.where(g == 0, 0, jnp.where(g == 3, 1, jnp.where(g == 5, 2, 3)))


def is_owner(g):
    return (g == 0) | (g == 3) | (g == 5) | (g == 6)


def my_half():
    return pl.ds(pl.multiple_of(lax.axis_index("head") * 256, 256), 256)


def block_start(n, g, b, rows):
    return (g + b * (n // 2)) * rows


def places(n, g, rows, shape, dim):
    at = iota(shape, dim)
    return at + g * rows + jnp.where(at >= rows, (n // 2 - 1) * rows, 0)


def norm_rows(x, gain, bias):
    x = x.astype(f32)
    xc = x - jnp.mean(x, axis=-1, keepdims=True)
    inv = lax.rsqrt(jnp.mean(xc * xc, axis=-1, keepdims=True) + EPSILON)
    return (xc * inv * gain + bias).astype(bf16)


def segment_sums(n, g, count, normed):
    rows = normed.shape[1]
    mine = my_half()
    return sum(mm(member(count, block_start(n, g, b, rows), rows), normed[b, :, mine]) for b in range(2))


def join_taps(kc, k7, k5, k3):
    mine = my_half()
    kc[...] = jnp.zeros_like(kc)
    for a in range(7):
        kc[a, 0:7] = k7[a, :, mine]
    for a in range(5):
        kc[a + 1, 1:6] = kc[a + 1, 1:6] + k5[a, :, mine]
    for a in range(3):
        kc[a + 2, 2:5] = kc[a + 2, 2:5] + k3[a, :, mine]


def load_grid(zs, pad, body, top, bottom):
    grid = body.shape[0] // GRID_W
    pad[...] = jnp.zeros_like(pad)
    pad[0:3, 8:8 + GRID_W] = top.reshape(3, GRID_W, 256)
    pad[3:3 + grid, 8:8 + GRID_W] = body.reshape(grid, GRID_W, 256)
    pad[3 + grid:6 + grid, 8:8 + GRID_W] = bottom.reshape(3, GRID_W, 256)
    for b in range(7):
        zs[b] = pad[:, 5 + b:5 + b + GRID_W, :]


def conv_row(zs, kc, i, flip):
    acc = jnp.zeros((GRID_W, 256), f32)
    for a in range(7):
        for b in range(7):
            ka, kb = (6 - a, 6 - b) if flip else (a, b)
            acc = acc + kc[ka, kb:kb + 1, :] * zs[b, i + a]
    return acc


def ends(n, top, bottom):
    me = lax.axis_index("seq")
    return jnp.where(me > 0, top.astype(f32), 0.0), jnp.where(me < n - 1, bottom.astype(f32), 0.0)


def back_conv(n, count, s, cot, halo, kc, dh, zs, pad):
    me = lax.axis_index("seq")
    rows = cot.shape[1]
    mine = my_half()
    top, bottom = ends(n, halo[0, s], halo[1, s])
    load_grid(zs, pad, cot[s, :, mine].astype(f32), top, bottom)

    @pl.loop(0, rows // GRID_W)
    def _(i):
        acc = conv_row(zs, kc, i, True)
        here = pl.ds(pl.multiple_of(i * GRID_W, GRID_W), GRID_W)
        slot = iota((GRID_W, 256), 0) + (me * rows + i * GRID_W)
        dh[s, here] = cot[s, here, mine].astype(f32) + jnp.where(slot < count, acc, 0.0)


def hidden_rows(count, s, tok, obias, part, hid):
    rows = tok.shape[1]
    mine = my_half()
    hid[s] = tok[s, :, mine].astype(f32) + part.astype(f32) + obias[:, mine]
    slot = iota((rows, 256), 0) + lax.axis_index("seq") * rows
    return jnp.where(slot < count, hid[s], 0.0)


def grid_forward(n, count, s, hid, halo, cot, kc, pbias, outh, zs, pad, gacc):
    rows = hid.shape[1]
    mine = my_half()
    slot = iota((rows, 256), 0) + lax.axis_index("seq") * rows
    top, bottom = ends(n, halo[0, s], halo[1, s])
    load_grid(zs, pad, jnp.where(slot < count, hid[s], 0.0), top, bottom)

    @pl.loop(0, rows // GRID_W)
    def _(i):
        here = pl.ds(pl.multiple_of(i * GRID_W, GRID_W), GRID_W)
        acc = conv_row(zs, kc, i, False)
        outh[s, here] = (hid[s, here] + acc + pbias[:, mine]).astype(bf16)
        g = cot[s, here, mine].astype(f32)
        for a in range(7):
            for b in range(7):
                part = (g * zs[b, i + a]).reshape(GRID_W // 8, 8, 256)
                gacc[a * 7 + b] = gacc[a * 7 + b] + jnp.sum(part, axis=0)


def grid_sums(gacc, dh, cot, gtaps, gk):
    mine = my_half()
    for t in range(49):
        gk[t:t + 1] = jnp.sum(gacc[t], axis=0, keepdims=True)
    gk[49:50] = jnp.sum(dh[0], axis=0, keepdims=True) + jnp.sum(dh[1], axis=0, keepdims=True)
    g = cot[0, :, mine].astype(f32) + cot[1, :, mine].astype(f32)
    gk[50:51] = jnp.sum(g, axis=0, keepdims=True)
    gk[51:55] = gtaps[0:4]
    gk[55:56] = jnp.zeros((1, 256), f32)


def norm_back(n, g, count, b, x, dn, dnr, eall, gain, small):
    rows = x.shape[1]
    low, high = edges(count, iota((MARKS, 512), 0))
    e = (eall[...].astype(f32) / (high - low).astype(f32)).astype(bf16)
    mem = member(count, block_start(n, g, b, rows), rows)
    total = (dn[b].astype(f32) + dnr[b].astype(f32)) + mm(mem, e, 0, 0)
    x = x[b].astype(f32)
    xc = x - jnp.mean(x, axis=-1, keepdims=True)
    inv = lax.rsqrt(jnp.mean(xc * xc, axis=-1, keepdims=True) + EPSILON)
    xh = xc * inv
    dg = total * gain[...]
    m1 = jnp.mean(dg, axis=-1, keepdims=True)
    m2 = jnp.mean(dg * xh, axis=-1, keepdims=True)
    small[0:1] = small[0:1] + jnp.sum(total * xh, axis=0, keepdims=True)
    small[1:2] = small[1:2] + jnp.sum(total, axis=0, keepdims=True)
    return (dg - m1 - xh * m2) * inv


def spill_kernels(gkall, k7o, k5o, k3o):
    for a in range(7):
        k7o[a] = gkall[7 * a:7 * a + 7]
    for a in range(5):
        k5o[a] = gkall[7 * a + 8:7 * a + 13]
    for a in range(3):
        k3o[a] = gkall[7 * a + 16:7 * a + 19]


def greet(peers, pair=True):
    sem = pltpu.get_barrier_semaphore()
    for peer in peers:
        pl.semaphore_signal(sem, inc=1, device_id={"seq": peer}, device_id_type=MESH)
    if pair:
        hd = lax.axis_index("head")
        pl.semaphore_signal(sem, inc=1, device_id={"head": 1 - hd}, device_id_type=MESH)
    pl.semaphore_wait(sem, len(peers) + (1 if pair else 0))


def everyone(n):
    me = lax.axis_index("seq")
    return [lax.rem(me + i, n) for i in range(n)]


def cube(n):
    half, g, _ = place(n)
    return [half * (n // 2) + lax.rem(g + i, n // 2) for i in range(n // 2)]


def remote(src, dst, sems, i, **where):
    return pltpu.make_async_remote_copy(
        src_ref=src, dst_ref=dst, send_sem=sems.at[0, i], recv_sem=sems.at[1, i], device_id=where, device_id_type=MESH
    )


def go(copies):
    for c in copies:
        c.start()
    return copies


def got(copies):
    for c in copies:
        c.wait_recv()


def sent(copies):
    for c in copies:
        c.wait_send()


def project(n, count, normed, wall, qt, kt, vt):
    _, g, _ = place(n)
    rows = normed.shape[1]
    nr = normed[...].reshape(2 * rows, 512)
    qt[...] = mm(wall[0], nr, 0, 1).astype(bf16)
    kt[...] = mm(wall[1], nr, 0, 1).astype(bf16)
    slots = places(n, g, rows, (256, 2 * rows), 1)
    vt[...] = jnp.where(slots < count, mm(wall[2], nr, 0, 1), 0.0).astype(bf16)


def value_edges(n, count, normed, wall, halv):
    _, g, _ = place(n)
    rows = normed.shape[1]
    for b in range(2):
        for side, first in ((0, 0), (1, rows - 16)):
            slot = iota((16, 256), 0) + (block_start(n, g, b, rows) + first)
            v = mm(normed[b, first:first + 16], wall[2])
            halv[side, b] = jnp.where(slot < count, v, 0.0).astype(bf16)


def landmarks(xbar, wall, qlt, klt):
    qlt[...] = mm(wall[0], xbar[...], 0, 1).astype(bf16)
    klt[...] = mm(wall[1], xbar[...], 0, 1).astype(bf16)


def head_rows(h):
    return pl.ds(pl.multiple_of(h * 64, 64), 64)


def key_scores(n, count, kt, qlt, vt, e3, blkb):
    _, g, _ = place(n)
    wide = kt.shape[1]
    ok = places(n, g, wide // 2, (wide, MARKS), 0) < count

    @pl.loop(0, 4)
    def _(h):
        here = head_rows(h)
        s3 = jnp.where(ok, mm(kt[here] * SCALE, qlt[here], 0, 0), -1e30)
        top = jnp.max(s3, axis=0, keepdims=True)
        e = jnp.where(ok, jnp.exp(s3 - top), 0.0)
        total = jnp.sum(e, axis=0, keepdims=True)
        er = e.astype(bf16)
        e3[h] = er
        blkb[h, 0:64] = mm(vt[here], er).astype(bf16)
        stat = jnp.concatenate(split3(top) + split3(total) + [jnp.zeros((10, MARKS), f32)], axis=0)
        blkb[h, 64:80] = stat.astype(bf16)


def query_scores(qt, klt, a1):
    @pl.loop(0, 4)
    def _(h):
        here = head_rows(h)
        s1 = mm(klt[here] * SCALE, qt[here], 0, 0)
        e1 = jnp.exp(s1 - jnp.max(s1, axis=0, keepdims=True))
        a1[h] = (e1 / jnp.sum(e1, axis=0, keepdims=True)).astype(bf16)


def out_grads(dhrb, wback, dot, hald):
    rows = dhrb.shape[1]
    dot[...] = mm(wback[...], dhrb[...].reshape(2 * rows, 512), 1, 1).astype(bf16)
    for b in range(2):
        for side, first in ((0, 0), (1, rows - 16)):
            hald[side, b] = mm(dhrb[b, first:first + 16], wback[...], 1, 1).astype(bf16)


def partial_dc(dot, a1, blkd):
    @pl.loop(0, 4)
    def _(h):
        blkd[h] = mm(dot[head_rows(h)], a1[h], 1, 1).astype(bf16)


def three(stat, first):
    return (stat[first:first + 1] + stat[first + 1:first + 2]) + stat[first + 2:first + 3]


def chain(ql, kl, recvb, recvd, res, dqz, ps, ts, xs, got_b=None, got_d=None):
    parts = recvb.shape[0]
    s2 = mm(ql * SCALE, kl, 0, 0)
    e2 = jnp.exp(s2 - jnp.max(s2, axis=1, keepdims=True))
    a = e2 / jnp.sum(e2, axis=1, keepdims=True)
    asp = split(a)
    cs, rs = jnp.sum(a, axis=0, keepdims=True), jnp.sum(a, axis=1, keepdims=True)
    cm, rm = jnp.max(cs, axis=1, keepdims=True), jnp.max(rs, axis=0, keepdims=True)
    inv = 1.0 / (cm * rm)
    p = mm3(asp, asp, 1, 1) * inv
    for k in range(SWEEPS):
        psp = split(p)
        t = mm3(psp, psp)
        tsp = split(t)
        ps[k, 0], ps[k, 1] = psp
        ts[k, 0], ts[k, 1] = tsp
        if k < SWEEPS - 1:
            p = 0.25 * (13.0 * p - 15.0 * t + mm3(tsp, split(7.0 * p - t)))
    if got_b:
        got_b()
    tops = [three(recvb[d, 64:80].astype(f32), 0) for d in range(parts)]
    top = functools.reduce(jnp.maximum, tops)
    total, value = 0.0, 0.0
    for d in range(parts):
        w = jnp.exp(tops[d] - top)
        total = total + three(recvb[d, 64:80].astype(f32), 3) * w
        value = value + recvb[d, 0:64].astype(f32) * w
    value = value / total
    x = value
    for k in range(SWEEPS):
        psp, tsp = (ps[k, 0], ps[k, 1]), (ts[k, 0], ts[k, 1])
        xs[k] = x
        xt = mm3(split(x), tsp)
        x = 0.25 * (13.0 * x + 7.0 * xt - mm3(split(15.0 * x + xt), psp))
    ct = mm3(split(x), asp) * inv
    res[0:64] = ct.astype(bf16)
    if got_d:
        got_d()
    dct = recvd[0].astype(f32)
    for d in range(1, parts):
        dct = dct + recvd[d].astype(f32)
    dcs = split(dct)
    y = mm3(dcs, asp, 1, 1) * inv
    da = mm3(split(x), dcs, 0, 0) * inv
    ds = -jnp.sum(jnp.sum(dct * ct, axis=0, keepdims=True), axis=1, keepdims=True) * inv
    e = None
    for k in range(SWEEPS - 1, -1, -1):
        psp, tsp = (ps[k, 0], ps[k, 1]), (ts[k, 0], ts[k, 1])
        outer = mm3(split(y), split(xs[k]), 0, 0) * 0.125
        d = outer + outer.T
        pd = mm3(psp, split(d))
        if e is None:
            new = -15.0 * d + mm3(split(-pd), psp)
            left = 7.0 * pd + mm3(tsp, split(-d))
        else:
            eq = 0.25 * e
            pe = mm3(psp, split(eq))
            new = 13.0 * eq - 15.0 * d + mm3(split(7.0 * pe - pd), psp)
            left = 7.0 * pd - 15.0 * pe + mm3(tsp, split(7.0 * eq - d - (pe + pe.T)))
        e = new + (left + left.T)
        yt = mm3(split(y), tsp)
        y = 0.25 * (13.0 * y + 7.0 * yt - mm3(split(15.0 * y + yt), psp))
    dbr = y.astype(bf16)
    res[64:128] = dbr
    rt = jnp.sum(dbr.astype(f32) * value, axis=0, keepdims=True)
    stat = jnp.concatenate(split3(top) + split3(total) + split3(rt) + [jnp.zeros((7, MARKS), f32)], axis=0)
    res[128:144] = stat.astype(bf16)

    def rest():
        p0 = ps[0, 0].astype(f32) + ps[0, 1].astype(f32)
        grad = da + mm3(split(e), asp) * (2.0 * inv)
        slope = ds - jnp.sum(jnp.sum(e * p0, axis=0, keepdims=True), axis=1, keepdims=True) * inv
        eqc, eqr = jnp.where(cs == cm, 1.0, 0.0), jnp.where(rs == rm, 1.0, 0.0)
        grad = grad + (slope * rm) * (eqc / jnp.sum(eqc, axis=1, keepdims=True))
        grad = grad + (slope * cm) * (eqr / jnp.sum(eqr, axis=0, keepdims=True))
        dsc = a * (grad - jnp.sum(a * grad, axis=1, keepdims=True)) * SCALE
        dh, dl = split(dsc)
        dqz[0] = mm(kl, dh, 1, 1) + mm(kl, dl, 1, 1)
        dqz[1] = mm(ql, dh) + mm(ql, dl)

    return rest


def band(base, shift, rows):
    wide = jnp.broadcast_to(base, (rows, 256))
    return pltpu.roll(wide, shift, 1, stride=1, stride_axis=0)


def diagonals(g, shift):
    return jnp.sum(pltpu.roll(g, shift, 1, stride=1, stride_axis=0), axis=0, keepdims=True)


def ring_ends(n, g, b, recv):
    top = jnp.where(g > 0, recv[0, b].astype(f32), recv[0, 0].astype(f32) if b else 0.0)
    bottom = jnp.where(g < n // 2 - 1, recv[1, b].astype(f32), 0.0 if b else recv[1, 1].astype(f32))
    return jnp.concatenate([top, bottom], axis=0)


def make_bands(taps, rows, tm, th):
    pi, pj = iota((rows, rows), 0), iota((rows, rows), 1)
    inside = (pi - pj <= 16) & (pj - pi <= 16)
    hi, hj = iota((32, rows), 0), iota((32, rows), 1)
    far = jnp.where(hi < 16, hi - hj, hj - hi - (rows - 32)) >= 0
    ti, tl = iota((33, 256), 0), iota((33, 256), 1)
    spots = [jnp.where(((ti + tl if f == 0 else tl - ti + 32) & 255) == 16, 1.0, 0.0).astype(bf16) for f in range(2)]
    pieces = [piece.astype(bf16) for piece in split3(taps[...])]
    for f in range(2):
        lines = mm(pieces[0], spots[f]) + mm(pieces[1], spots[f]) + mm(pieces[2], spots[f])
        for h in range(4):
            line = lines[h:h + 1, :]
            full = jnp.where(inside, band(line, 0, rows), 0.0)
            tm[f, h, 0], tm[f, h, 1] = split(full)
            both = jnp.concatenate([band(line, 240, 16), band(line, 0, 16)], axis=0)
            th[f, h, 0], th[f, h, 1] = split(jnp.where(far, both, 0.0))


def value_conv(n, vt, recvv, tm, th, hv, vr, hvr, conv):
    _, g, _ = place(n)
    rows = vt.shape[1] // 2
    pi, pj = iota((rows, rows), 0), iota((rows, rows), 1)
    mirror = jnp.where(pi + pj == rows - 1, 1.0, 0.0).astype(bf16)
    si, sj = iota((32, 32), 0), iota((32, 32), 1)
    mirror32 = jnp.where(si + sj == jnp.where(si < 16, 15, 47), 1.0, 0.0).astype(bf16)
    for b in range(2):
        part = slice(b * rows, (b + 1) * rows)
        hv[b] = ring_ends(n, g, b, recvv).T.astype(bf16)
        vr[b] = mm(vt[:, part], mirror).astype(bf16)
        hvr[b] = mm(hv[b], mirror32).astype(bf16)

        @pl.loop(0, 4)
        def _(h):
            here = head_rows(h)
            v, vh = vt[here, part], hv[b, here]
            conv[here, part] = mm(v, tm[0, h, 0]) + mm(v, tm[0, h, 1]) + mm(vh, th[0, h, 0]) + mm(vh, th[0, h, 1])


def value_conv_back(n, dot, recvd, tm, th, hd, vr, hvr, dconv, gsum, gtaps):
    _, g, _ = place(n)
    rows = dot.shape[1] // 2
    pi, pj = iota((rows, rows), 0), iota((rows, rows), 1)
    hi, hj = iota((32, rows), 0), iota((32, rows), 1)
    near = (pi + pj >= rows - 17) & (pi + pj <= rows + 15)
    beyond = jnp.where(hi < 16, 15 - hi - hj, hi + hj - (rows + 15)) >= 0
    for b in range(2):
        hd[b] = ring_ends(n, g, b, recvd).T.astype(bf16)

    @pl.loop(0, 4)
    def _(h):
        here = head_rows(h)
        s, sh = 0.0, 0.0
        for b in range(2):
            part = slice(b * rows, (b + 1) * rows)
            d, dh = dot[here, part], hd[b, here]
            dconv[here, part] = mm(d, tm[1, h, 0]) + mm(d, tm[1, h, 1]) + mm(dh, th[1, h, 0]) + mm(dh, th[1, h, 1])
            s = s + mm(vr[b, here], d, 0, 0)
            sh = sh + mm(hvr[b, here], d, 0, 0)
        s, sh = jnp.where(near, s, 0.0), jnp.where(beyond, sh, 0.0)
        gsum[h] = jnp.broadcast_to(diagonals(s, 1) + diagonals(sh[0:16], 1) + diagonals(sh[16:32], 241), (8, 256))

    for h in range(4):
        gtaps[h:h + 1, :] = gsum[h, 0:1]
    gtaps[4:8, :] = jnp.zeros((4, 256), f32)


def attend(res, a1, conv, att):
    @pl.loop(0, 4)
    def _(h):
        here = head_rows(h)
        att[here] = (mm(res[h, 0:64], a1[h]) + conv[here]).astype(bf16)


def score_grads(n, count, qt, kt, vt, qlt, klt, dot, a1, e3, blkb, res, dqz, dconv, dp, dlm):
    _, g, _ = place(n)
    wide = qt.shape[1]
    mine = head_of(g)
    use = jnp.where(is_owner(g), 1.0, 0.0)
    slots = places(n, g, wide // 2, (64, wide), 1)

    @pl.loop(0, 4)
    def _(h):
        here = head_rows(h)
        ct, dbt = res[h, 0:64], res[h, 64:128]
        stat = res[h, 128:144].astype(f32)
        own = three(blkb[h, 64:80].astype(f32), 0)
        factor = jnp.exp(own - three(stat, 0)) / three(stat, 3)
        rt = three(stat, 6)
        do, v = dot[here], vt[here]
        a = a1[h].astype(f32)
        da = mm(ct, do, 0, 0)
        d1 = (a * (da - jnp.sum(a * da, axis=0, keepdims=True))).astype(bf16)
        dp[0, here] = mm(klt[here] * SCALE, d1).astype(bf16)
        own_chain = jnp.where(h == mine, use, 0.0)
        dlm[1, here] = (mm(qt[here] * SCALE, d1, 1, 1) + own_chain * dqz[1]).astype(bf16)
        a3 = e3[h].astype(f32) * factor
        d3 = (a3 * (mm(v, dbt, 0, 0) - rt)).astype(bf16)
        dlm[0, here] = (mm(kt[here] * SCALE, d3) + own_chain * dqz[0]).astype(bf16)
        dp[1, here] = mm(qlt[here] * SCALE, d3, 1, 1).astype(bf16)
        dv = mm(dbt, a3.astype(bf16), 1, 1) + dconv[here]
        dp[2, here] = jnp.where(slots < count, dv, 0.0).astype(bf16)


def mark_rows(wall, dlm, ep):
    ep[...] = (mm(wall[0], dlm[0]) + mm(wall[1], dlm[1])).T.astype(bf16)


def input_rows(wall, dp, dn):
    rows = dn.shape[1]
    d = mm(wall[0], dp[0]) + mm(wall[1], dp[1]) + mm(wall[2], dp[2])
    dn[...] = d.T.astype(bf16).reshape(2, rows, 512)


def output_rows(att, wback, po):
    rows = po.shape[1]
    po[...] = mm(att[...], wback[...], 0, 0).astype(bf16).reshape(2, rows, 512)


def weight_grads(normed, xbar, dhrb, att, dp, dlm, wpart):
    rows = normed.shape[1]
    nr = normed[...].reshape(2 * rows, 512)
    for j in range(3):
        grad = mm(dp[j], nr)
        if j < 2:
            grad = grad + mm(dlm[j], xbar[...])
        wpart[j] = grad.T.astype(bf16)
    wpart[3] = mm(att[...], dhrb[...].reshape(2 * rows, 512)).T.astype(bf16)


class Refs:
    def __init__(self, names, refs):
        self.__dict__.update(zip(names, refs))


INPUTS = ("cnt", "tok", "cot", "gain", "bias", "wqkv", "woutt", "taps", "obias", "pbias", "k7", "k5", "k3")


def layer_results(n, rows, wr):
    return dict(
        outf=((2, rows, 512), bf16), lnf=((2, rows, 512), f32), dhf=((2, rows, 512), f32), gw=((4, wr, 256), f32),
        sums=((8, 128), f32), gkall=((56, 512), f32),
    )


def layer_buffers(n, rows, wr):
    size = n // 2
    mb, wide, grid = MARKS // size, 2 * rows, rows // GRID_W
    half2 = (2, rows, 256)
    return dict(
        wts=((4, wr, 256), bf16), wall=((4, 512, 256), bf16), wback=((256, 512), bf16),
        xblk=((2, rows, 512), bf16), normed=((2, rows, 512), bf16), xbar=((MARKS, 512), bf16),
        xp=((MARKS, 256), bf16), xr=((size, mb, 256), bf16), xm=((mb, 256), bf16),
        halo=((2, 2, 192, 256), bf16), dh=(half2, f32), dhs=((rows, 256), bf16), dhrb=((2, rows, 512), bf16),
        kc=((7, 8, 256), f32), zs=((7, grid + 6, GRID_W, 256), f32), pad=((grid + 6, GRID_W + 16, 256), f32),
        qt=((256, wide), bf16), kt=((256, wide), bf16), vt=((256, wide), bf16), dot=((256, wide), bf16),
        qlt=((256, MARKS), bf16), klt=((256, MARKS), bf16), a1=((4, MARKS, wide), bf16), e3=((4, wide, MARKS), bf16),
        blkb=((4, PART, MARKS), bf16), blkd=((4, 64, MARKS), bf16),
        recvb=((size, PART, MARKS), bf16), recvd=((size, 64, MARKS), bf16),
        halv=((2, 2, 16, 256), bf16), hald=((2, 2, 16, 256), bf16), rhv=((2, 2, 16, 256), bf16), rhd=((2, 2, 16, 256), bf16),
        ps=((SWEEPS, 2, 256, 256), bf16), ts=((SWEEPS, 2, 256, 256), bf16), xs=((SWEEPS, 64, 256), f32),
        res=((BLK, MARKS), bf16), resall=((4, BLK, MARKS), bf16), dqz=((2, 64, MARKS), f32),
        tm=((2, 4, 2, rows, rows), bf16), th=((2, 4, 2, 32, rows), bf16), hv=((2, 256, 32), bf16), hdt=((2, 256, 32), bf16),
        hvr=((2, 256, 32), bf16), vr=((2, 256, rows), bf16), conv=((256, wide), f32), dconv=((256, wide), f32),
        gsum=((4, 8, 256), f32), gtaps=((8, 256), f32), att=((256, wide), bf16), dp=((3, 256, wide), bf16),
        dlm=((2, 256, MARKS), bf16), po=((2, rows, 512), bf16), dn=((2, rows, 512), bf16), ep=((MARKS, 512), bf16),
        wpart=((4, 512, 256), bf16), er=((MARKS, 256), bf16), es=((MARKS, 256), bf16), erv=((size, mb, 256), bf16),
        em=((mb, 256), bf16), eall=((MARKS, 512), bf16), por=(half2, bf16), pos=(half2, bf16), psr=((rows, 256), bf16),
        dnr=((2, rows, 512), bf16), hid=(half2, f32), z=(half2, bf16), zhalo=((2, 2, 192, 256), bf16),
        lnr=((rows, 512), bf16), lns=((rows, 256), bf16), wrv=((size, 2, 4, wr, 256), bf16), wsum=((4, wr, 256), bf16),
        wone=((4, wr, 256), bf16), gacc=((49, 8, 256), f32), outh=(half2, bf16), gk=((56, 256), f32),
        gkr=((n, 8, 256), f32), gkm=((8, 256), f32), small=((8, 512), f32), smr=((n, 8, 128), f32), smx=((8, 128), f32),
    )


SEMS = ("s_w", "s_v", "s_t", "s_h", "s_x", "s_g", "s_p", "s_d", "s_b", "s_c", "s_r", "s_q", "s_a", "s_e", "s_f", "s_o",
        "s_z", "s_l", "s_y", "s_u", "s_k", "s_m", "s_s")


def layer_kernel(n, names, *refs):
    r = Refs(names, refs)
    half, g, partner = place(n)
    me = lax.axis_index("seq")
    hd = lax.axis_index("head")
    other = 1 - half
    size = n // 2
    rows = r.tok.shape[1]
    mb, wr = MARKS // size, r.wts.shape[1]
    mine = my_half()
    theirs = pl.ds(pl.multiple_of((1 - hd) * 256, 256), 256)
    count = r.cnt[half]
    near, far = cube(n), everyone(n)
    core = 1 - hd

    def wrow(device):
        return pl.ds(pl.multiple_of(device * wr, wr), wr)

    def marks(i):
        return pl.ds(pl.multiple_of(lax.rem(g + i, size) * mb, mb), mb)

    r.wts[0:3] = r.wqkv[...]
    r.wts[3] = r.woutt[...]
    greet(far[1:])
    c_t = go([remote(r.tok.at[other, :, mine], r.xblk.at[half, :, mine], r.s_t, 0, seq=partner)])
    c_w = go([remote(r.wts, r.wall.at[:, wrow(me)], r.s_w, 0, seq=partner)])
    c_v = go([remote(r.wts, r.wall.at[:, wrow(me)], r.s_v, i, seq=near[i]) for i in range(1, size)])
    c_h = go([
        remote(r.cot.at[:, pl.ds(rows - 192, 192), mine], r.halo.at[0], r.s_h, 0, seq=far[1]),
        remote(r.cot.at[:, pl.ds(0, 192), mine], r.halo.at[1], r.s_h, 1, seq=far[n - 1]),
    ])
    r.wall[:, wrow(me)] = r.wts[...]
    r.xblk[half] = r.tok[half]
    r.normed[half] = norm_rows(r.tok[half], r.gain[...], r.bias[...])
    join_taps(r.kc, r.k7, r.k5, r.k3)
    make_bands(r.taps, rows, r.tm, r.th)

    got(c_t)
    c_p = go([remote(r.xblk.at[other, :, mine], r.xblk.at[other, :, mine], r.s_p, 0, head=core)])
    got(c_p)
    r.normed[other] = norm_rows(r.xblk[other], r.gain[...], r.bias[...])
    r.xp[...] = segment_sums(n, g, count, r.normed).astype(bf16)
    c_x = go([remote(r.xp.at[marks(i)], r.xr.at[g], r.s_x, i, seq=near[i]) for i in range(1, size)])
    row = marks(0)
    r.xr[pl.ds(g, 1)] = r.xp[row][None]
    got(c_w)
    c_v += go([
        remote(r.wall.at[:, wrow(partner)], r.wall.at[:, wrow(partner)], r.s_v, size + i, seq=near[i]) for i in range(1, size)
    ])
    got(c_h)
    back_conv(n, r.cnt[other], other, r.cot, r.halo, r.kc, r.dh, r.zs, r.pad)
    r.dhs[...] = r.dh[other].astype(bf16)
    c_d = go([remote(r.dhs, r.dhrb.at[half, :, mine], r.s_d, 0, seq=partner)])
    got(c_x)
    total = r.xr[0].astype(f32)
    for d in range(1, size):
        total = total + r.xr[d].astype(f32)
    low, high = edges(count, iota((mb, 256), 0) + g * mb)
    r.xm[...] = (total / (high - low).astype(f32)).astype(bf16)
    r.xbar[row, mine] = r.xm[...]
    c_g = go([remote(r.xm, r.xbar.at[row, mine], r.s_g, i, seq=near[i]) for i in range(1, size)])
    back_conv(n, count, half, r.cot, r.halo, r.kc, r.dh, r.zs, r.pad)
    r.dhrb[half, :, mine] = r.dh[half].astype(bf16)
    c_p += go([remote(r.dh, r.dhf.at[:, :, mine], r.s_p, 1, head=core)])
    r.dhf[:, :, mine] = r.dh[...]
    got(c_g)
    c_p += go([remote(r.xbar.at[:, mine], r.xbar.at[:, mine], r.s_p, 2, head=core)])
    got(c_v)

    project(n, count, r.normed, r.wall, r.qt, r.kt, r.vt)
    value_edges(n, count, r.normed, r.wall, r.halv)
    c_q = go([
        remote(r.halv.at[1], r.rhv.at[0], r.s_q, 0, seq=near[1]),
        remote(r.halv.at[0], r.rhv.at[1], r.s_q, 1, seq=near[size - 1]),
    ])
    got(c_p[2:3])
    landmarks(r.xbar, r.wall, r.qlt, r.klt)
    key_scores(n, count, r.kt, r.qlt, r.vt, r.e3, r.blkb)

    def to_owner(blk, recv, sems, h, d):
        return pltpu.make_async_remote_copy(
            src_ref=blk.at[h], dst_ref=recv.at[d], send_sem=sems.at[0, h], recv_sem=sems.at[1, d],
            device_id={"seq": half * size + OWNERS[h]}, device_id_type=MESH,
        )

    def give(blk, recv, sems):
        for h, o in enumerate(OWNERS):

            @pl.when(g != o)
            def _():
                to_owner(blk, recv, sems, h, g).start()

            @pl.when(g == o)
            def _():
                recv[pl.ds(g, 1)] = blk[h:h + 1]

    def given(blk, recv, sems, h):
        for d in range(size):
            if d != OWNERS[h]:
                to_owner(blk, recv, sems, h, d).wait_recv()

    give(r.blkb, r.recvb, r.s_b)
    query_scores(r.qt, r.klt, r.a1)
    r.wback[...] = r.wall[3].astype(f32).T.astype(bf16)
    got(c_d)
    c_p += go([remote(r.dhrb.at[:, :, mine], r.dhrb.at[:, :, mine], r.s_p, 3, head=core)])
    got(c_p[3:4])
    out_grads(r.dhrb, r.wback, r.dot, r.hald)
    c_q += go([
        remote(r.hald.at[1], r.rhd.at[0], r.s_q, 2, seq=near[1]),
        remote(r.hald.at[0], r.rhd.at[1], r.s_q, 3, seq=near[size - 1]),
    ])
    partial_dc(r.dot, r.a1, r.blkd)
    give(r.blkd, r.recvd, r.s_c)

    r.dqz[...] = jnp.zeros_like(r.dqz)

    def spread(h, i):
        return pltpu.make_async_remote_copy(
            src_ref=r.res, dst_ref=r.resall.at[h], send_sem=r.s_r.at[0, i], recv_sem=r.s_r.at[1, h],
            device_id={"seq": near[i]}, device_id_type=MESH,
        )

    @pl.when(is_owner(g))
    def _():
        here = head_rows(head_of(g))

        def wait_for(blk, recv, sems):
            def wait():
                for d in range(size):

                    @pl.when(g != d)
                    def _():
                        to_owner(blk, recv, sems, 0, d).wait_recv()

            return wait

        rest = chain(
            r.qlt[here], r.klt[here], r.recvb, r.recvd, r.res, r.dqz, r.ps, r.ts, r.xs,
            wait_for(r.blkb, r.recvb, r.s_b), wait_for(r.blkd, r.recvd, r.s_c),
        )
        for h, o in enumerate(OWNERS):

            @pl.when(g == o)
            def _():
                for i in range(1, size):
                    spread(h, i).start()
                r.resall[h] = r.res[...]

        rest()

    got(c_q)
    value_conv(n, r.vt, r.rhv, r.tm, r.th, r.hv, r.vr, r.hvr, r.conv)
    value_conv_back(n, r.dot, r.rhd, r.tm, r.th, r.hdt, r.vr, r.hvr, r.dconv, r.gsum, r.gtaps)
    r.small[...] = jnp.zeros_like(r.small)
    r.gacc[...] = jnp.zeros_like(r.gacc)
    for h, o in enumerate(OWNERS):

        @pl.when(g != o)
        def _():
            spread(h, 1).wait_recv()

    attend(r.resall, r.a1, r.conv, r.att)
    output_rows(r.att, r.wback, r.po)
    c_a = go([remote(r.po.at[:, :, theirs], r.por, r.s_a, 0, head=core)])
    score_grads(n, count, r.qt, r.kt, r.vt, r.qlt, r.klt, r.dot, r.a1, r.e3, r.blkb, r.resall, r.dqz, r.dconv, r.dp, r.dlm)
    got(c_a)
    r.pos[...] = (r.po[:, :, mine].astype(f32) + r.por[...].astype(f32)).astype(bf16)
    c_o = go([remote(r.pos.at[other], r.psr, r.s_o, 0, seq=partner)])
    mark_rows(r.wall, r.dlm, r.ep)
    c_a += go([remote(r.ep.at[:, theirs], r.er, r.s_a, 1, head=core)])
    input_rows(r.wall, r.dp, r.dn)
    c_a += go([remote(r.dn, r.dnr, r.s_a, 2, head=core)])
    got(c_a[1:2])
    r.es[...] = (r.ep[:, mine].astype(f32) + r.er[...].astype(f32)).astype(bf16)
    c_e = go([remote(r.es.at[marks(i)], r.erv.at[g], r.s_e, i, seq=near[i]) for i in range(1, size)])
    r.erv[pl.ds(g, 1)] = r.es[row][None]
    r.z[half] = hidden_rows(count, half, r.tok, r.obias, r.pos[half], r.hid).astype(bf16)
    got(c_o)
    r.z[other] = hidden_rows(r.cnt[other], other, r.tok, r.obias, r.psr[...], r.hid).astype(bf16)
    got(c_e)
    total = r.erv[0].astype(f32)
    for d in range(1, size):
        total = total + r.erv[d].astype(f32)
    r.em[...] = total.astype(bf16)
    r.eall[row, mine] = r.em[...]
    c_f = go([remote(r.em, r.eall.at[row, mine], r.s_f, i, seq=near[i]) for i in range(1, size)])
    c_z = go([
        remote(r.z.at[:, pl.ds(rows - 192, 192)], r.zhalo.at[0], r.s_z, 0, seq=far[1]),
        remote(r.z.at[:, pl.ds(0, 192)], r.zhalo.at[1], r.s_z, 1, seq=far[n - 1]),
    ])
    weight_grads(r.normed, r.xbar, r.dhrb, r.att, r.dp, r.dlm, r.wpart)
    c_y = []
    for i in range(1, size):
        for k, device in enumerate((near[i], lax.rem(near[i] + size, n))):
            c_y += go([remote(r.wpart.at[:, wrow(device)], r.wrv.at[g, k], r.s_y, 2 * i + k, seq=near[i])])
    r.wrv[pl.ds(g, 1), 0] = r.wpart[:, wrow(me)][None]
    r.wrv[pl.ds(g, 1), 1] = r.wpart[:, wrow(partner)][None]

    got(c_f)
    c_a += go([remote(r.eall.at[:, mine], r.eall.at[:, mine], r.s_a, 3, head=core)])
    got(c_a[2:4])
    r.lnf[other] = norm_back(n, g, count, other, r.xblk, r.dn, r.dnr, r.eall, r.gain, r.small)
    r.lns[...] = r.lnf[other, :, mine].astype(bf16)
    c_l = go([remote(r.lns, r.lnr.at[:, mine], r.s_l, 0, seq=partner)])
    r.lnf[half] = norm_back(n, g, count, half, r.xblk, r.dn, r.dnr, r.eall, r.gain, r.small)
    for a in range(2):
        for b in range(4):
            r.smx[4 * a + b:4 * a + b + 1] = r.small[a:a + 1, 128 * b:128 * b + 128]
    c_s = go([remote(r.smx, r.smr.at[me], r.s_s, i, seq=far[i]) for i in range(1, n)])
    r.smr[pl.ds(me, 1)] = r.smx[...][None]

    got(c_z)
    for s in range(2):
        grid_forward(n, r.cnt[s], s, r.hid, r.zhalo, r.cot, r.kc, r.pbias, r.outh, r.zs, r.pad, r.gacc)
    c_l += go([remote(r.outh, r.outf.at[:, :, mine], r.s_l, 1, head=core)])
    r.outf[:, :, mine] = r.outh[...]
    grid_sums(r.gacc, r.dh, r.cot, r.gtaps, r.gk)
    blocks = r.gk.shape[0] // 8

    def to(b, d):
        return pltpu.make_async_remote_copy(
            src_ref=r.gk.at[pl.ds(8 * b, 8)], dst_ref=r.gkr.at[d], send_sem=r.s_k.at[0, b], recv_sem=r.s_k.at[1, d],
            device_id={"seq": b}, device_id_type=MESH,
        )

    def back(b, i):
        return pltpu.make_async_remote_copy(
            src_ref=r.gkm, dst_ref=r.gkall.at[pl.ds(8 * b, 8), mine], send_sem=r.s_m.at[0, i], recv_sem=r.s_m.at[1, b],
            device_id={"seq": far[i]}, device_id_type=MESH,
        )

    for b in range(blocks):

        @pl.when(me != b)
        def _():
            to(b, me).start()

    got(c_l[0:1])
    c_l += go([remote(r.lnr.at[:, mine], r.lnr.at[:, mine], r.s_l, 2, head=core)])
    got(c_y)
    c_u = []
    for k in (1, 0):
        total = r.wrv[0, k].astype(f32)
        for d in range(1, size):
            total = total + r.wrv[d, k].astype(f32)
        if k == 1:
            r.wsum[...] = total.astype(bf16)
            c_u = go([remote(r.wsum, r.wone, r.s_u, 0, seq=partner)])
    for b in range(blocks):

        @pl.when(me == b)
        def _():
            r.gkr[pl.ds(me, 1)] = r.gk[pl.ds(8 * b, 8)][None]
            for d in range(n):
                if d != b:
                    to(b, d).wait_recv()
            gsum = r.gkr[0]
            for d in range(1, n):
                gsum = gsum + r.gkr[d]
            r.gkm[...] = gsum
            r.gkall[pl.ds(8 * b, 8), mine] = gsum
            for i in range(1, n):
                back(b, i).start()

    got(c_l[2:3])
    r.lnf[other] = r.lnr[...].astype(f32)
    got(c_s)
    acc = r.smr[0]
    for d in range(1, n):
        acc = acc + r.smr[d]
    r.sums[...] = acc
    for b in range(blocks):

        @pl.when(me != b)
        def _():
            back(b, 0).wait_recv()

    c_k = go([remote(r.gkall.at[:, mine], r.gkall.at[:, mine], r.s_l, 3, head=core)])
    got(c_u)
    r.gw[...] = total + r.wone[...].astype(f32)
    got(c_k + c_l[1:2] + c_p[1:2])

    sent(c_t + c_w + c_v + c_h + c_p + c_x + c_d + c_g + c_q + c_a + c_o + c_e + c_f + c_z + c_y + c_l + c_s + c_u + c_k)
    for h, o in enumerate(OWNERS):

        @pl.when(g != o)
        def _():
            to_owner(r.blkb, r.recvb, r.s_b, h, g).wait_send()
            to_owner(r.blkd, r.recvd, r.s_c, h, g).wait_send()

        @pl.when(g == o)
        def _():
            for i in range(1, size):
                spread(h, i).wait_send()

    for b in range(blocks):

        @pl.when(me != b)
        def _():
            to(b, me).wait_send()

        @pl.when(me == b)
        def _():
            for i in range(1, n):
                back(b, i).wait_send()


def result_kernel(outf, lnf, dhf, gw, sums, gkall, out, gx, gwqkv, gwoutt, ggain, gbias, gtaps, gob, k7o, k5o, k3o, gpb):
    out[...] = outf[...]
    gx[...] = dhf[...] + lnf[...]
    gwqkv[...] = gw[0:3]
    gwoutt[...] = gw[3]
    for i in range(4):
        ggain[:, 128 * i:128 * i + 128] = sums[i:i + 1]
        gbias[:, 128 * i:128 * i + 128] = sums[4 + i:5 + i]
    rows = gkall[51:55, my_half()]
    li, lt = iota((256, 33), 0), iota((256, 33), 1)
    spot = jnp.where(((li + lt) & 255) == 16, 1.0, 0.0).astype(bf16)
    parts = [mm(piece.astype(bf16), spot) for piece in split3(rows)]
    gtaps[...] = parts[0] + parts[1] + parts[2]
    gob[...] = gkall[49:50]
    gpb[...] = gkall[50:51]
    spill_kernels(gkall, k7o, k5o, k3o)


def ring(rows_up, rows_down):
    count = lax.axis_size("seq")
    up = lax.ppermute(rows_up, "seq", [(i, (i + 1) % count) for i in range(count)])
    down = lax.ppermute(rows_down, "seq", [((i + 1) % count, i) for i in range(count)])
    return jnp.stack([up, down])


def half_of(full, axis):
    return lax.dynamic_slice_in_dim(full, lax.axis_index("head") * 256, 256, axis)


def swap(n, blocks):
    half, _, _ = place(n)
    theirs = lax.ppermute(jnp.where(half == 0, blocks[1], blocks[0]), "seq", [(i, (i + n // 2) % n) for i in range(n)])
    own = jnp.where(half == 0, blocks[0], blocks[1])
    return jnp.where(half == 0, jnp.stack([own, theirs]), jnp.stack([theirs, own]))


def half_sum(n, value):
    half, _, _ = place(n)
    pair = lax.psum(jnp.stack([jnp.where(half == s, value, 0.0) for s in range(2)]), "seq")
    return jnp.where(half == 0, pair[0], pair[1])


def half_max(n, value):
    half, _, _ = place(n)
    pair = lax.pmax(jnp.stack([jnp.where(half == s, value, -jnp.inf) for s in range(2)]), "seq")
    return jnp.where(half == 0, pair[0], pair[1])


def norm_kernel(n, cnt, xblk, gain, bias, normed, xp):
    half, g, _ = place(n)
    for b in range(2):
        normed[b] = norm_rows(xblk[b], gain[...], bias[...])
    xp[...] = segment_sums(n, g, cnt[half], normed)


def back_conv_kernel(n, cnt, cot, halo, k7, k5, k3, dh, kc, zs, pad):
    join_taps(kc, k7, k5, k3)
    for s in range(2):
        back_conv(n, cnt[s], s, cot, halo, kc, dh, zs, pad)


def start_plain(n, counts, tok, cot, gain, bias, wqkv, woutt, k7, k5, k3, scratch):
    half, _, _ = place(n)
    rows = tok.shape[1]
    count = counts[half]
    xblk = swap(n, tok)
    normed, xp = call(
        functools.partial(norm_kernel, n), [sds((2, rows, 512), bf16), sds((MARKS, 256))], [SMEM] + [VMEM] * 3
    )(counts, xblk, gain, bias)
    low, high = edges(count, jnp.arange(MARKS, dtype=jnp.int32))
    xbar = (half_sum(n, xp) / (high - low).astype(f32)[:, None]).astype(bf16)
    xbar = lax.all_gather(xbar, "head", axis=1, tiled=True)
    wts = jnp.concatenate([wqkv, woutt[None]], axis=0)
    wall = lax.all_gather(wts, "seq", axis=1, tiled=True)
    mine = half_of(cot, 2)
    dh = call(functools.partial(back_conv_kernel, n), sds((2, rows, 256)), [SMEM] + [VMEM] * 5, scratch)(
        counts, cot, ring(mine[:, -192:], mine[:, :192]), k7, k5, k3
    )
    dhrb = swap(n, lax.all_gather(dh.astype(bf16), "head", axis=2, tiled=True))
    return xblk, normed, xbar, wall, dh, dhrb


def half_ring(n, hal):
    size = n // 2
    up = [(i, i // size * size + (i + 1) % size) for i in range(n)]
    return jnp.stack([lax.ppermute(hal[1], "seq", up), lax.ppermute(hal[0], "seq", [(j, i) for i, j in up])])


def three_rows(stat, first):
    return (stat[:, first:first + 1] + stat[:, first + 1:first + 2]) + stat[:, first + 2:first + 3]


def reduce_plain(n, blkb, blkd, halv, hald):
    _, g, _ = place(n)
    stat = blkb[:, 64:].astype(f32)
    top, total = three_rows(stat, 0), three_rows(stat, 3)
    best = half_max(n, top)
    w = jnp.exp(top - best)
    total = half_sum(n, total * w)
    value = half_sum(n, blkb[:, 0:64].astype(f32) * w)
    dct = half_sum(n, blkd.astype(f32)).astype(bf16)
    stat = jnp.concatenate(split3(best) + split3(total) + [jnp.zeros((4, 10, MARKS), f32)], axis=1)
    whole = jnp.concatenate([value, stat], axis=1).astype(bf16)
    h = head_of(g)
    recvb, recvd = lax.dynamic_slice_in_dim(whole, h, 1, 0), lax.dynamic_slice_in_dim(dct, h, 1, 0)
    return recvb, recvd, half_ring(n, halv), half_ring(n, hald)


def spread_plain(n, res):
    _, g, _ = place(n)
    held = ((jnp.arange(4) == head_of(g)) & is_owner(g))[:, None, None]
    return half_sum(n, jnp.where(held, res[None].astype(f32), 0.0)).astype(bf16)


def scores_kernel(n, cnt, normed, xbar, wall, dhrb, qt, kt, vt, qlt, klt, dot, wback, a1, e3, blkb, blkd, halv, hald):
    half, _, _ = place(n)
    count = cnt[half]
    wback[...] = wall[3].astype(f32).T.astype(bf16)
    project(n, count, normed, wall, qt, kt, vt)
    value_edges(n, count, normed, wall, halv)
    landmarks(xbar, wall, qlt, klt)
    key_scores(n, count, kt, qlt, vt, e3, blkb)
    query_scores(qt, klt, a1)
    out_grads(dhrb, wback, dot, hald)
    partial_dc(dot, a1, blkd)


def chain_kernel(n, recvb, recvd, qlt, klt, res, dqz, ps, ts, xs):
    _, g, _ = place(n)
    here = head_rows(head_of(g))
    dqz[...] = jnp.zeros_like(dqz)

    @pl.when(is_owner(g))
    def _():
        chain(qlt[here], klt[here], recvb, recvd, res, dqz, ps, ts, xs)()


def grads_kernel(n, cnt, normed, xbar, wall, wback, dhrb, qt, kt, vt, qlt, klt, dot, a1, e3, blkb, resall, rhv, rhd, taps,
                 dqz, po, dn, ep, wpart, gtaps, tm, th, hv, hdt, hvr, vr, conv, dconv, gsum, att, dp, dlm):
    half, _, _ = place(n)
    make_bands(taps, normed.shape[1], tm, th)
    value_conv(n, vt, rhv, tm, th, hv, vr, hvr, conv)
    value_conv_back(n, dot, rhd, tm, th, hdt, vr, hvr, dconv, gsum, gtaps)
    attend(resall, a1, conv, att)
    output_rows(att, wback, po)
    score_grads(n, cnt[half], qt, kt, vt, qlt, klt, dot, a1, e3, blkb, resall, dqz, dconv, dp, dlm)
    mark_rows(wall, dlm, ep)
    input_rows(wall, dp, dn)
    weight_grads(normed, xbar, dhrb, att, dp, dlm, wpart)


def hidden_kernel(cnt, tok, obias, part, hid, z):
    for s in range(2):
        z[s] = hidden_rows(cnt[s], s, tok, obias, part[s], hid).astype(bf16)


def final_kernel(n, cnt, hid, halo, cot, k7, k5, k3, pbias, xblk, dn, dnr, eall, gain, dh, gtaps,
                 outh, lnb, gk, small, kc, zs, pad, gacc):
    half, g, _ = place(n)
    join_taps(kc, k7, k5, k3)
    gacc[...] = jnp.zeros_like(gacc)
    small[...] = jnp.zeros_like(small)
    for s in range(2):
        grid_forward(n, cnt[s], s, hid, halo, cot, kc, pbias, outh, zs, pad, gacc)
    grid_sums(gacc, dh, cot, gtaps, gk)
    for b in range(2):
        lnb[b] = norm_back(n, g, cnt[half], b, xblk, dn, dnr, eall, gain, small)


def late_plain(n, counts, tok, cot, xblk, dh, po, ep, dn, wpart, gtaps, gain, obias, pbias, k7, k5, k3, scratch):
    rows = tok.shape[1]
    part = half_of(swap(n, lax.psum(po.astype(f32), "head").astype(bf16)), 2)
    hid, z = call(hidden_kernel, [sds((2, rows, 256)), sds((2, rows, 256), bf16)], [SMEM] + [VMEM] * 3)(
        counts, tok, obias, part
    )
    dnr = lax.ppermute(dn, "head", [(0, 1), (1, 0)])
    eall = half_sum(n, lax.psum(ep.astype(f32), "head")).astype(bf16)
    outh, lnb, gk, small = call(
        functools.partial(final_kernel, n),
        [sds((2, rows, 256), bf16), sds((2, rows, 512)), sds((56, 256)), sds((8, 512))],
        [SMEM] + [VMEM] * 14,
        scratch + [pltpu.VMEM((49, 8, 256), f32)],
    )(counts, hid, ring(z[:, -192:], z[:, :192]), cot, k7, k5, k3, pbias, xblk, dn, dnr, eall, gain, dh, gtaps)
    out = lax.all_gather(outh, "head", axis=2, tiled=True)
    dhf = lax.all_gather(dh, "head", axis=2, tiled=True)
    gw = lax.psum_scatter(wpart.astype(f32), "seq", scatter_dimension=1, tiled=True)
    gk, small = lax.psum((gk, small), "seq")
    gkall = lax.all_gather(gk, "head", axis=1, tiled=True)
    return out, swap(n, lnb), dhf, gw, small[0:2].reshape(8, 128), gkall


def layer_plain(n, counts, tok, cot, gain, bias, wqkv, woutt, taps, obias, pbias, k7, k5, k3):
    rows = tok.shape[1]
    made = layer_buffers(n, rows, wqkv.shape[1])

    def out(*names):
        return [sds(*made[name]) for name in names]

    def tmp(*names):
        return [pltpu.VMEM(*made[name]) for name in names]

    conv_tmp = tmp("kc", "zs", "pad")
    xblk, normed, xbar, wall, dh, dhrb = start_plain(
        n, counts, tok, cot, gain, bias, wqkv, woutt, k7, k5, k3, conv_tmp
    )
    qt, kt, vt, qlt, klt, dot, wback, a1, e3, blkb, blkd, halv, hald = call(
        functools.partial(scores_kernel, n),
        out("qt", "kt", "vt", "qlt", "klt", "dot", "wback", "a1", "e3", "blkb", "blkd", "halv", "hald"),
        [SMEM] + [VMEM] * 4,
    )(counts, normed, xbar, wall, dhrb)
    recvb, recvd, rhv, rhd = reduce_plain(n, blkb, blkd, halv, hald)
    res, dqz = call(
        functools.partial(chain_kernel, n), out("res", "dqz"), [VMEM] * 4, tmp("ps", "ts", "xs")
    )(recvb, recvd, qlt, klt)
    resall = spread_plain(n, res)
    po, dn, ep, wpart, gtaps = call(
        functools.partial(grads_kernel, n),
        out("po", "dn", "ep", "wpart", "gtaps"),
        [SMEM] + [VMEM] * 19,
        tmp("tm", "th", "hv", "hdt", "hvr", "vr", "conv", "dconv", "gsum", "att", "dp", "dlm"),
    )(counts, normed, xbar, wall, wback, dhrb, qt, kt, vt, qlt, klt, dot, a1, e3, blkb, resall, rhv, rhd, taps, dqz)
    return late_plain(
        n, counts, tok, cot, xblk, dh, po, ep, dn, wpart, gtaps, gain, obias, pbias, k7, k5, k3, conv_tmp
    )


def shards(n, tokens, counts, ln_gain, ln_bias, w_qkv, conv_taps, w_out, out_bias, kernel7, kernel5, kernel3, ppeg_bias, cotangent):
    rows, wr = tokens.shape[1], w_qkv.shape[1]
    gain, bias, obias, pbias = (v[None, :] for v in (ln_gain, ln_bias, out_bias, ppeg_bias))
    args = (counts, tokens, cotangent, gain, bias, w_qkv, w_out.T, conv_taps, obias, pbias, kernel7, kernel5, kernel3)
    if n == 16:
        results, buffers = layer_results(n, rows, wr), layer_buffers(n, rows, wr)
        names = INPUTS + tuple(results) + tuple(buffers) + SEMS
        made = call(
            functools.partial(layer_kernel, n, names),
            [sds(*v) for v in results.values()],
            [SMEM] + [VMEM] * 12,
            [pltpu.VMEM(*v) for v in buffers.values()] + [DMA((2, n)) for _ in SEMS],
            cid=0,
            vmem=60,
        )(*args)
    else:
        made = layer_plain(n, *args)
    vec = sds((1, 512))
    out, gx, gwqkv, gwoutt, ggain, gbias, gtaps, gob, k7o, k5o, k3o, gpb = call(
        result_kernel,
        [sds((2, rows, 512), bf16), sds((2, rows, 512)), sds((3, wr, 256)), sds((wr, 256)), vec, vec, sds((4, 33)), vec,
         sds((7, 7, 512)), sds((5, 5, 512)), sds((3, 3, 512)), vec],
        [VMEM] * 6,
    )(*made)
    return out, gx, ggain[0], gbias[0], gwqkv, gtaps, gwoutt.T, gob[0], k7o, k5o, k3o, gpb[0]


def solution(mesh):
    rows, cols = P(None, "seq", None), P(None, "seq", "head")
    return jax.shard_map(
        functools.partial(shards, mesh.shape["seq"]),
        mesh=mesh,
        in_specs=(rows, P(), P(), P(), cols, P("head", None), P("head", "seq"), P(), P(), P(), P(), P(), rows),
        out_specs=(rows, rows, P(), P(), cols, P("head", None), P("head", "seq"), P(), P(), P(), P(), P()),
        check_vma=False,
    )
```

time: 174 us -> 127 us (0.73)
  Pallas kernels: 159 us -> 125 us
  local copies, waits for them, and re-layouts: 12.9 us -> 0 us
    pallas_call x7 -> x2, Pallas kernels: 159 us -> 125 us  [the longest x1 122 us: shards(): call(functools.partial(layer_kernel, n, names), [sds(*v) for v in results...]
    unnamed x18 -> x0, local copies, waits for them, and re-layouts: 9.09 us -> none
    slice x4 -> x0, local copies, waits for them, and re-layouts: 2.24 us -> none  [the longest x1 1.38 us: shards(): gkall[50]]
where the time goes in v3:
time: 127 us; the launch traced here: 126 us
  Pallas kernels  125 us (98%)
    pallas_call x1, Pallas kernels, shards(): call(functools.partial(layer_kernel, n, names), [sds(*v) for v in results...  122 us
    pallas_call x1, Pallas kernels, shards(): call(result_kernel, [sds((2, rows, 512), bf16), sds((2, rows, 512)), sds(...  3.24 us

profile of v3, /device:TPU:0, one launch (start us, length us, event | category | flops | bytes accessed | tf_op | source)
XLA Modules:
  0.0 126.3 jit_solution(15769448787356991506)
XLA Ops:
  0.6 122.2 %shard_map.220 = (bf16[2,256,512]{2,1,0:T(8,128)(2,1)}, f32[2,256,512]{2,1,0:T(8,128)}, f32[2,256,512]{2,1,0:T(8,128)}, f32[4,32,256]{2,1,0:T(8,128)}, f32[8,128]{1,0:T(8,128)}, /*index=5*/f32[56,512]{1,0:T(8,128)}) custom-call(s32[2]{0:T(128)} %refs_0_.1, bf16[2,256,512]{2,1,0:T(8,128)(2,1)} %refs_1_.1, bf16[2,256,512]{2,1,0:T(8,128)(2,1)} %refs_2_.1, ...), custom_call_target="tpu_custom_call" | custom-call | tf_op jit(solution)/shard_map/pallas_call | solution.py:1165
  122.9 3.2 %shard_map.221 = (bf16[2,256,512]{2,1,0:T(8,128)(2,1)}, f32[2,256,512]{2,1,0:T(8,128)}, f32[3,32,256]{2,1,0:T(8,128)}, f32[32,256]{1,0:T(8,128)}, f32[1,512]{1,0...) custom-call(bf16[2,256,512]{2,1,0:T(8,128)(2,1)} %get-tuple-element., ...), custom_call_target="tpu_custom_call" | custom-call | tf_op jit(solution)/shard_map/pallas_call | solution.py:1176

commit v4 on v3

v4 whole, which is shorter than its diff:
```python
import functools

import jax
import jax.numpy as jnp
from jax import lax
from jax.experimental import pallas as pl
from jax.experimental.pallas import tpu as pltpu
from jax.sharding import PartitionSpec as P

MESH = pl.DeviceIdType.MESH
GRID_W = 64
MARKS = 256
SWEEPS = 6
EPSILON = 1e-05
f32, bf16 = jnp.float32, jnp.bfloat16
VMEM = pl.BlockSpec(memory_space=pltpu.VMEM)
SMEM = pl.BlockSpec(memory_space=pltpu.SMEM)
DMA = pltpu.SemaphoreType.DMA
SCALE = 64 ** -0.5
BLK = 144
PART = 80


def sds(shape, dtype=f32):
    return jax.ShapeDtypeStruct(shape, dtype)


def call(kernel, outs, specs, scratch=(), cid=None, vmem=56):
    extra = {} if cid is None else dict(collective_id=cid, has_side_effects=True)
    return pl.pallas_call(
        kernel,
        out_shape=outs,
        in_specs=specs,
        out_specs=jax.tree.map(lambda _: VMEM, outs),
        scratch_shapes=list(scratch),
        compiler_params=pltpu.CompilerParams(vmem_limit_bytes=vmem * 2**20, **extra),
    )


def mm(left, right, cl=1, cr=0):
    return lax.dot_general(left, right, (((cl,), (cr,)), ((), ())), preferred_element_type=f32)


def split(value):
    high = value.astype(bf16)
    return high, (value - high.astype(f32)).astype(bf16)


def split3(row):
    high = row.astype(bf16).astype(f32)
    rest = row - high
    mid = rest.astype(bf16).astype(f32)
    return [high, mid, rest - mid]


def mm3(left, right, cl=1, cr=0):
    (lh, ll), (rh, rl) = left, right
    return mm(lh, rh, cl, cr) + (mm(lh, rl, cl, cr) + mm(ll, rh, cl, cr))


def iota(shape, dim):
    return lax.broadcasted_iota(jnp.int32, shape, dim)


def edges(count, marks):
    return (marks * count + (MARKS - 1)) >> 8, ((marks + 1) * count + (MARKS - 1)) >> 8


def member(count, start, rows):
    low, high = edges(count, iota((MARKS, rows), 0))
    slot = iota((MARKS, rows), 1) + start
    return jnp.where((slot >= low) & (slot < high), 1.0, 0.0).astype(bf16)

OWNERS = (0, 3, 5, 6)


def place(n):
    me = lax.axis_index("seq")
    return me // (n // 2), lax.rem(me, n // 2), lax.rem(me + n // 2, n)


def head_of(g):
    return jnp.where(g == 0, 0, jnp.where(g == 3, 1, jnp.where(g == 5, 2, 3)))


def is_owner(g):
    return (g == 0) | (g == 3) | (g == 5) | (g == 6)


def my_half():
    return pl.ds(pl.multiple_of(lax.axis_index("head") * 256, 256), 256)


def block_start(n, g, b, rows):
    return (g + b * (n // 2)) * rows


def places(n, g, rows, shape, dim):
    at = iota(shape, dim)
    return at + g * rows + jnp.where(at >= rows, (n // 2 - 1) * rows, 0)


def norm_rows(x, gain, bias):
    x = x.astype(f32)
    xc = x - jnp.mean(x, axis=-1, keepdims=True)
    inv = lax.rsqrt(jnp.mean(xc * xc, axis=-1, keepdims=True) + EPSILON)
    return (xc * inv * gain + bias).astype(bf16)


def segment_sums(n, g, count, normed):
    rows = normed.shape[1]
    mine = my_half()
    return sum(mm(member(count, block_start(n, g, b, rows), rows), normed[b, :, mine]) for b in range(2))


def join_taps(kc, k7, k5, k3):
    mine = my_half()
    kc[...] = jnp.zeros_like(kc)
    for a in range(7):
        kc[a, 0:7] = k7[a, :, mine]
    for a in range(5):
        kc[a + 1, 1:6] = kc[a + 1, 1:6] + k5[a, :, mine]
    for a in range(3):
        kc[a + 2, 2:5] = kc[a + 2, 2:5] + k3[a, :, mine]


def load_grid(zs, pad, body, top, bottom):
    grid = body.shape[0] // GRID_W
    pad[...] = jnp.zeros_like(pad)
    pad[0:3, 8:8 + GRID_W] = top.reshape(3, GRID_W, 256)
    pad[3:3 + grid, 8:8 + GRID_W] = body.reshape(grid, GRID_W, 256)
    pad[3 + grid:6 + grid, 8:8 + GRID_W] = bottom.reshape(3, GRID_W, 256)
    for b in range(7):
        zs[b] = pad[:, 5 + b:5 + b + GRID_W, :]


def conv_row(zs, kc, i, flip):
    acc = jnp.zeros((GRID_W, 256), f32)
    for a in range(7):
        for b in range(7):
            ka, kb = (6 - a, 6 - b) if flip else (a, b)
            acc = acc + kc[ka, kb:kb + 1, :] * zs[b, i + a]
    return acc


def load_cot(n, b, cotb, top, bottom, zs, pad):
    at = block_start(n, place(n)[1], b, cotb.shape[1])
    top = jnp.where(at > 0, top.astype(f32), 0.0)
    bottom = jnp.where(at < (n - 1) * cotb.shape[1], bottom.astype(f32), 0.0)
    load_grid(zs, pad, cotb[b].astype(f32), top, bottom)


def back_conv(n, count, b, cotb, zs, kc, dh):
    _, g, _ = place(n)
    rows = cotb.shape[1]

    @pl.loop(0, rows // GRID_W)
    def _(i):
        acc = conv_row(zs, kc, i, True)
        here = pl.ds(pl.multiple_of(i * GRID_W, GRID_W), GRID_W)
        slot = iota((GRID_W, 256), 0) + (block_start(n, g, b, rows) + i * GRID_W)
        dh[b, here] = cotb[b, here].astype(f32) + jnp.where(slot < count, acc, 0.0)


def kernel_grads(n, count, b, i, hid, zs, gacc):
    _, g, _ = place(n)
    rows = hid.shape[1]
    here = pl.ds(pl.multiple_of(i * GRID_W, GRID_W), GRID_W)
    slot = iota((GRID_W, 256), 0) + (block_start(n, g, b, rows) + i * GRID_W)
    z = jnp.where(slot < count, hid[b, here], 0.0)
    for ka in range(7):
        for kb in range(7):
            part = (z * zs[6 - kb, i + 6 - ka]).reshape(GRID_W // 8, 8, 256)
            gacc[ka * 7 + kb] = gacc[ka * 7 + kb] + jnp.sum(part, axis=0)


def hidden_rows(n, count, b, x, obias, part, hid):
    _, g, _ = place(n)
    rows = x.shape[1]
    mine = my_half()
    hid[b] = x[b, :, mine].astype(f32) + part.astype(f32) + obias[:, mine]
    slot = iota((rows, 256), 0) + block_start(n, g, b, rows)
    return jnp.where(slot < count, hid[b], 0.0)


def ring_ends(n, g, b, recv):
    top = jnp.where(g > 0, recv[0, b].astype(f32), recv[0, 0].astype(f32) * b)
    bottom = jnp.where(g < n // 2 - 1, recv[1, b].astype(f32), recv[1, 1].astype(f32) * (1 - b))
    return top, bottom


def grid_forward(n, count, b, hid, halo, kc, pbias, outh, zs, pad):
    _, g, _ = place(n)
    rows = hid.shape[1]
    mine = my_half()
    slot = iota((rows, 256), 0) + block_start(n, g, b, rows)
    top, bottom = ring_ends(n, g, b, halo)
    load_grid(zs, pad, jnp.where(slot < count, hid[b], 0.0), top, bottom)

    @pl.loop(0, rows // GRID_W)
    def _(i):
        here = pl.ds(pl.multiple_of(i * GRID_W, GRID_W), GRID_W)
        acc = conv_row(zs, kc, i, False)
        outh[b, here] = (hid[b, here] + acc + pbias[:, mine]).astype(bf16)


def grid_sums(gacc, dh, cotb, gtaps, gk):
    for t in range(49):
        gk[t:t + 1] = jnp.sum(gacc[t], axis=0, keepdims=True)
    gk[49:50] = jnp.sum(dh[0], axis=0, keepdims=True) + jnp.sum(dh[1], axis=0, keepdims=True)
    g = cotb[0].astype(f32) + cotb[1].astype(f32)
    gk[50:51] = jnp.sum(g, axis=0, keepdims=True)
    gk[51:55] = gtaps[0:4]
    gk[55:56] = jnp.zeros((1, 256), f32)


def norm_back(n, g, count, b, x, dn, dnr, eall, gain, small):
    rows = x.shape[1]
    low, high = edges(count, iota((MARKS, 512), 0))
    e = (eall[...].astype(f32) / (high - low).astype(f32)).astype(bf16)
    mem = member(count, block_start(n, g, b, rows), rows)
    total = (dn[b].astype(f32) + dnr[b].astype(f32)) + mm(mem, e, 0, 0)
    x = x[b].astype(f32)
    xc = x - jnp.mean(x, axis=-1, keepdims=True)
    inv = lax.rsqrt(jnp.mean(xc * xc, axis=-1, keepdims=True) + EPSILON)
    xh = xc * inv
    dg = total * gain[...]
    m1 = jnp.mean(dg, axis=-1, keepdims=True)
    m2 = jnp.mean(dg * xh, axis=-1, keepdims=True)
    small[0:1] = small[0:1] + jnp.sum(total * xh, axis=0, keepdims=True)
    small[1:2] = small[1:2] + jnp.sum(total, axis=0, keepdims=True)
    return (dg - m1 - xh * m2) * inv


def spill_kernels(gkall, k7o, k5o, k3o):
    for a in range(7):
        k7o[a] = gkall[7 * a:7 * a + 7]
    for a in range(5):
        k5o[a] = gkall[7 * a + 8:7 * a + 13]
    for a in range(3):
        k3o[a] = gkall[7 * a + 16:7 * a + 19]


def greet(peers, pair=True):
    sem = pltpu.get_barrier_semaphore()
    for peer in peers:
        pl.semaphore_signal(sem, inc=1, device_id={"seq": peer}, device_id_type=MESH)
    if pair:
        hd = lax.axis_index("head")
        pl.semaphore_signal(sem, inc=1, device_id={"head": 1 - hd}, device_id_type=MESH)
    pl.semaphore_wait(sem, len(peers) + (1 if pair else 0))


def everyone(n):
    me = lax.axis_index("seq")
    return [lax.rem(me + i, n) for i in range(n)]


def cube(n):
    half, g, _ = place(n)
    return [half * (n // 2) + lax.rem(g + i, n // 2) for i in range(n // 2)]


def remote(src, dst, sems, i, **where):
    return pltpu.make_async_remote_copy(
        src_ref=src, dst_ref=dst, send_sem=sems.at[0, i], recv_sem=sems.at[1, i], device_id=where, device_id_type=MESH
    )


def go(copies):
    for c in copies:
        c.start()
    return copies


def got(copies):
    for c in copies:
        c.wait_recv()


def sent(copies):
    for c in copies:
        c.wait_send()


def project(n, count, normed, wall, wt, qt, kt, vt):
    _, g, _ = place(n)
    for j in range(3):
        wt[j] = wall[j].T
    rows = normed.shape[1]
    nr = normed[...].reshape(2 * rows, 512)
    qt[...] = mm(wt[0], nr, 1, 1).astype(bf16)
    kt[...] = mm(wt[1], nr, 1, 1).astype(bf16)
    slots = places(n, g, rows, (256, 2 * rows), 1)
    vt[...] = jnp.where(slots < count, mm(wt[2], nr, 1, 1), 0.0).astype(bf16)


def value_edges(n, count, normed, wall, halv):
    _, g, _ = place(n)
    rows = normed.shape[1]
    for b in range(2):
        for side, first in ((0, 0), (1, rows - 16)):
            slot = iota((16, 256), 0) + (block_start(n, g, b, rows) + first)
            v = mm(normed[b, first:first + 16], wall[2])
            halv[side, b] = jnp.where(slot < count, v, 0.0).astype(bf16)


def landmarks(xbar, wt, qlt, klt):
    qlt[...] = mm(wt[0], xbar[...], 1, 1).astype(bf16)
    klt[...] = mm(wt[1], xbar[...], 1, 1).astype(bf16)


def head_rows(h):
    return pl.ds(pl.multiple_of(h * 64, 64), 64)


def key_scores(n, count, kt, qlt, vt, e3, blkb, beside=None):
    _, g, _ = place(n)
    wide = kt.shape[1]
    ok = places(n, g, wide // 2, (wide, MARKS), 0) < count
    for h in range(4):
        here = slice(64 * h, 64 * h + 64)
        s3 = jnp.where(ok, mm(kt[here] * SCALE, qlt[here], 0, 0), -1e30)
        top = jnp.max(s3, axis=0, keepdims=True)
        e = jnp.where(ok, jnp.exp(s3 - top), 0.0)
        total = jnp.sum(e, axis=0, keepdims=True)
        er = e.astype(bf16)
        e3[h] = er
        blkb[h, 0:64] = mm(vt[here], er).astype(bf16)
        stat = jnp.concatenate(split3(top) + split3(total) + [jnp.zeros((10, MARKS), f32)], axis=0)
        blkb[h, 64:80] = stat.astype(bf16)
        if beside:
            beside(h)


def query_scores(qt, klt, a1, beside=None):
    for h in range(4):
        here = slice(64 * h, 64 * h + 64)
        s1 = mm(klt[here] * SCALE, qt[here], 0, 0)
        e1 = jnp.exp(s1 - jnp.max(s1, axis=0, keepdims=True))
        a1[h] = (e1 / jnp.sum(e1, axis=0, keepdims=True)).astype(bf16)
        if beside:
            beside(h)


def out_grads(dhrb, wback, dot, hald):
    rows = dhrb.shape[1]
    dot[...] = mm(wback[...], dhrb[...].reshape(2 * rows, 512), 1, 1).astype(bf16)
    for b in range(2):
        for side, first in ((0, 0), (1, rows - 16)):
            hald[side, b] = mm(dhrb[b, first:first + 16], wback[...], 1, 1).astype(bf16)


def partial_dc(dot, a1, blkd):
    @pl.loop(0, 4, unroll=4)
    def _(h):
        blkd[h] = mm(dot[head_rows(h)], a1[h], 1, 1).astype(bf16)


def three(stat, first):
    return (stat[first:first + 1] + stat[first + 1:first + 2]) + stat[first + 2:first + 3]


class Chain:
    def __init__(self, ql, kl, r):
        self.ql, self.kl, self.r = ql, kl, r

    def begin(self):
        r = self.r
        s2 = mm(self.ql[...] * SCALE, self.kl[...], 0, 0)
        e2 = jnp.exp(s2 - jnp.max(s2, axis=1, keepdims=True))
        a = e2 / jnp.sum(e2, axis=1, keepdims=True)
        r.amat[...] = a
        asp = split(a)
        r.asp[0], r.asp[1] = asp
        inv = self.sums()[4]
        r.pcur[...] = mm3(asp, asp, 1, 1) * inv

    def sums(self):
        a = self.r.amat[...]
        cs, rs = jnp.sum(a, axis=0, keepdims=True), jnp.sum(a, axis=1, keepdims=True)
        cm, rm = jnp.max(cs, axis=1, keepdims=True), jnp.max(rs, axis=0, keepdims=True)
        return cs, rs, cm, rm, 1.0 / (cm * rm)

    def sweep(self, k):
        r = self.r
        p = r.pcur[...]
        psp = split(p)
        t = mm3(psp, psp)
        tsp = split(t)
        r.ps[k, 0], r.ps[k, 1] = psp
        r.ts[k, 0], r.ts[k, 1] = tsp
        if k < SWEEPS - 1:
            r.pcur[...] = 0.25 * (13.0 * p - 15.0 * t + mm3(tsp, split(7.0 * p - t)))

    def powers(self, k):
        r = self.r
        return (r.ps[k, 0], r.ps[k, 1]), (r.ts[k, 0], r.ts[k, 1])

    def apply(self, x, k):
        psp, tsp = self.powers(k)
        xt = mm3(split(x), tsp)
        return 0.25 * (13.0 * x + 7.0 * xt - mm3(split(15.0 * x + xt), psp))

    def forward(self):
        r = self.r
        parts = r.recvb.shape[0]
        tops = [three(r.recvb[d, 64:80].astype(f32), 0) for d in range(parts)]
        top = functools.reduce(jnp.maximum, tops)
        total, value = 0.0, 0.0
        for d in range(parts):
            w = jnp.exp(tops[d] - top)
            total = total + three(r.recvb[d, 64:80].astype(f32), 3) * w
            value = value + r.recvb[d, 0:64].astype(f32) * w
        value = value / total
        x = value
        for k in range(SWEEPS):
            r.xs[k] = x
            x = self.apply(x, k)
        r.xs[SWEEPS] = x
        ct = mm3(split(x), (r.asp[0], r.asp[1])) * self.sums()[4]
        r.res[0:64] = ct.astype(bf16)
        r.ctf[...] = ct
        self.top, self.total, self.value = top, total, value

    def backward(self):
        r = self.r
        dct = r.recvd[0].astype(f32)
        for d in range(1, r.recvd.shape[0]):
            dct = dct + r.recvd[d].astype(f32)
        r.dctf[...] = dct
        y = mm3(split(dct), (r.asp[0], r.asp[1]), 1, 1) * self.sums()[4]
        for k in range(SWEEPS - 1, -1, -1):
            r.ys[k] = y
            y = self.apply(y, k)
        dbr = y.astype(bf16)
        r.res[64:128] = dbr
        rt = jnp.sum(dbr.astype(f32) * self.value, axis=0, keepdims=True)
        stat = split3(self.top) + split3(self.total) + split3(rt) + [jnp.zeros((7, MARKS), f32)]
        r.res[128:144] = jnp.concatenate(stat, axis=0).astype(bf16)

    def power_grad(self, k):
        r = self.r
        psp, tsp = self.powers(k)
        outer = mm3(split(r.ys[k]), split(r.xs[k]), 0, 0) * 0.125
        d = outer + outer.T
        eq = 0.25 * r.ecur[...]
        pd = mm3(psp, split(d))
        pe = mm3(psp, split(eq))
        new = 13.0 * eq - 15.0 * d + mm3(split(7.0 * pe - pd), psp)
        left = 7.0 * pd - 15.0 * pe + mm3(tsp, split(7.0 * eq - d - (pe + pe.T)))
        r.ecur[...] = new + (left + left.T)

    def finish(self):
        r = self.r
        ql, kl, a, dct, e = self.ql[...], self.kl[...], r.amat[...], r.dctf[...], r.ecur[...]
        cs, rs, cm, rm, inv = self.sums()
        grad = mm3(split(r.xs[SWEEPS]), split(dct), 0, 0) * inv + mm3(split(e), (r.asp[0], r.asp[1])) * (2.0 * inv)
        p0 = r.ps[0, 0].astype(f32) + r.ps[0, 1].astype(f32)
        slope = jnp.sum(jnp.sum(dct * r.ctf[...], axis=0, keepdims=True), axis=1, keepdims=True)
        slope = -inv * (slope + jnp.sum(jnp.sum(e * p0, axis=0, keepdims=True), axis=1, keepdims=True))
        eqc, eqr = jnp.where(cs == cm, 1.0, 0.0), jnp.where(rs == rm, 1.0, 0.0)
        grad = grad + (slope * rm) * (eqc / jnp.sum(eqc, axis=1, keepdims=True))
        grad = grad + (slope * cm) * (eqr / jnp.sum(eqr, axis=0, keepdims=True))
        dsc = a * (grad - jnp.sum(a * grad, axis=1, keepdims=True)) * SCALE
        dh, dl = split(dsc)
        return mm(kl, dh, 1, 1) + mm(kl, dl, 1, 1), mm(ql, dh) + mm(ql, dl)


def add_chain(here, dlm, grads):
    for j in range(2):
        dlm[j, here] = (dlm[j, here].astype(f32) + grads[j]).astype(bf16)


def band(base, shift, rows):
    wide = jnp.broadcast_to(base, (rows, 256))
    return pltpu.roll(wide, shift, 1, stride=1, stride_axis=0)


def diagonals(g, shift):
    return jnp.sum(pltpu.roll(g, shift, 1, stride=1, stride_axis=0), axis=0, keepdims=True)


def make_bands(taps, rows, tm, th):
    pi, pj = iota((rows, rows), 0), iota((rows, rows), 1)
    inside = (pi - pj <= 16) & (pj - pi <= 16)
    hi, hj = iota((32, rows), 0), iota((32, rows), 1)
    far = jnp.where(hi < 16, hi - hj, hj - hi - (rows - 32)) >= 0
    ti, tl = iota((33, 256), 0), iota((33, 256), 1)
    spots = [jnp.where(((ti + tl if f == 0 else tl - ti + 32) & 255) == 16, 1.0, 0.0).astype(bf16) for f in range(2)]
    pieces = [piece.astype(bf16) for piece in split3(taps[...])]
    for f in range(2):
        lines = mm(pieces[0], spots[f]) + mm(pieces[1], spots[f]) + mm(pieces[2], spots[f])
        for h in range(4):
            line = lines[h:h + 1, :]
            full = jnp.where(inside, band(line, 0, rows), 0.0)
            tm[f, h, 0], tm[f, h, 1] = split(full)
            both = jnp.concatenate([band(line, 240, 16), band(line, 0, 16)], axis=0)
            th[f, h, 0], th[f, h, 1] = split(jnp.where(far, both, 0.0))


def value_conv(n, vt, recvv, tm, th, hv, vr, hvr, conv):
    _, g, _ = place(n)
    rows = vt.shape[1] // 2
    pi, pj = iota((rows, rows), 0), iota((rows, rows), 1)
    mirror = jnp.where(pi + pj == rows - 1, 1.0, 0.0).astype(bf16)
    si, sj = iota((32, 32), 0), iota((32, 32), 1)
    mirror32 = jnp.where(si + sj == jnp.where(si < 16, 15, 47), 1.0, 0.0).astype(bf16)
    for b in range(2):
        part = slice(b * rows, (b + 1) * rows)
        hv[b] = jnp.concatenate(ring_ends(n, g, b, recvv), axis=0).T.astype(bf16)
        vr[b] = mm(vt[:, part], mirror).astype(bf16)
        hvr[b] = mm(hv[b], mirror32).astype(bf16)

        @pl.loop(0, 4, unroll=4)
        def _(h):
            here = head_rows(h)
            v, vh = vt[here, part], hv[b, here]
            conv[here, part] = mm(v, tm[0, h, 0]) + mm(v, tm[0, h, 1]) + mm(vh, th[0, h, 0]) + mm(vh, th[0, h, 1])


def value_conv_back(n, dot, recvd, tm, th, hd, vr, hvr, dconv, gsum, gtaps):
    _, g, _ = place(n)
    rows = dot.shape[1] // 2
    pi, pj = iota((rows, rows), 0), iota((rows, rows), 1)
    hi, hj = iota((32, rows), 0), iota((32, rows), 1)
    near = (pi + pj >= rows - 17) & (pi + pj <= rows + 15)
    beyond = jnp.where(hi < 16, 15 - hi - hj, hi + hj - (rows + 15)) >= 0
    for b in range(2):
        hd[b] = jnp.concatenate(ring_ends(n, g, b, recvd), axis=0).T.astype(bf16)

    @pl.loop(0, 4, unroll=4)
    def _(h):
        here = head_rows(h)
        s, sh = 0.0, 0.0
        for b in range(2):
            part = slice(b * rows, (b + 1) * rows)
            d, dh = dot[here, part], hd[b, here]
            dconv[here, part] = mm(d, tm[1, h, 0]) + mm(d, tm[1, h, 1]) + mm(dh, th[1, h, 0]) + mm(dh, th[1, h, 1])
            s = s + mm(vr[b, here], d, 0, 0)
            sh = sh + mm(hvr[b, here], d, 0, 0)
        s, sh = jnp.where(near, s, 0.0), jnp.where(beyond, sh, 0.0)
        gsum[h] = jnp.broadcast_to(diagonals(s, 1) + diagonals(sh[0:16], 1) + diagonals(sh[16:32], 241), (8, 256))

    for h in range(4):
        gtaps[h:h + 1, :] = gsum[h, 0:1]
    gtaps[4:8, :] = jnp.zeros((4, 256), f32)


def attend(res, a1, conv, att):
    @pl.loop(0, 4, unroll=4)
    def _(h):
        here = head_rows(h)
        att[here] = (mm(res[h, 0:64], a1[h]) + conv[here]).astype(bf16)


def score_grads(n, count, qt, kt, vt, qlt, klt, dot, a1, e3, blkb, res, dconv, dp, dlm):
    _, g, _ = place(n)
    wide = qt.shape[1]
    slots = places(n, g, wide // 2, (64, wide), 1)

    @pl.loop(0, 4, unroll=4)
    def _(h):
        here = head_rows(h)
        ct, dbt = res[h, 0:64], res[h, 64:128]
        stat = res[h, 128:144].astype(f32)
        own = three(blkb[h, 64:80].astype(f32), 0)
        factor = jnp.exp(own - three(stat, 0)) / three(stat, 3)
        rt = three(stat, 6)
        do, v = dot[here], vt[here]
        a = a1[h].astype(f32)
        da = mm(ct, do, 0, 0)
        d1 = (a * (da - jnp.sum(a * da, axis=0, keepdims=True))).astype(bf16)
        dp[0, here] = mm(klt[here] * SCALE, d1).astype(bf16)
        dlm[1, here] = mm(qt[here] * SCALE, d1, 1, 1).astype(bf16)
        a3 = e3[h].astype(f32) * factor
        d3 = (a3 * (mm(v, dbt, 0, 0) - rt)).astype(bf16)
        dlm[0, here] = mm(kt[here] * SCALE, d3).astype(bf16)
        dp[1, here] = mm(qlt[here] * SCALE, d3, 1, 1).astype(bf16)
        dv = mm(dbt, a3.astype(bf16), 1, 1) + dconv[here]
        dp[2, here] = jnp.where(slots < count, dv, 0.0).astype(bf16)


def mark_rows(wall, dlm, ep):
    ep[...] = (mm(wall[0], dlm[0]) + mm(wall[1], dlm[1])).T.astype(bf16)


def input_rows(wall, dp, dn):
    rows = dn.shape[1]
    d = mm(wall[0], dp[0]) + mm(wall[1], dp[1]) + mm(wall[2], dp[2])
    dn[...] = d.T.astype(bf16).reshape(2, rows, 512)


def output_rows(att, wback, po):
    rows = po.shape[1]
    po[...] = mm(att[...], wback[...], 0, 0).astype(bf16).reshape(2, rows, 512)


def weight_grad(j, normed, xbar, dhrb, att, dp, dlm, wpart):
    rows = normed.shape[1]
    if j == 3:
        grad = mm(att[...], dhrb[...].reshape(2 * rows, 512))
    else:
        grad = mm(dp[j], normed[...].reshape(2 * rows, 512))
        if j < 2:
            grad = grad + mm(dlm[j], xbar[...])
    wpart[j] = grad.T.astype(bf16)


class Refs:
    def __init__(self, names, refs):
        self.__dict__.update(zip(names, refs))


INPUTS = ("cnt", "tok", "cot", "gain", "bias", "wqkv", "woutt", "taps", "obias", "pbias", "k7", "k5", "k3")


def layer_results(n, rows, wr):
    return dict(
        outf=((2, rows, 512), bf16), gxf=((2, rows, 512), f32), gw=((4, wr, 256), f32),
        sums=((8, 128), f32), gkall=((56, 512), f32),
    )


def layer_buffers(n, rows, wr):
    size = n // 2
    mb, wide, grid = MARKS // size, 2 * rows, rows // GRID_W
    half2 = (2, rows, 256)
    return dict(
        wts=((4, wr, 256), bf16), wall=((4, 512, 256), bf16), wback=((256, 512), bf16), wt=((3, 256, 512), bf16),
        xblk=((2, rows, 512), bf16), normed=((2, rows, 512), bf16), xbar=((MARKS, 512), bf16),
        xp=((MARKS, 256), bf16), xr=((size, mb, 256), bf16), xm=((mb, 256), bf16),
        halo=((2, 2, 192, 256), bf16), dh=(half2, f32), dhrb=((2, rows, 512), bf16),
        kc=((7, 8, 256), f32), zs=((7, grid + 6, GRID_W, 256), f32), zc=((2, 7, grid + 6, GRID_W, 256), f32), pad=((grid + 6, GRID_W + 16, 256), f32),
        qt=((256, wide), bf16), kt=((256, wide), bf16), vt=((256, wide), bf16), dot=((256, wide), bf16),
        qlt=((256, MARKS), bf16), klt=((256, MARKS), bf16), a1=((4, MARKS, wide), bf16), e3=((4, wide, MARKS), bf16),
        blkb=((4, PART, MARKS), bf16), blkd=((4, 64, MARKS), bf16),
        recvb=((size, PART, MARKS), bf16), recvd=((size, 64, MARKS), bf16),
        halv=((2, 2, 16, 256), bf16), hald=((2, 2, 16, 256), bf16), rhv=((2, 2, 16, 256), bf16), rhd=((2, 2, 16, 256), bf16),
        ps=((SWEEPS, 2, 256, 256), bf16), ts=((SWEEPS, 2, 256, 256), bf16), xs=((SWEEPS + 1, 64, 256), f32), ys=((SWEEPS, 64, 256), f32), ctf=((64, 256), f32), dctf=((64, 256), f32),
        amat=((256, 256), f32), asp=((2, 256, 256), bf16), pcur=((256, 256), f32), ecur=((256, 256), f32),
        res=((BLK, MARKS), bf16), resall=((8, BLK, MARKS), bf16),
        tm=((2, 4, 2, rows, rows), bf16), th=((2, 4, 2, 32, rows), bf16), hv=((2, 256, 32), bf16), hdt=((2, 256, 32), bf16),
        hvr=((2, 256, 32), bf16), vr=((2, 256, rows), bf16), conv=((256, wide), f32), dconv=((256, wide), f32),
        gsum=((4, 8, 256), f32), gtaps=((8, 256), f32), att=((256, wide), bf16), dp=((3, 256, wide), bf16),
        dlm=((2, 256, MARKS), bf16), po=((2, rows, 512), bf16), dn=((2, rows, 512), bf16), ep=((MARKS, 512), bf16),
        wpart=((4, 512, 256), bf16), er=((MARKS, 256), bf16), es=((MARKS, 256), bf16), erv=((size, mb, 256), bf16),
        em=((mb, 256), bf16), eall=((MARKS, 512), bf16), por=(half2, bf16),
        dnr=((2, rows, 512), bf16), hid=(half2, f32), z=(half2, bf16), cotb=(half2, bf16), lnf=((rows, 512), f32), dhf=((rows, 512), f32), zhalo=((2, 2, 192, 256), bf16),
        lnr=((rows, 512), bf16), lns=((rows, 256), bf16), wrv=((size, 2, 4, wr, 256), bf16), wsum=((4, wr, 256), bf16),
        wone=((4, wr, 256), bf16), gacc=((49, 8, 256), f32), outh=(half2, bf16), gk=((56, 256), f32),
        gkr=((n, 8, 256), f32), gkm=((8, 256), f32), small=((8, 512), f32), smr=((n, 8, 128), f32), smx=((8, 128), f32),
    )


SEMS = dict(
    s_w=2, s_v=2, s_n=2, s_t=1, s_h=4, s_x=1, s_g=1, s_p=4, s_d=1, s_b=1, s_c=1, s_r=1, s_q=4, s_a=4, s_e=1, s_f=1, s_z=2, s_l=5,
    s_y=1, s_u=1, s_k=1, s_m=1, s_s=1,
)


class Many:
    def __init__(self, total, sems, i, **where):
        self.sems, self.i, self.all = sems, i, remote(total, total, sems, i, **where)

    def add(self, src, dst, **where):
        remote(src, dst, self.sems, self.i, **where).start()

    def wait_recv(self):
        self.all.wait_recv()

    def wait_send(self):
        self.all.wait_send()


def layer_kernel(n, names, *refs):
    r = Refs(names, refs)
    half, g, partner = place(n)
    me = lax.axis_index("seq")
    hd = lax.axis_index("head")
    other = 1 - half
    size = n // 2
    rows = r.tok.shape[1]
    mb, wr = MARKS // size, r.wts.shape[1]
    mine = my_half()
    theirs = pl.ds(pl.multiple_of((1 - hd) * 256, 256), 256)
    count = r.cnt[half]
    near, far = cube(n), everyone(n)
    core = 1 - hd

    def wrow(device):
        return pl.ds(pl.multiple_of(device * wr, wr), wr)

    def marks(i):
        return pl.ds(pl.multiple_of(lax.rem(g + i, size) * mb, mb), mb)

    cube_rows = pl.ds(0, (size - 1) * wr)
    cube_marks = pl.ds(0, (size - 1) * mb)

    def fan(total, sems, i, pieces):
        group = Many(total, sems, i, seq=near[1])
        for j, (src, dst) in enumerate(pieces, 1):
            group.add(src, dst, seq=near[j])
        return [group]

    r.wts[0:3] = r.wqkv[...]
    r.wts[3] = r.woutt[...]
    greet(far[1:])
    qkv = slice(0, 3)
    c_w = go([remote(r.wts.at[qkv], r.wall.at[qkv, wrow(me)], r.s_w, 0, seq=partner)])
    c_t = go([remote(r.tok.at[other, :, mine], r.xblk.at[half, :, mine], r.s_t, 0, seq=partner)])
    c_v = fan(r.wall.at[qkv, cube_rows], r.s_v, 0, [(r.wts.at[qkv], r.wall.at[qkv, wrow(me)])] * (size - 1))
    up, down = far[1], far[n - 1]
    first, final = pl.ds(0, 192), pl.ds(rows - 192, 192)
    c_h = go([
        remote(r.cot.at[up // size, final, mine], r.halo.at[0, up // size], r.s_h, 0, seq=up),
        remote(r.cot.at[down // size, first, mine], r.halo.at[1, down // size], r.s_h, 1, seq=down),
    ])
    r.wall[:, wrow(me)] = r.wts[...]
    r.cotb[half] = r.cot[half, :, mine]
    r.xblk[half] = r.tok[half]
    r.normed[half] = norm_rows(r.tok[half], r.gain[...], r.bias[...])
    join_taps(r.kc, r.k7, r.k5, r.k3)
    got(c_w)
    pair_rows = (r.wall.at[qkv, wrow(partner)],) * 2
    c_v += fan(r.wall.at[qkv, cube_rows], r.s_v, 1, [pair_rows] * (size - 1))
    make_bands(r.taps, rows, r.tm, r.th)

    got(c_t)
    c_p = go([remote(r.xblk.at[other, :, mine], r.xblk.at[other, :, mine], r.s_p, 0, head=core)])
    c_d = go([remote(r.cot.at[other, :, mine], r.cotb.at[half], r.s_d, 0, seq=partner)])
    got(c_p)
    r.normed[other] = norm_rows(r.xblk[other], r.gain[...], r.bias[...])
    r.xp[...] = segment_sums(n, g, count, r.normed).astype(bf16)
    c_x = fan(r.xr.at[pl.ds(0, size - 1)], r.s_x, 0, [(r.xp.at[marks(i)], r.xr.at[g]) for i in range(1, size)])
    row = marks(0)
    r.xr[pl.ds(g, 1)] = r.xp[row][None]
    c_w += go([remote(r.wts.at[3], r.wall.at[3, wrow(me)], r.s_w, 1, seq=partner)])
    got(c_h)
    load_cot(n, half, r.cotb, r.halo[0, half], r.halo[1, half], r.zc.at[half], r.pad)
    back_conv(n, count, half, r.cotb, r.zc.at[half], r.kc, r.dh)
    c_p += go([remote(r.dh.at[half], r.dhf.at[:, mine], r.s_p, 2, head=core)])
    r.dhf[:, mine] = r.dh[half]
    got(c_x)
    total = r.xr[0].astype(f32)
    for d in range(1, size):
        total = total + r.xr[d].astype(f32)
    low, high = edges(count, iota((mb, 256), 0) + g * mb)
    r.xm[...] = (total / (high - low).astype(f32)).astype(bf16)
    r.xbar[row, mine] = r.xm[...]
    c_g = fan(r.xbar.at[cube_marks, mine], r.s_g, 0, [(r.xm, r.xbar.at[row, mine])] * (size - 1))
    got(c_d)
    above = jnp.where((g == size - 1) & (half == 0), half, other)
    below = jnp.where((g == 0) & (half == 1), half, other)
    c_h += go([
        remote(r.cotb.at[above, final], r.halo.at[0, other], r.s_h, 2, seq=near[1]),
        remote(r.cotb.at[below, first], r.halo.at[1, other], r.s_h, 3, seq=near[size - 1]),
    ])
    got(c_v)
    project(n, count, r.normed, r.wall, r.wt, r.qt, r.kt, r.vt)
    c_n = fan(r.wall.at[3, cube_rows], r.s_n, 0, [(r.wts.at[3], r.wall.at[3, wrow(me)])] * (size - 1))
    got(c_w[1:])
    pair_row = (r.wall.at[3, wrow(partner)],) * 2
    c_n += fan(r.wall.at[3, cube_rows], r.s_n, 1, [pair_row] * (size - 1))
    got(c_g)
    c_p += go([remote(r.xbar.at[:, mine], r.xbar.at[:, mine], r.s_p, 1, head=core)])
    value_edges(n, count, r.normed, r.wall, r.halv)
    c_q = go([
        remote(r.halv.at[1], r.rhv.at[0], r.s_q, 0, seq=near[1]),
        remote(r.halv.at[0], r.rhv.at[1], r.s_q, 1, seq=near[size - 1]),
    ])
    got(c_h[2:])
    load_cot(n, other, r.cotb, r.halo[0, other], r.halo[1, other], r.zc.at[other], r.pad)
    back_conv(n, count, other, r.cotb, r.zc.at[other], r.kc, r.dh)
    r.dhrb[:, :, mine] = r.dh[...].astype(bf16)
    c_p += go([remote(r.dhrb.at[:, :, mine], r.dhrb.at[:, :, mine], r.s_p, 3, head=core)])

    got(c_p[2:3])
    landmarks(r.xbar, r.wt, r.qlt, r.klt)
    here = head_rows(head_of(g))
    one = Chain(r.qlt.at[here], r.klt.at[here], r)
    one.begin()
    key_scores(n, count, r.kt, r.qlt, r.vt, r.e3, r.blkb, one.sweep)

    def give(blk, recv, sems):
        for h, o in enumerate(OWNERS):

            @pl.when(g != o)
            def _():
                remote(blk.at[h], recv.at[g], sems, 0, seq=half * size + o).start()

            @pl.when(g == o)
            def _():
                recv[pl.ds(g, 1)] = blk[h:h + 1]

    def gave(blk, sems):
        remote(blk, blk, sems, 0, seq=near[1]).wait_send()

    give(r.blkb, r.recvb, r.s_b)
    query_scores(r.qt, r.klt, r.a1, lambda h: one.sweep(4 + h) if h < 2 else None)
    got(c_n)
    r.wback[...] = r.wall[3].T
    got(c_p[3:4])
    out_grads(r.dhrb, r.wback, r.dot, r.hald)
    c_q += go([
        remote(r.hald.at[1], r.rhd.at[0], r.s_q, 2, seq=near[1]),
        remote(r.hald.at[0], r.rhd.at[1], r.s_q, 3, seq=near[size - 1]),
    ])
    partial_dc(r.dot, r.a1, r.blkd)
    give(r.blkd, r.recvd, r.s_c)

    @pl.when(is_owner(g))
    def _():
        def wait_for(recv, sems):
            remote(recv.at[pl.ds(0, size - 1)], recv.at[pl.ds(0, size - 1)], sems, 0, seq=near[1]).wait_recv()

        wait_for(r.recvb, r.s_b)
        one.forward()
        wait_for(r.recvd, r.s_c)
        one.backward()
        for h, o in enumerate(OWNERS):

            @pl.when(g == o)
            def _():
                for i in range(1, size):
                    remote(r.res, r.resall.at[h], r.s_r, 0, seq=near[i]).start()
                r.resall[h] = r.res[...]

    got(c_q)
    value_conv(n, r.vt, r.rhv, r.tm, r.th, r.hv, r.vr, r.hvr, r.conv)
    value_conv_back(n, r.dot, r.rhd, r.tm, r.th, r.hdt, r.vr, r.hvr, r.dconv, r.gsum, r.gtaps)
    r.small[...] = jnp.zeros_like(r.small)
    r.gacc[...] = jnp.zeros_like(r.gacc)

    def results(count):
        return remote(r.resall.at[pl.ds(0, count)], r.resall.at[pl.ds(0, count)], r.s_r, 0, seq=near[1])

    @pl.when(is_owner(g))
    def _():
        results(3).wait_recv()

    @pl.when(jnp.logical_not(is_owner(g)))
    def _():
        results(4).wait_recv()

    attend(r.resall, r.a1, r.conv, r.att)
    output_rows(r.att, r.wback, r.po)
    c_a = go([remote(r.po.at[:, :, theirs], r.por, r.s_a, 0, head=core)])
    weights = (r.normed, r.xbar, r.dhrb, r.att, r.dp, r.dlm, r.wpart)
    c_y = [Many(r.wrv.at[pl.ds(0, size - 1)], r.s_y, 0, seq=near[1])]

    def send_weights(j):
        for i in range(1, size):
            for k, device in enumerate((near[i], lax.rem(near[i] + size, n))):
                c_y[0].add(r.wpart.at[j, wrow(device)], r.wrv.at[g, k, j], seq=near[i])

    score_grads(n, count, r.qt, r.kt, r.vt, r.qlt, r.klt, r.dot, r.a1, r.e3, r.blkb, r.resall, r.dconv, r.dp, r.dlm)
    got(c_a[0:1])
    for b in range(2):
        part = r.po[b, :, mine].astype(f32) + r.por[b].astype(f32)
        r.z[b] = hidden_rows(n, count, b, r.xblk, r.obias, part, r.hid).astype(bf16)
    c_z = go([
        remote(r.z.at[:, final], r.zhalo.at[0], r.s_z, 0, seq=near[1]),
        remote(r.z.at[:, first], r.zhalo.at[1], r.s_z, 1, seq=near[size - 1]),
    ])
    r.ecur[...] = jnp.zeros_like(r.ecur)
    lines = rows // GRID_W

    @pl.loop(0, 2 * lines)
    def _(i):
        kernel_grads(n, count, i // lines, lax.rem(i, lines), r.hid, r.zc.at[i // lines], r.gacc)

        @pl.when(i < SWEEPS)
        def _():
            one.power_grad(jnp.maximum(SWEEPS - 1 - i, 0))

    @pl.when(is_owner(g))
    def _():
        add_chain(here, r.dlm, one.finish())

    mark_rows(r.wall, r.dlm, r.ep)
    c_a += go([remote(r.ep.at[:, theirs], r.er, r.s_a, 1, head=core)])
    grid_sums(r.gacc, r.dh, r.cotb, r.gtaps, r.gk)
    blocks = r.gk.shape[0] // 8

    def block(b):
        return r.gk.at[pl.ds(8 * b, 8)]

    def on_block_owner(inside, outside):
        pl.when(me < blocks)(inside)
        pl.when(me >= blocks)(outside)

    for b in range(blocks):

        @pl.when(me != b)
        def _():
            remote(block(b), r.gkr.at[me], r.s_k, 0, seq=b).start()

        @pl.when(me == b)
        def _():
            r.gkr[pl.ds(me, 1)] = block(b)[...][None]

    got(c_a[1:2])
    r.es[...] = (r.ep[:, mine].astype(f32) + r.er[...].astype(f32)).astype(bf16)
    c_e = fan(r.erv.at[pl.ds(0, size - 1)], r.s_e, 0, [(r.es.at[marks(i)], r.erv.at[g]) for i in range(1, size)])
    r.erv[pl.ds(g, 1)] = r.es[row][None]
    input_rows(r.wall, r.dp, r.dn)
    c_a += go([remote(r.dn, r.dnr, r.s_a, 2, head=core)])
    weight_grad(3, *weights)
    weight_grad(2, *weights)
    got(c_e)
    total = r.erv[0].astype(f32)
    for d in range(1, size):
        total = total + r.erv[d].astype(f32)
    r.em[...] = total.astype(bf16)
    r.eall[row, mine] = r.em[...]
    c_f = fan(r.eall.at[cube_marks, mine], r.s_f, 0, [(r.em, r.eall.at[row, mine])] * (size - 1))
    send_weights(3)
    send_weights(2)
    for j in range(2):
        weight_grad(j, *weights)
        send_weights(j)
    r.wrv[pl.ds(g, 1), 0] = r.wpart[:, wrow(me)][None]
    r.wrv[pl.ds(g, 1), 1] = r.wpart[:, wrow(partner)][None]

    got(c_f)
    c_a += go([remote(r.eall.at[:, mine], r.eall.at[:, mine], r.s_a, 3, head=core)])
    everything = r.gkr.at[pl.ds(0, n - 1)]

    @pl.when(me < blocks)
    def _():
        remote(everything, everything, r.s_k, 0, seq=partner).wait_recv()
        gsum = r.gkr[0]
        for d in range(1, n):
            gsum = gsum + r.gkr[d]
        r.gkm[...] = gsum
        here = pl.ds(pl.multiple_of(8 * me, 8), 8)
        r.gkall[here, mine] = gsum
        for i in range(1, n):
            remote(r.gkm, r.gkall.at[here, mine], r.s_m, 0, seq=far[i]).start()

    got(c_a[2:4])
    back = norm_back(n, g, count, other, r.xblk, r.dn, r.dnr, r.eall, r.gain, r.small)
    r.lnf[...] = back
    r.lns[...] = (r.lnf[:, mine] + r.dh[other]).astype(bf16)
    c_l = go([remote(r.lns, r.lnr.at[:, mine], r.s_l, 0, seq=partner)])
    got(c_p[1:2])
    r.gxf[half] = r.dhf[...] + norm_back(n, g, count, half, r.xblk, r.dn, r.dnr, r.eall, r.gain, r.small)
    for a in range(2):
        for b in range(4):
            r.smx[4 * a + b:4 * a + b + 1] = r.small[a:a + 1, 128 * b:128 * b + 128]
    c_s = [Many(r.smr.at[pl.ds(0, n - 1)], r.s_s, 0, seq=partner)]
    for i in range(1, n):
        c_s[0].add(r.smx, r.smr.at[me], seq=far[i])
    r.smr[pl.ds(me, 1)] = r.smx[...][None]

    got(c_z)
    grid_forward(n, count, other, r.hid, r.zhalo, r.kc, r.pbias, r.outh, r.zs, r.pad)
    c_l += go([remote(r.outh.at[other], r.outf.at[half, :, mine], r.s_l, 1, seq=partner)])
    grid_forward(n, count, half, r.hid, r.zhalo, r.kc, r.pbias, r.outh, r.zs, r.pad)
    r.outf[half, :, mine] = r.outh[half]
    got(c_l[0:1])
    c_l += go([remote(r.lnr.at[:, mine], r.lnr.at[:, mine], r.s_l, 2, head=core)])
    got(c_y)
    c_u = []
    for k in (1, 0):
        total = r.wrv[0, k].astype(f32)
        for d in range(1, size):
            total = total + r.wrv[d, k].astype(f32)
        if k == 1:
            r.wsum[...] = total.astype(bf16)
            c_u = go([remote(r.wsum, r.wone, r.s_u, 0, seq=partner)])

    def blocks_back(count):
        part = r.gkall.at[pl.ds(0, 8 * count), mine]
        return remote(part, part, r.s_m, 0, seq=partner)

    on_block_owner(blocks_back(blocks - 1).wait_recv, blocks_back(blocks).wait_recv)
    c_l += go([remote(r.gkall.at[:, mine], r.gkall.at[:, mine], r.s_l, 4, head=core)])
    got(c_s)
    acc = r.smr[0]
    for d in range(1, n):
        acc = acc + r.smr[d]
    r.sums[...] = acc
    got(c_l[1:2])
    c_l += go([remote(r.outf.at[:, :, mine], r.outf.at[:, :, mine], r.s_l, 3, head=core)])
    got(c_l[2:3])
    r.gxf[other] = r.lnr[...].astype(f32)
    got(c_u)
    r.gw[...] = total + r.wone[...].astype(f32)
    got(c_l[3:])

    sent(c_t + c_w + c_v + c_n + c_h + c_p + c_x + c_d + c_g + c_q + c_a + c_e + c_f + c_z + c_y + c_l + c_s + c_u)

    @pl.when(is_owner(g))
    def _():
        gave(r.blkb.at[pl.ds(0, 3)], r.s_b)
        gave(r.blkd.at[pl.ds(0, 3)], r.s_c)
        gave(r.resall.at[pl.ds(0, size - 1)], r.s_r)

    @pl.when(jnp.logical_not(is_owner(g)))
    def _():
        gave(r.blkb, r.s_b)
        gave(r.blkd, r.s_c)

    def blocks_left(count):
        part = r.gk.at[pl.ds(0, 8 * count)]
        return remote(part, part, r.s_k, 0, seq=partner)

    on_block_owner(blocks_left(blocks - 1).wait_send, blocks_left(blocks).wait_send)

    @pl.when(me < blocks)
    def _():
        remote(everything, everything, r.s_m, 0, seq=partner).wait_send()


def result_kernel(outf, gxf, gw, sums, gkall, out, gx, gwqkv, gwoutt, ggain, gbias, gtaps, gob, k7o, k5o, k3o, gpb):
    out[...] = outf[...]
    gx[...] = gxf[...]
    gwqkv[...] = gw[0:3]
    gwoutt[...] = gw[3]
    for i in range(4):
        ggain[:, 128 * i:128 * i + 128] = sums[i:i + 1]
        gbias[:, 128 * i:128 * i + 128] = sums[4 + i:5 + i]
    rows = gkall[51:55, my_half()]
    li, lt = iota((256, 33), 0), iota((256, 33), 1)
    spot = jnp.where(((li + lt) & 255) == 16, 1.0, 0.0).astype(bf16)
    parts = [mm(piece.astype(bf16), spot) for piece in split3(rows)]
    gtaps[...] = parts[0] + parts[1] + parts[2]
    gob[...] = gkall[49:50]
    gpb[...] = gkall[50:51]
    spill_kernels(gkall, k7o, k5o, k3o)


def half_of(full, axis):
    return lax.dynamic_slice_in_dim(full, lax.axis_index("head") * 256, 256, axis)


def swap(n, blocks):
    half, _, _ = place(n)
    theirs = lax.ppermute(jnp.where(half == 0, blocks[1], blocks[0]), "seq", [(i, (i + n // 2) % n) for i in range(n)])
    own = jnp.where(half == 0, blocks[0], blocks[1])
    return jnp.where(half == 0, jnp.stack([own, theirs]), jnp.stack([theirs, own]))


def half_sum(n, value):
    half, _, _ = place(n)
    pair = lax.psum(jnp.stack([jnp.where(half == s, value, 0.0) for s in range(2)]), "seq")
    return jnp.where(half == 0, pair[0], pair[1])


def half_max(n, value):
    half, _, _ = place(n)
    pair = lax.pmax(jnp.stack([jnp.where(half == s, value, -jnp.inf) for s in range(2)]), "seq")
    return jnp.where(half == 0, pair[0], pair[1])


def norm_kernel(n, cnt, xblk, gain, bias, normed, xp):
    half, g, _ = place(n)
    for b in range(2):
        normed[b] = norm_rows(xblk[b], gain[...], bias[...])
    xp[...] = segment_sums(n, g, cnt[half], normed)


def back_conv_kernel(n, cnt, cotb, halo, k7, k5, k3, dh, kc, zs, pad):
    half, _, _ = place(n)
    join_taps(kc, k7, k5, k3)
    for b in range(2):
        load_cot(n, b, cotb, *ring_ends(n, place(n)[1], b, halo), zs, pad)
        back_conv(n, cnt[half], b, cotb, zs, kc, dh)


def start_plain(n, counts, tok, cot, gain, bias, wqkv, woutt, k7, k5, k3, scratch):
    half, _, _ = place(n)
    rows = tok.shape[1]
    count = counts[half]
    xblk = swap(n, tok)
    normed, xp = call(
        functools.partial(norm_kernel, n), [sds((2, rows, 512), bf16), sds((MARKS, 256))], [SMEM] + [VMEM] * 3
    )(counts, xblk, gain, bias)
    low, high = edges(count, jnp.arange(MARKS, dtype=jnp.int32))
    xbar = (half_sum(n, xp) / (high - low).astype(f32)[:, None]).astype(bf16)
    xbar = lax.all_gather(xbar, "head", axis=1, tiled=True)
    wts = jnp.concatenate([wqkv, woutt[None]], axis=0)
    wall = lax.all_gather(wts, "seq", axis=1, tiled=True)
    cotb = half_of(swap(n, cot), 2)
    halo = half_ring(n, jnp.stack([cotb[:, :192], cotb[:, -192:]]))
    dh = call(functools.partial(back_conv_kernel, n), sds((2, rows, 256)), [SMEM] + [VMEM] * 5, scratch)(
        counts, cotb, halo, k7, k5, k3
    )
    dhrb = lax.all_gather(dh.astype(bf16), "head", axis=2, tiled=True)
    return xblk, normed, xbar, wall, cotb, halo, dh, dhrb


def half_ring(n, hal):
    size = n // 2
    up = [(i, i // size * size + (i + 1) % size) for i in range(n)]
    return jnp.stack([lax.ppermute(hal[1], "seq", up), lax.ppermute(hal[0], "seq", [(j, i) for i, j in up])])


def three_rows(stat, first):
    return (stat[:, first:first + 1] + stat[:, first + 1:first + 2]) + stat[:, first + 2:first + 3]


def reduce_plain(n, blkb, blkd, halv, hald):
    _, g, _ = place(n)
    stat = blkb[:, 64:].astype(f32)
    top, total = three_rows(stat, 0), three_rows(stat, 3)
    best = half_max(n, top)
    w = jnp.exp(top - best)
    total = half_sum(n, total * w)
    value = half_sum(n, blkb[:, 0:64].astype(f32) * w)
    dct = half_sum(n, blkd.astype(f32)).astype(bf16)
    stat = jnp.concatenate(split3(best) + split3(total) + [jnp.zeros((4, 10, MARKS), f32)], axis=1)
    whole = jnp.concatenate([value, stat], axis=1).astype(bf16)
    h = head_of(g)
    recvb, recvd = lax.dynamic_slice_in_dim(whole, h, 1, 0), lax.dynamic_slice_in_dim(dct, h, 1, 0)
    return recvb, recvd, half_ring(n, halv), half_ring(n, hald)


def spread_plain(n, res):
    _, g, _ = place(n)
    held = ((jnp.arange(4) == head_of(g)) & is_owner(g))[:, None, None]
    return half_sum(n, jnp.where(held, res[None].astype(f32), 0.0)).astype(bf16)


def scores_kernel(n, cnt, normed, xbar, wall, dhrb, qt, kt, vt, qlt, klt, dot, wback, a1, e3, blkb, blkd, halv, hald, wt):
    half, _, _ = place(n)
    count = cnt[half]
    wback[...] = wall[3].T
    project(n, count, normed, wall, wt, qt, kt, vt)
    value_edges(n, count, normed, wall, halv)
    landmarks(xbar, wt, qlt, klt)
    key_scores(n, count, kt, qlt, vt, e3, blkb)
    query_scores(qt, klt, a1)
    out_grads(dhrb, wback, dot, hald)
    partial_dc(dot, a1, blkd)


CHAIN = ("res", "amat", "asp", "pcur", "ps", "ts", "xs", "ys", "ctf", "dctf", "ecur")


def chain_kernel(n, recvb, recvd, qlt, klt, dqz, *refs):
    _, g, _ = place(n)
    here = head_rows(head_of(g))
    dqz[...] = jnp.zeros_like(dqz)
    refs[0][...] = jnp.zeros_like(refs[0])

    @pl.when(is_owner(g))
    def _():
        one = Chain(qlt.at[here], klt.at[here], Refs(("recvb", "recvd") + CHAIN, (recvb, recvd) + refs))
        one.begin()
        for k in range(SWEEPS):
            one.sweep(k)
        one.forward()
        one.backward()
        one.r.ecur[...] = jnp.zeros_like(one.r.ecur)
        for k in range(SWEEPS):
            one.power_grad(SWEEPS - 1 - k)
        dqz[0], dqz[1] = one.finish()


def grads_kernel(n, cnt, normed, xbar, wall, wback, dhrb, qt, kt, vt, qlt, klt, dot, a1, e3, blkb, resall, rhv, rhd, taps,
                 dqz, po, dn, ep, wpart, gtaps, tm, th, hv, hdt, hvr, vr, conv, dconv, gsum, att, dp, dlm):
    half, _, _ = place(n)
    make_bands(taps, normed.shape[1], tm, th)
    value_conv(n, vt, rhv, tm, th, hv, vr, hvr, conv)
    value_conv_back(n, dot, rhd, tm, th, hdt, vr, hvr, dconv, gsum, gtaps)
    attend(resall, a1, conv, att)
    output_rows(att, wback, po)
    score_grads(n, cnt[half], qt, kt, vt, qlt, klt, dot, a1, e3, blkb, resall, dconv, dp, dlm)
    add_chain(head_rows(head_of(place(n)[1])), dlm, dqz)
    mark_rows(wall, dlm, ep)
    input_rows(wall, dp, dn)
    for j in range(4):
        weight_grad(j, normed, xbar, dhrb, att, dp, dlm, wpart)


def hidden_kernel(n, cnt, x, obias, part, hid, z):
    half, _, _ = place(n)
    for b in range(2):
        z[b] = hidden_rows(n, cnt[half], b, x, obias, part[b], hid).astype(bf16)


def final_kernel(n, cnt, hid, halo, cotb, chalo, k7, k5, k3, pbias, xblk, dn, dnr, eall, gain, dh, gtaps,
                 outh, lnb, gk, small, kc, zs, pad, gacc):
    half, g, _ = place(n)
    join_taps(kc, k7, k5, k3)
    gacc[...] = jnp.zeros_like(gacc)
    small[...] = jnp.zeros_like(small)
    for b in range(2):
        grid_forward(n, cnt[half], b, hid, halo, kc, pbias, outh, zs, pad)
        load_cot(n, b, cotb, *ring_ends(n, g, b, chalo), zs, pad)
        pl.loop(0, hid.shape[1] // GRID_W)(lambda i: kernel_grads(n, cnt[half], b, i, hid, zs, gacc))
    grid_sums(gacc, dh, cotb, gtaps, gk)
    for b in range(2):
        lnb[b] = norm_back(n, g, cnt[half], b, xblk, dn, dnr, eall, gain, small)


def late_plain(n, counts, cotb, chalo, xblk, dh, po, ep, dn, wpart, gtaps, gain, obias, pbias, k7, k5, k3, scratch):
    rows = xblk.shape[1]
    part = half_of(lax.psum(po.astype(f32), "head").astype(bf16), 2)
    hid, z = call(functools.partial(hidden_kernel, n), [sds((2, rows, 256)), sds((2, rows, 256), bf16)], [SMEM] + [VMEM] * 3)(
        counts, xblk, obias, part
    )
    halo = half_ring(n, jnp.stack([z[:, :192], z[:, -192:]]))
    dnr = lax.ppermute(dn, "head", [(0, 1), (1, 0)])
    eall = half_sum(n, lax.psum(ep.astype(f32), "head")).astype(bf16)
    outh, lnb, gk, small = call(
        functools.partial(final_kernel, n),
        [sds((2, rows, 256), bf16), sds((2, rows, 512)), sds((56, 256)), sds((8, 512))],
        [SMEM] + [VMEM] * 15,
        scratch + [pltpu.VMEM((49, 8, 256), f32)],
    )(counts, hid, halo, cotb, chalo, k7, k5, k3, pbias, xblk, dn, dnr, eall, gain, dh, gtaps)
    out = swap(n, lax.all_gather(outh, "head", axis=2, tiled=True))
    gx = swap(n, lax.all_gather(dh, "head", axis=2, tiled=True) + lnb)
    gw = lax.psum_scatter(wpart.astype(f32), "seq", scatter_dimension=1, tiled=True)
    gk, small = lax.psum((gk, small), "seq")
    gkall = lax.all_gather(gk, "head", axis=1, tiled=True)
    return out, gx, gw, small[0:2].reshape(8, 128), gkall


def layer_plain(n, counts, tok, cot, gain, bias, wqkv, woutt, taps, obias, pbias, k7, k5, k3):
    rows = tok.shape[1]
    made = layer_buffers(n, rows, wqkv.shape[1])

    def out(*names):
        return [sds(*made[name]) for name in names]

    def tmp(*names):
        return [pltpu.VMEM(*made[name]) for name in names]

    conv_tmp = tmp("kc", "zs", "pad")
    xblk, normed, xbar, wall, cotb, chalo, dh, dhrb = start_plain(
        n, counts, tok, cot, gain, bias, wqkv, woutt, k7, k5, k3, conv_tmp
    )
    qt, kt, vt, qlt, klt, dot, wback, a1, e3, blkb, blkd, halv, hald = call(
        functools.partial(scores_kernel, n),
        out("qt", "kt", "vt", "qlt", "klt", "dot", "wback", "a1", "e3", "blkb", "blkd", "halv", "hald"),
        [SMEM] + [VMEM] * 4,
        tmp("wt"),
    )(counts, normed, xbar, wall, dhrb)
    recvb, recvd, rhv, rhd = reduce_plain(n, blkb, blkd, halv, hald)
    dqz, res = call(
        functools.partial(chain_kernel, n), [sds((2, 64, MARKS)), sds((BLK, MARKS), bf16)], [VMEM] * 4, tmp(*CHAIN[1:])
    )(recvb, recvd, qlt, klt)
    resall = spread_plain(n, res)
    po, dn, ep, wpart, gtaps = call(
        functools.partial(grads_kernel, n),
        out("po", "dn", "ep", "wpart", "gtaps"),
        [SMEM] + [VMEM] * 19,
        tmp("tm", "th", "hv", "hdt", "hvr", "vr", "conv", "dconv", "gsum", "att", "dp", "dlm"),
    )(counts, normed, xbar, wall, wback, dhrb, qt, kt, vt, qlt, klt, dot, a1, e3, blkb, resall, rhv, rhd, taps, dqz)
    return late_plain(
        n, counts, cotb, chalo, xblk, dh, po, ep, dn, wpart, gtaps, gain, obias, pbias, k7, k5, k3, conv_tmp
    )


def shards(n, tokens, counts, ln_gain, ln_bias, w_qkv, conv_taps, w_out, out_bias, kernel7, kernel5, kernel3, ppeg_bias, cotangent):
    rows, wr = tokens.shape[1], w_qkv.shape[1]
    gain, bias, obias, pbias = (v[None, :] for v in (ln_gain, ln_bias, out_bias, ppeg_bias))
    args = (counts, tokens, cotangent, gain, bias, w_qkv, w_out.T, conv_taps, obias, pbias, kernel7, kernel5, kernel3)
    if n == 16:
        results, buffers = layer_results(n, rows, wr), layer_buffers(n, rows, wr)
        names = INPUTS + tuple(results) + tuple(buffers) + tuple(SEMS)
        made = call(
            functools.partial(layer_kernel, n, names),
            [sds(*v) for v in results.values()],
            [SMEM] + [VMEM] * 12,
            [pltpu.VMEM(*v) for v in buffers.values()] + [DMA((2, k)) for k in SEMS.values()],
            cid=0,
            vmem=60,
        )(*args)
    else:
        made = layer_plain(n, *args)
    vec = sds((1, 512))
    out, gx, gwqkv, gwoutt, ggain, gbias, gtaps, gob, k7o, k5o, k3o, gpb = call(
        result_kernel,
        [sds((2, rows, 512), bf16), sds((2, rows, 512)), sds((3, wr, 256)), sds((wr, 256)), vec, vec, sds((4, 33)), vec,
         sds((7, 7, 512)), sds((5, 5, 512)), sds((3, 3, 512)), vec],
        [VMEM] * 5,
    )(*made)
    return out, gx, ggain[0], gbias[0], gwqkv, gtaps, gwoutt.T, gob[0], k7o, k5o, k3o, gpb[0]


def solution(mesh):
    rows, cols = P(None, "seq", None), P(None, "seq", "head")
    return jax.shard_map(
        functools.partial(shards, mesh.shape["seq"]),
        mesh=mesh,
        in_specs=(rows, P(), P(), P(), cols, P("head", None), P("head", "seq"), P(), P(), P(), P(), P(), rows),
        out_specs=(rows, rows, P(), P(), cols, P("head", None), P("head", "seq"), P(), P(), P(), P(), P()),
        check_vma=False,
    )
```

time: 127 us -> 109 us (0.86)
  Pallas kernels: 125 us -> 108 us
    pallas_call x1, Pallas kernels: 122 us -> 105 us  [shards(): call(functools.partial(layer_kernel, n, names), [sds(*v) for v in results...]
where the time goes in v4:
time: 109 us
  Pallas kernels  108 us (99%)
    pallas_call x1, Pallas kernels, shards(): call(functools.partial(layer_kernel, n, names), [sds(*v) for v in results...  105 us
    pallas_call x1, Pallas kernels, shards(): call(result_kernel, [sds((2, rows, 512), bf16), sds((2, rows, 512)), sds(...  2.78 us

profile of v4, /device:TPU:0, one launch (start us, length us, event | category | flops | bytes accessed | tf_op | source)
XLA Modules:
  0.0 108.8 jit_solution(6976015415203448780)
XLA Ops:
  0.6 105.3 %shard_map.220 = (bf16[2,256,512]{2,1,0:T(8,128)(2,1)}, f32[2,256,512]{2,1,0:T(8,128)}, f32[4,32,256]{2,1,0:T(8,128)}, f32[8,128]{1,0:T(8,128)}, f32[56,512]{1,0:T(8,128)}) custom-call(s32[2]{0:T(128)} %refs_0_.1, bf16[2,256,512]{2,1,0:T(8,128)(2,1)} %refs_1_.1, bf16[2,256,512]{2,1,0:T(8,128)(2,1)} %refs_2_.1, f32[1,512]{1,0:T(1,128)} %bitcast.11, ...), custom_call_target="tpu_custom_call" | custom-call | tf_op jit(solution)/shard_map/pallas_call | solution.py:1266
  105.9 2.8 %shard_map.221 = (bf16[2,256,512]{2,1,0:T(8,128)(2,1)}, f32[2,256,512]{2,1,0:T(8,128)}, f32[3,32,256]{2,1,0:T(8,128)}, f32[32,256]{1,0:T(8,128)}, f32[1,512]{1,0...) custom-call(bf16[2,256,512]{2,1,0:T(8,128)(2,1)} %get-tuple-element., ...), custom_call_target="tpu_custom_call" | custom-call | tf_op jit(solution)/shard_map/pallas_call | solution.py:1277

commit v5 on v4

--- a/solution.py
+++ b/solution.py
@@ -17,7 +17,6 @@
 SMEM = pl.BlockSpec(memory_space=pltpu.SMEM)
 DMA = pltpu.SemaphoreType.DMA
 SCALE = 64 ** -0.5
-BLK = 144
 PART = 80
 
 
@@ -100,11 +99,17 @@
     return at + g * rows + jnp.where(at >= rows, (n // 2 - 1) * rows, 0)
 
 
-def norm_rows(x, gain, bias):
-    x = x.astype(f32)
-    xc = x - jnp.mean(x, axis=-1, keepdims=True)
-    inv = lax.rsqrt(jnp.mean(xc * xc, axis=-1, keepdims=True) + EPSILON)
-    return (xc * inv * gain + bias).astype(bf16)
+CHUNK = 64
+
+
+def norm_rows(x, gain, bias, out):
+    @pl.loop(0, x.shape[0] // CHUNK)
+    def _(i):
+        here = pl.ds(pl.multiple_of(i * CHUNK, CHUNK), CHUNK)
+        v = x[here].astype(f32)
+        vc = v - jnp.mean(v, axis=-1, keepdims=True)
+        inv = lax.rsqrt(jnp.mean(vc * vc, axis=-1, keepdims=True) + EPSILON)
+        out[here] = (vc * inv * gain[...] + bias[...]).astype(bf16)
 
 
 def segment_sums(n, g, count, normed):
@@ -126,12 +131,16 @@
 
 def load_grid(zs, pad, body, top, bottom):
     grid = body.shape[0] // GRID_W
-    pad[...] = jnp.zeros_like(pad)
+    side = jnp.zeros((grid + 6, 8, 256), f32)
+    pad[:, 0:8], pad[:, 8 + GRID_W:16 + GRID_W] = side, side
     pad[0:3, 8:8 + GRID_W] = top.reshape(3, GRID_W, 256)
     pad[3:3 + grid, 8:8 + GRID_W] = body.reshape(grid, GRID_W, 256)
     pad[3 + grid:6 + grid, 8:8 + GRID_W] = bottom.reshape(3, GRID_W, 256)
-    for b in range(7):
-        zs[b] = pad[:, 5 + b:5 + b + GRID_W, :]
+
+    @pl.loop(0, grid + 6)
+    def _(i):
+        for b in range(7):
+            zs[b, i] = pad[i, 5 + b:5 + b + GRID_W, :]
 
 
 def conv_row(zs, kc, i, flip):
@@ -214,22 +223,27 @@
     gk[55:56] = jnp.zeros((1, 256), f32)
 
 
-def norm_back(n, g, count, b, x, dn, dnr, eall, gain, small):
+def norm_back(n, g, count, b, x, dn, dnr, eall, gain, small, out):
     rows = x.shape[1]
     low, high = edges(count, iota((MARKS, 512), 0))
     e = (eall[...].astype(f32) / (high - low).astype(f32)).astype(bf16)
     mem = member(count, block_start(n, g, b, rows), rows)
-    total = (dn[b].astype(f32) + dnr[b].astype(f32)) + mm(mem, e, 0, 0)
-    x = x[b].astype(f32)
-    xc = x - jnp.mean(x, axis=-1, keepdims=True)
-    inv = lax.rsqrt(jnp.mean(xc * xc, axis=-1, keepdims=True) + EPSILON)
-    xh = xc * inv
-    dg = total * gain[...]
-    m1 = jnp.mean(dg, axis=-1, keepdims=True)
-    m2 = jnp.mean(dg * xh, axis=-1, keepdims=True)
-    small[0:1] = small[0:1] + jnp.sum(total * xh, axis=0, keepdims=True)
-    small[1:2] = small[1:2] + jnp.sum(total, axis=0, keepdims=True)
-    return (dg - m1 - xh * m2) * inv
+    out[...] = mm(mem, e, 0, 0)
+
+    @pl.loop(0, rows // CHUNK)
+    def _(i):
+        here = pl.ds(pl.multiple_of(i * CHUNK, CHUNK), CHUNK)
+        total = (dn[b, here].astype(f32) + dnr[b, here].astype(f32)) + out[here]
+        v = x[b, here].astype(f32)
+        vc = v - jnp.mean(v, axis=-1, keepdims=True)
+        inv = lax.rsqrt(jnp.mean(vc * vc, axis=-1, keepdims=True) + EPSILON)
+        vh = vc * inv
+        dg = total * gain[...]
+        m1 = jnp.mean(dg, axis=-1, keepdims=True)
+        m2 = jnp.mean(dg * vh, axis=-1, keepdims=True)
+        small[0:1] = small[0:1] + jnp.sum(total * vh, axis=0, keepdims=True)
+        small[1:2] = small[1:2] + jnp.sum(total, axis=0, keepdims=True)
+        out[here] = (dg - m1 - vh * m2) * inv
 
 
 def spill_kernels(gkall, k7o, k5o, k3o):
@@ -241,14 +255,15 @@
         k3o[a] = gkall[7 * a + 16:7 * a + 19]
 
 
-def greet(peers, pair=True):
+def hail(peers):
     sem = pltpu.get_barrier_semaphore()
     for peer in peers:
         pl.semaphore_signal(sem, inc=1, device_id={"seq": peer}, device_id_type=MESH)
-    if pair:
-        hd = lax.axis_index("head")
-        pl.semaphore_signal(sem, inc=1, device_id={"head": 1 - hd}, device_id_type=MESH)
-    pl.semaphore_wait(sem, len(peers) + (1 if pair else 0))
+    pl.semaphore_signal(sem, inc=1, device_id={"head": 1 - lax.axis_index("head")}, device_id_type=MESH)
+
+
+def heard(peers):
+    pl.semaphore_wait(pltpu.get_barrier_semaphore(), len(peers) + 1)
 
 
 def everyone(n):
@@ -283,10 +298,15 @@
         c.wait_send()
 
 
+def matrix(wall, j):
+    n, _, wr, cols = wall.shape
+    return wall[:, j].reshape(n * wr, cols)
+
+
 def project(n, count, normed, wall, wt, qt, kt, vt):
     _, g, _ = place(n)
     for j in range(3):
-        wt[j] = wall[j].T
+        wt[j] = matrix(wall, j).T
     rows = normed.shape[1]
     nr = normed[...].reshape(2 * rows, 512)
     qt[...] = mm(wt[0], nr, 1, 1).astype(bf16)
@@ -301,7 +321,7 @@
     for b in range(2):
         for side, first in ((0, 0), (1, rows - 16)):
             slot = iota((16, 256), 0) + (block_start(n, g, b, rows) + first)
-            v = mm(normed[b, first:first + 16], wall[2])
+            v = mm(normed[b, first:first + 16], matrix(wall, 2))
             halv[side, b] = jnp.where(slot < count, v, 0.0).astype(bf16)
 
 
@@ -314,12 +334,14 @@
     return pl.ds(pl.multiple_of(h * 64, 64), 64)
 
 
-def key_scores(n, count, kt, qlt, vt, e3, blkb, beside=None):
+def key_scores(n, count, kt, qlt, vt, e3, blkb):
     _, g, _ = place(n)
     wide = kt.shape[1]
-    ok = places(n, g, wide // 2, (wide, MARKS), 0) < count
-    for h in range(4):
-        here = slice(64 * h, 64 * h + 64)
+
+    @pl.loop(0, 4, unroll=4)
+    def _(h):
+        here = head_rows(h)
+        ok = places(n, g, wide // 2, (wide, MARKS), 0) < count
         s3 = jnp.where(ok, mm(kt[here] * SCALE, qlt[here], 0, 0), -1e30)
         top = jnp.max(s3, axis=0, keepdims=True)
         e = jnp.where(ok, jnp.exp(s3 - top), 0.0)
@@ -329,18 +351,15 @@
         blkb[h, 0:64] = mm(vt[here], er).astype(bf16)
         stat = jnp.concatenate(split3(top) + split3(total) + [jnp.zeros((10, MARKS), f32)], axis=0)
         blkb[h, 64:80] = stat.astype(bf16)
-        if beside:
-            beside(h)
-
-
-def query_scores(qt, klt, a1, beside=None):
-    for h in range(4):
-        here = slice(64 * h, 64 * h + 64)
+
+
+def query_scores(qt, klt, a1):
+    @pl.loop(0, 4, unroll=4)
+    def _(h):
+        here = head_rows(h)
         s1 = mm(klt[here] * SCALE, qt[here], 0, 0)
         e1 = jnp.exp(s1 - jnp.max(s1, axis=0, keepdims=True))
         a1[h] = (e1 / jnp.sum(e1, axis=0, keepdims=True)).astype(bf16)
-        if beside:
-            beside(h)
 
 
 def out_grads(dhrb, wback, dot, hald):
@@ -390,8 +409,7 @@
         tsp = split(t)
         r.ps[k, 0], r.ps[k, 1] = psp
         r.ts[k, 0], r.ts[k, 1] = tsp
-        if k < SWEEPS - 1:
-            r.pcur[...] = 0.25 * (13.0 * p - 15.0 * t + mm3(tsp, split(7.0 * p - t)))
+        r.pcur[...] = 0.25 * (13.0 * p - 15.0 * t + mm3(tsp, split(7.0 * p - t)))
 
     def powers(self, k):
         r = self.r
@@ -413,15 +431,17 @@
             total = total + three(r.recvb[d, 64:80].astype(f32), 3) * w
             value = value + r.recvb[d, 0:64].astype(f32) * w
         value = value / total
-        x = value
-        for k in range(SWEEPS):
-            r.xs[k] = x
-            x = self.apply(x, k)
-        r.xs[SWEEPS] = x
-        ct = mm3(split(x), (r.asp[0], r.asp[1])) * self.sums()[4]
-        r.res[0:64] = ct.astype(bf16)
+        r.xs[0] = value
+
+        @pl.loop(0, SWEEPS)
+        def _(k):
+            r.xs[k + 1] = self.apply(r.xs[k], k)
+
+        ct = mm3(split(r.xs[SWEEPS]), (r.asp[0], r.asp[1])) * self.sums()[4]
+        r.res[0, 0:64] = ct.astype(bf16)
+        stat = split3(top) + split3(total) + [jnp.zeros((10, MARKS), f32)]
+        r.res[0, 64:80] = jnp.concatenate(stat, axis=0).astype(bf16)
         r.ctf[...] = ct
-        self.top, self.total, self.value = top, total, value
 
     def backward(self):
         r = self.r
@@ -429,20 +449,21 @@
         for d in range(1, r.recvd.shape[0]):
             dct = dct + r.recvd[d].astype(f32)
         r.dctf[...] = dct
-        y = mm3(split(dct), (r.asp[0], r.asp[1]), 1, 1) * self.sums()[4]
-        for k in range(SWEEPS - 1, -1, -1):
-            r.ys[k] = y
-            y = self.apply(y, k)
-        dbr = y.astype(bf16)
-        r.res[64:128] = dbr
-        rt = jnp.sum(dbr.astype(f32) * self.value, axis=0, keepdims=True)
-        stat = split3(self.top) + split3(self.total) + split3(rt) + [jnp.zeros((7, MARKS), f32)]
-        r.res[128:144] = jnp.concatenate(stat, axis=0).astype(bf16)
+        r.ys[SWEEPS] = mm3(split(dct), (r.asp[0], r.asp[1]), 1, 1) * self.sums()[4]
+
+        @pl.loop(0, SWEEPS)
+        def _(i):
+            r.ys[SWEEPS - 1 - i] = self.apply(r.ys[SWEEPS - i], SWEEPS - 1 - i)
+
+        dbr = r.ys[0].astype(bf16)
+        r.res[1, 0:64] = dbr
+        rt = jnp.sum(dbr.astype(f32) * r.xs[0], axis=0, keepdims=True)
+        r.res[1, 64:80] = jnp.concatenate(split3(rt) + [jnp.zeros((13, MARKS), f32)], axis=0).astype(bf16)
 
     def power_grad(self, k):
         r = self.r
         psp, tsp = self.powers(k)
-        outer = mm3(split(r.ys[k]), split(r.xs[k]), 0, 0) * 0.125
+        outer = mm3(split(r.ys[k + 1]), split(r.xs[k]), 0, 0) * 0.125
         d = outer + outer.T
         eq = 0.25 * r.ecur[...]
         pd = mm3(psp, split(d))
@@ -481,7 +502,7 @@
     return jnp.sum(pltpu.roll(g, shift, 1, stride=1, stride_axis=0), axis=0, keepdims=True)
 
 
-def make_bands(taps, rows, tm, th):
+def make_bands(taps, rows, base, tm, th):
     pi, pj = iota((rows, rows), 0), iota((rows, rows), 1)
     inside = (pi - pj <= 16) & (pj - pi <= 16)
     hi, hj = iota((32, rows), 0), iota((32, rows), 1)
@@ -492,11 +513,15 @@
     for f in range(2):
         lines = mm(pieces[0], spots[f]) + mm(pieces[1], spots[f]) + mm(pieces[2], spots[f])
         for h in range(4):
-            line = lines[h:h + 1, :]
-            full = jnp.where(inside, band(line, 0, rows), 0.0)
-            tm[f, h, 0], tm[f, h, 1] = split(full)
-            both = jnp.concatenate([band(line, 240, 16), band(line, 0, 16)], axis=0)
-            th[f, h, 0], th[f, h, 1] = split(jnp.where(far, both, 0.0))
+            base[4 * f + h] = jnp.broadcast_to(lines[h:h + 1, :], (8, 256))
+
+    @pl.loop(0, 8)
+    def _(i):
+        f, h = i // 4, lax.rem(i, 4)
+        line = base[i, 0:1]
+        tm[f, h, 0], tm[f, h, 1] = split(jnp.where(inside, band(line, 0, rows), 0.0))
+        both = jnp.concatenate([band(line, 240, 16), band(line, 0, 16)], axis=0)
+        th[f, h, 0], th[f, h, 1] = split(jnp.where(far, both, 0.0))
 
 
 def value_conv(n, vt, recvv, tm, th, hv, vr, hvr, conv):
@@ -551,7 +576,7 @@
     @pl.loop(0, 4, unroll=4)
     def _(h):
         here = head_rows(h)
-        att[here] = (mm(res[h, 0:64], a1[h]) + conv[here]).astype(bf16)
+        att[here] = (mm(res[0, h, 0:64], a1[h]) + conv[here]).astype(bf16)
 
 
 def score_grads(n, count, qt, kt, vt, qlt, klt, dot, a1, e3, blkb, res, dconv, dp, dlm):
@@ -562,11 +587,11 @@
     @pl.loop(0, 4, unroll=4)
     def _(h):
         here = head_rows(h)
-        ct, dbt = res[h, 0:64], res[h, 64:128]
-        stat = res[h, 128:144].astype(f32)
+        ct, dbt = res[0, h, 0:64], res[1, h, 0:64]
+        stat = res[0, h, 64:80].astype(f32)
         own = three(blkb[h, 64:80].astype(f32), 0)
         factor = jnp.exp(own - three(stat, 0)) / three(stat, 3)
-        rt = three(stat, 6)
+        rt = three(res[1, h, 64:80].astype(f32), 0)
         do, v = dot[here], vt[here]
         a = a1[h].astype(f32)
         da = mm(ct, do, 0, 0)
@@ -582,12 +607,12 @@
 
 
 def mark_rows(wall, dlm, ep):
-    ep[...] = (mm(wall[0], dlm[0]) + mm(wall[1], dlm[1])).T.astype(bf16)
+    ep[...] = (mm(matrix(wall, 0), dlm[0]) + mm(matrix(wall, 1), dlm[1])).T.astype(bf16)
 
 
 def input_rows(wall, dp, dn):
     rows = dn.shape[1]
-    d = mm(wall[0], dp[0]) + mm(wall[1], dp[1]) + mm(wall[2], dp[2])
+    d = mm(matrix(wall, 0), dp[0]) + mm(matrix(wall, 1), dp[1]) + mm(matrix(wall, 2), dp[2])
     dn[...] = d.T.astype(bf16).reshape(2, rows, 512)
 
 
@@ -604,7 +629,12 @@
         grad = mm(dp[j], normed[...].reshape(2 * rows, 512))
         if j < 2:
             grad = grad + mm(dlm[j], xbar[...])
-    wpart[j] = grad.T.astype(bf16)
+    low = grad.T.astype(bf16)
+    size, _, _, wr, _ = wpart.shape
+    for half in range(2):
+        for g in range(size):
+            first = (half * size + g) * wr
+            wpart[g, half, j] = low[first:first + wr]
 
 
 class Refs:
@@ -627,9 +657,9 @@
     mb, wide, grid = MARKS // size, 2 * rows, rows // GRID_W
     half2 = (2, rows, 256)
     return dict(
-        wts=((4, wr, 256), bf16), wall=((4, 512, 256), bf16), wback=((256, 512), bf16), wt=((3, 256, 512), bf16),
+        wts=((4, wr, 256), bf16), wall=((n, 4, wr, 256), bf16), wback=((256, 512), bf16), wt=((3, 256, 512), bf16),
         xblk=((2, rows, 512), bf16), normed=((2, rows, 512), bf16), xbar=((MARKS, 512), bf16),
-        xp=((MARKS, 256), bf16), xr=((size, mb, 256), bf16), xm=((mb, 256), bf16),
+        nown=((2, rows, 512), bf16), xp=((2, MARKS, 256), bf16), xr=((n, mb, 256), bf16), xm=((mb, 256), bf16),
         halo=((2, 2, 192, 256), bf16), dh=(half2, f32), dhrb=((2, rows, 512), bf16),
         kc=((7, 8, 256), f32), zs=((7, grid + 6, GRID_W, 256), f32), zc=((2, 7, grid + 6, GRID_W, 256), f32), pad=((grid + 6, GRID_W + 16, 256), f32),
         qt=((256, wide), bf16), kt=((256, wide), bf16), vt=((256, wide), bf16), dot=((256, wide), bf16),
@@ -637,14 +667,14 @@
         blkb=((4, PART, MARKS), bf16), blkd=((4, 64, MARKS), bf16),
         recvb=((size, PART, MARKS), bf16), recvd=((size, 64, MARKS), bf16),
         halv=((2, 2, 16, 256), bf16), hald=((2, 2, 16, 256), bf16), rhv=((2, 2, 16, 256), bf16), rhd=((2, 2, 16, 256), bf16),
-        ps=((SWEEPS, 2, 256, 256), bf16), ts=((SWEEPS, 2, 256, 256), bf16), xs=((SWEEPS + 1, 64, 256), f32), ys=((SWEEPS, 64, 256), f32), ctf=((64, 256), f32), dctf=((64, 256), f32),
+        ps=((SWEEPS, 2, 256, 256), bf16), ts=((SWEEPS, 2, 256, 256), bf16), xs=((SWEEPS + 1, 64, 256), f32), ys=((SWEEPS + 1, 64, 256), f32), ctf=((64, 256), f32), dctf=((64, 256), f32),
         amat=((256, 256), f32), asp=((2, 256, 256), bf16), pcur=((256, 256), f32), ecur=((256, 256), f32),
-        res=((BLK, MARKS), bf16), resall=((8, BLK, MARKS), bf16),
+        res=((2, PART, MARKS), bf16), resall=((2, 8, PART, MARKS), bf16),
         tm=((2, 4, 2, rows, rows), bf16), th=((2, 4, 2, 32, rows), bf16), hv=((2, 256, 32), bf16), hdt=((2, 256, 32), bf16),
         hvr=((2, 256, 32), bf16), vr=((2, 256, rows), bf16), conv=((256, wide), f32), dconv=((256, wide), f32),
-        gsum=((4, 8, 256), f32), gtaps=((8, 256), f32), att=((256, wide), bf16), dp=((3, 256, wide), bf16),
+        base=((8, 8, 256), f32), gsum=((4, 8, 256), f32), gtaps=((8, 256), f32), att=((256, wide), bf16), dp=((3, 256, wide), bf16),
         dlm=((2, 256, MARKS), bf16), po=((2, rows, 512), bf16), dn=((2, rows, 512), bf16), ep=((MARKS, 512), bf16),
-        wpart=((4, 512, 256), bf16), er=((MARKS, 256), bf16), es=((MARKS, 256), bf16), erv=((size, mb, 256), bf16),
+        wpart=((size, 2, 4, wr, 256), bf16), er=((MARKS, 256), bf16), es=((MARKS, 256), bf16), erv=((size, mb, 256), bf16),
         em=((mb, 256), bf16), eall=((MARKS, 512), bf16), por=(half2, bf16),
         dnr=((2, rows, 512), bf16), hid=(half2, f32), z=(half2, bf16), cotb=(half2, bf16), lnf=((rows, 512), f32), dhf=((rows, 512), f32), zhalo=((2, 2, 192, 256), bf16),
         lnr=((rows, 512), bf16), lns=((rows, 256), bf16), wrv=((size, 2, 4, wr, 256), bf16), wsum=((4, wr, 256), bf16),
@@ -654,7 +684,7 @@
 
 
 SEMS = dict(
-    s_w=2, s_v=2, s_n=2, s_t=1, s_h=4, s_x=1, s_g=1, s_p=4, s_d=1, s_b=1, s_c=1, s_r=1, s_q=4, s_a=4, s_e=1, s_f=1, s_z=2, s_l=5,
+    s_w=2, s_v=4, s_t=1, s_h=4, s_x=1, s_g=1, s_p=4, s_d=1, s_b=1, s_c=1, s_r=2, s_q=4, s_a=4, s_e=1, s_f=1, s_z=2, s_l=5,
     s_y=1, s_u=1, s_k=1, s_m=1, s_s=1,
 )
 
@@ -688,13 +718,9 @@
     near, far = cube(n), everyone(n)
     core = 1 - hd
 
-    def wrow(device):
-        return pl.ds(pl.multiple_of(device * wr, wr), wr)
-
     def marks(i):
         return pl.ds(pl.multiple_of(lax.rem(g + i, size) * mb, mb), mb)
 
-    cube_rows = pl.ds(0, (size - 1) * wr)
     cube_marks = pl.ds(0, (size - 1) * mb)
 
     def fan(total, sems, i, pieces):
@@ -703,52 +729,94 @@
             group.add(src, dst, seq=near[j])
         return [group]
 
+    hail(far[1:])
     r.wts[0:3] = r.wqkv[...]
     r.wts[3] = r.woutt[...]
-    greet(far[1:])
-    qkv = slice(0, 3)
-    c_w = go([remote(r.wts.at[qkv], r.wall.at[qkv, wrow(me)], r.s_w, 0, seq=partner)])
+    for k in range(2):
+        norm_rows(r.tok.at[k], r.gain, r.bias, r.nown.at[k])
+        mem = member(r.cnt[k], me * rows, rows)
+        r.xp[k] = mm(mem, r.nown[k, :, mine]).astype(bf16)
+    heard(far[1:])
+    c_x = [Many(r.xr.at[pl.ds(0, n - 1)], r.s_x, 0, seq=partner)]
+    for i in range(1, n):
+        at = pl.ds(pl.multiple_of(lax.rem(far[i], size) * mb, mb), mb)
+        c_x[0].add(r.xp.at[far[i] // size, at], r.xr.at[me], seq=far[i])
+    row = marks(0)
+    r.xr[pl.ds(me, 1)] = r.xp[half, row][None]
+    first3 = pl.ds(0, 3)
+    others = r.wall.at[pl.ds(0, size - 1), first3]
+    others_out = r.wall.at[pl.ds(0, size - 1), 3]
+    c_w = go([remote(r.wts.at[first3], r.wall.at[me, first3], r.s_w, 0, seq=partner)])
     c_t = go([remote(r.tok.at[other, :, mine], r.xblk.at[half, :, mine], r.s_t, 0, seq=partner)])
-    c_v = fan(r.wall.at[qkv, cube_rows], r.s_v, 0, [(r.wts.at[qkv], r.wall.at[qkv, wrow(me)])] * (size - 1))
+    c_v = fan(others, r.s_v, 0, [(r.wts.at[first3], r.wall.at[me, first3])] * (size - 1))
     up, down = far[1], far[n - 1]
     first, final = pl.ds(0, 192), pl.ds(rows - 192, 192)
     c_h = go([
         remote(r.cot.at[up // size, final, mine], r.halo.at[0, up // size], r.s_h, 0, seq=up),
         remote(r.cot.at[down // size, first, mine], r.halo.at[1, down // size], r.s_h, 1, seq=down),
     ])
-    r.wall[:, wrow(me)] = r.wts[...]
+    r.wall[pl.ds(me, 1)] = r.wts[...][None]
     r.cotb[half] = r.cot[half, :, mine]
     r.xblk[half] = r.tok[half]
-    r.normed[half] = norm_rows(r.tok[half], r.gain[...], r.bias[...])
+    r.normed[half] = r.nown[half]
     join_taps(r.kc, r.k7, r.k5, r.k3)
     got(c_w)
-    pair_rows = (r.wall.at[qkv, wrow(partner)],) * 2
-    c_v += fan(r.wall.at[qkv, cube_rows], r.s_v, 1, [pair_rows] * (size - 1))
-    make_bands(r.taps, rows, r.tm, r.th)
-
+    c_v += fan(others, r.s_v, 1, [(r.wall.at[partner, first3],) * 2] * (size - 1))
+    make_bands(r.taps, rows, r.base, r.tm, r.th)
+
+    got(c_x)
+    total = r.xr[0].astype(f32)
+    for d in range(1, n):
+        total = total + r.xr[d].astype(f32)
+    low, high = edges(count, iota((mb, 256), 0) + g * mb)
+    r.xm[...] = (total / (high - low).astype(f32)).astype(bf16)
+    r.xbar[row, mine] = r.xm[...]
+    c_g = fan(r.xbar.at[cube_marks, mine], r.s_g, 0, [(r.xm, r.xbar.at[row, mine])] * (size - 1))
     got(c_t)
     c_p = go([remote(r.xblk.at[other, :, mine], r.xblk.at[other, :, mine], r.s_p, 0, head=core)])
     c_d = go([remote(r.cot.at[other, :, mine], r.cotb.at[half], r.s_d, 0, seq=partner)])
-    got(c_p)
-    r.normed[other] = norm_rows(r.xblk[other], r.gain[...], r.bias[...])
-    r.xp[...] = segment_sums(n, g, count, r.normed).astype(bf16)
-    c_x = fan(r.xr.at[pl.ds(0, size - 1)], r.s_x, 0, [(r.xp.at[marks(i)], r.xr.at[g]) for i in range(1, size)])
-    row = marks(0)
-    r.xr[pl.ds(g, 1)] = r.xp[row][None]
-    c_w += go([remote(r.wts.at[3], r.wall.at[3, wrow(me)], r.s_w, 1, seq=partner)])
+    c_w += go([remote(r.wts.at[3], r.wall.at[me, 3], r.s_w, 1, seq=partner)])
     got(c_h)
     load_cot(n, half, r.cotb, r.halo[0, half], r.halo[1, half], r.zc.at[half], r.pad)
     back_conv(n, count, half, r.cotb, r.zc.at[half], r.kc, r.dh)
     c_p += go([remote(r.dh.at[half], r.dhf.at[:, mine], r.s_p, 2, head=core)])
     r.dhf[:, mine] = r.dh[half]
-    got(c_x)
-    total = r.xr[0].astype(f32)
-    for d in range(1, size):
-        total = total + r.xr[d].astype(f32)
-    low, high = edges(count, iota((mb, 256), 0) + g * mb)
-    r.xm[...] = (total / (high - low).astype(f32)).astype(bf16)
-    r.xbar[row, mine] = r.xm[...]
-    c_g = fan(r.xbar.at[cube_marks, mine], r.s_g, 0, [(r.xm, r.xbar.at[row, mine])] * (size - 1))
+    got(c_g)
+    c_p += go([remote(r.xbar.at[:, mine], r.xbar.at[:, mine], r.s_p, 1, head=core)])
+    got(c_p[0:1])
+    norm_rows(r.xblk.at[other], r.gain, r.bias, r.normed.at[other])
+    got(c_v[0:2])
+    project(n, count, r.normed, r.wall, r.wt, r.qt, r.kt, r.vt)
+    got(c_w[1:])
+    c_v += fan(others_out, r.s_v, 2, [(r.wts.at[3], r.wall.at[me, 3])] * (size - 1))
+    c_v += fan(others_out, r.s_v, 3, [(r.wall.at[partner, 3],) * 2] * (size - 1))
+    value_edges(n, count, r.normed, r.wall, r.halv)
+    c_q = go([
+        remote(r.halv.at[1], r.rhv.at[0], r.s_q, 0, seq=near[1]),
+        remote(r.halv.at[0], r.rhv.at[1], r.s_q, 1, seq=near[size - 1]),
+    ])
+
+    got(c_p[2:3])
+    landmarks(r.xbar, r.wt, r.qlt, r.klt)
+    here = head_rows(head_of(g))
+    one = Chain(r.qlt.at[here], r.klt.at[here], r)
+    key_scores(n, count, r.kt, r.qlt, r.vt, r.e3, r.blkb)
+
+    def give(blk, recv, sems):
+        for h, o in enumerate(OWNERS):
+
+            @pl.when(g != o)
+            def _():
+                remote(blk.at[h], recv.at[g], sems, 0, seq=half * size + o).start()
+
+            @pl.when(g == o)
+            def _():
+                recv[pl.ds(g, 1)] = blk[h:h + 1]
+
+    def gave(blk, sems):
+        remote(blk, blk, sems, 0, seq=near[1]).wait_send()
+
+    give(r.blkb, r.recvb, r.s_b)
     got(c_d)
     above = jnp.where((g == size - 1) & (half == 0), half, other)
     below = jnp.where((g == 0) & (half == 1), half, other)
@@ -756,50 +824,49 @@
         remote(r.cotb.at[above, final], r.halo.at[0, other], r.s_h, 2, seq=near[1]),
         remote(r.cotb.at[below, first], r.halo.at[1, other], r.s_h, 3, seq=near[size - 1]),
     ])
-    got(c_v)
-    project(n, count, r.normed, r.wall, r.wt, r.qt, r.kt, r.vt)
-    c_n = fan(r.wall.at[3, cube_rows], r.s_n, 0, [(r.wts.at[3], r.wall.at[3, wrow(me)])] * (size - 1))
-    got(c_w[1:])
-    pair_row = (r.wall.at[3, wrow(partner)],) * 2
-    c_n += fan(r.wall.at[3, cube_rows], r.s_n, 1, [pair_row] * (size - 1))
-    got(c_g)
-    c_p += go([remote(r.xbar.at[:, mine], r.xbar.at[:, mine], r.s_p, 1, head=core)])
-    value_edges(n, count, r.normed, r.wall, r.halv)
-    c_q = go([
-        remote(r.halv.at[1], r.rhv.at[0], r.s_q, 0, seq=near[1]),
-        remote(r.halv.at[0], r.rhv.at[1], r.s_q, 1, seq=near[size - 1]),
-    ])
+    one.begin()
+    pl.loop(0, SWEEPS, unroll=SWEEPS)(one.sweep)
+
+    def spread(k):
+        for h, o in enumerate(OWNERS):
+
+            @pl.when(g == o)
+            def _():
+                for i in range(1, size):
+                    remote(r.res.at[k], r.resall.at[k, h], r.s_r, k, seq=near[i]).start()
+                r.resall[k, h] = r.res[k]
+
+    def results(k):
+        def arrive(count):
+            part = r.resall.at[k, pl.ds(0, count)]
+            remote(part, part, r.s_r, k, seq=near[1]).wait_recv()
+
+        @pl.when(is_owner(g))
+        def _():
+            arrive(3)
+
+        @pl.when(jnp.logical_not(is_owner(g)))
+        def _():
+            arrive(4)
+
+    def wait_for(recv, sems):
+        part = recv.at[pl.ds(0, size - 1)]
+        remote(part, part, sems, 0, seq=near[1]).wait_recv()
+
+    @pl.when(is_owner(g))
+    def _():
+        wait_for(r.recvb, r.s_b)
+        one.forward()
+        spread(0)
+
     got(c_h[2:])
     load_cot(n, other, r.cotb, r.halo[0, other], r.halo[1, other], r.zc.at[other], r.pad)
     back_conv(n, count, other, r.cotb, r.zc.at[other], r.kc, r.dh)
     r.dhrb[:, :, mine] = r.dh[...].astype(bf16)
     c_p += go([remote(r.dhrb.at[:, :, mine], r.dhrb.at[:, :, mine], r.s_p, 3, head=core)])
-
-    got(c_p[2:3])
-    landmarks(r.xbar, r.wt, r.qlt, r.klt)
-    here = head_rows(head_of(g))
-    one = Chain(r.qlt.at[here], r.klt.at[here], r)
-    one.begin()
-    key_scores(n, count, r.kt, r.qlt, r.vt, r.e3, r.blkb, one.sweep)
-
-    def give(blk, recv, sems):
-        for h, o in enumerate(OWNERS):
-
-            @pl.when(g != o)
-            def _():
-                remote(blk.at[h], recv.at[g], sems, 0, seq=half * size + o).start()
-
-            @pl.when(g == o)
-            def _():
-                recv[pl.ds(g, 1)] = blk[h:h + 1]
-
-    def gave(blk, sems):
-        remote(blk, blk, sems, 0, seq=near[1]).wait_send()
-
-    give(r.blkb, r.recvb, r.s_b)
-    query_scores(r.qt, r.klt, r.a1, lambda h: one.sweep(4 + h) if h < 2 else None)
-    got(c_n)
-    r.wback[...] = r.wall[3].T
+    query_scores(r.qt, r.klt, r.a1)
+    got(c_v[2:4])
+    r.wback[...] = matrix(r.wall, 3).T
     got(c_p[3:4])
     out_grads(r.dhrb, r.wback, r.dot, r.hald)
     c_q += go([
@@ -809,52 +876,22 @@
     partial_dc(r.dot, r.a1, r.blkd)
     give(r.blkd, r.recvd, r.s_c)
 
+    got(c_q)
+    value_conv(n, r.vt, r.rhv, r.tm, r.th, r.hv, r.vr, r.hvr, r.conv)
+    results(0)
+    attend(r.resall, r.a1, r.conv, r.att)
+    output_rows(r.att, r.wback, r.po)
+    c_a = go([remote(r.po.at[:, :, theirs], r.por, r.s_a, 0, head=core)])
+
     @pl.when(is_owner(g))
     def _():
-        def wait_for(recv, sems):
-            remote(recv.at[pl.ds(0, size - 1)], recv.at[pl.ds(0, size - 1)], sems, 0, seq=near[1]).wait_recv()
-
-        wait_for(r.recvb, r.s_b)
-        one.forward()
         wait_for(r.recvd, r.s_c)
         one.backward()
-        for h, o in enumerate(OWNERS):
-
-            @pl.when(g == o)
-            def _():
-                for i in range(1, size):
-                    remote(r.res, r.resall.at[h], r.s_r, 0, seq=near[i]).start()
-                r.resall[h] = r.res[...]
-
-    got(c_q)
-    value_conv(n, r.vt, r.rhv, r.tm, r.th, r.hv, r.vr, r.hvr, r.conv)
+        spread(1)
+
     value_conv_back(n, r.dot, r.rhd, r.tm, r.th, r.hdt, r.vr, r.hvr, r.dconv, r.gsum, r.gtaps)
     r.small[...] = jnp.zeros_like(r.small)
     r.gacc[...] = jnp.zeros_like(r.gacc)
-
-    def results(count):
-        return remote(r.resall.at[pl.ds(0, count)], r.resall.at[pl.ds(0, count)], r.s_r, 0, seq=near[1])
-
-    @pl.when(is_owner(g))
-    def _():
-        results(3).wait_recv()
-
-    @pl.when(jnp.logical_not(is_owner(g)))
-    def _():
-        results(4).wait_recv()
-
-    attend(r.resall, r.a1, r.conv, r.att)
-    output_rows(r.att, r.wback, r.po)
-    c_a = go([remote(r.po.at[:, :, theirs], r.por, r.s_a, 0, head=core)])
-    weights = (r.normed, r.xbar, r.dhrb, r.att, r.dp, r.dlm, r.wpart)
-    c_y = [Many(r.wrv.at[pl.ds(0, size - 1)], r.s_y, 0, seq=near[1])]
-
-    def send_weights(j):
-        for i in range(1, size):
-            for k, device in enumerate((near[i], lax.rem(near[i] + size, n))):
-                c_y[0].add(r.wpart.at[j, wrow(device)], r.wrv.at[g, k, j], seq=near[i])
-
-    score_grads(n, count, r.qt, r.kt, r.vt, r.qlt, r.klt, r.dot, r.a1, r.e3, r.blkb, r.resall, r.dconv, r.dp, r.dlm)
     got(c_a[0:1])
     for b in range(2):
         part = r.po[b, :, mine].astype(f32) + r.por[b].astype(f32)
@@ -863,47 +900,53 @@
         remote(r.z.at[:, final], r.zhalo.at[0], r.s_z, 0, seq=near[1]),
         remote(r.z.at[:, first], r.zhalo.at[1], r.s_z, 1, seq=near[size - 1]),
     ])
-    r.ecur[...] = jnp.zeros_like(r.ecur)
-    lines = rows // GRID_W
-
-    @pl.loop(0, 2 * lines)
-    def _(i):
-        kernel_grads(n, count, i // lines, lax.rem(i, lines), r.hid, r.zc.at[i // lines], r.gacc)
-
-        @pl.when(i < SWEEPS)
-        def _():
-            one.power_grad(jnp.maximum(SWEEPS - 1 - i, 0))
-
+
+    @pl.when(is_owner(g))
+    def _():
+        r.ecur[...] = jnp.zeros_like(r.ecur)
+        pl.loop(0, SWEEPS, unroll=SWEEPS)(lambda i: one.power_grad(SWEEPS - 1 - i))
+
+    results(1)
+    weights = (r.normed, r.xbar, r.dhrb, r.att, r.dp, r.dlm, r.wpart)
+    c_y = [Many(r.wrv.at[pl.ds(0, size - 1)], r.s_y, 0, seq=near[1])]
+
+    score_grads(n, count, r.qt, r.kt, r.vt, r.qlt, r.klt, r.dot, r.a1, r.e3, r.blkb, r.resall, r.dconv, r.dp, r.dlm)
     @pl.when(is_owner(g))
     def _():
         add_chain(here, r.dlm, one.finish())
 
     mark_rows(r.wall, r.dlm, r.ep)
     c_a += go([remote(r.ep.at[:, theirs], r.er, r.s_a, 1, head=core)])
-    grid_sums(r.gacc, r.dh, r.cotb, r.gtaps, r.gk)
-    blocks = r.gk.shape[0] // 8
-
-    def block(b):
-        return r.gk.at[pl.ds(8 * b, 8)]
-
-    def on_block_owner(inside, outside):
-        pl.when(me < blocks)(inside)
-        pl.when(me >= blocks)(outside)
-
-    for b in range(blocks):
-
-        @pl.when(me != b)
-        def _():
-            remote(block(b), r.gkr.at[me], r.s_k, 0, seq=b).start()
-
-        @pl.when(me == b)
-        def _():
-            r.gkr[pl.ds(me, 1)] = block(b)[...][None]
-
     got(c_a[1:2])
     r.es[...] = (r.ep[:, mine].astype(f32) + r.er[...].astype(f32)).astype(bf16)
     c_e = fan(r.erv.at[pl.ds(0, size - 1)], r.s_e, 0, [(r.es.at[marks(i)], r.erv.at[g]) for i in range(1, size)])
     r.erv[pl.ds(g, 1)] = r.es[row][None]
+    lines = rows // GRID_W
+
+    @pl.loop(0, 2 * lines)
+    def _(i):
+        kernel_grads(n, count, i // lines, lax.rem(i, lines), r.hid, r.zc.at[i // lines], r.gacc)
+
+    grid_sums(r.gacc, r.dh, r.cotb, r.gtaps, r.gk)
+    blocks = r.gk.shape[0] // 8
+
+    def block(b):
+        return r.gk.at[pl.ds(8 * b, 8)]
+
+    def on_block_owner(inside, outside):
+        pl.when(me < blocks)(inside)
+        pl.when(me >= blocks)(outside)
+
+    for b in range(blocks):
+
+        @pl.when(me != b)
+        def _():
+            remote(block(b), r.gkr.at[me], r.s_k, 0, seq=b).start()
+
+        @pl.when(me == b)
+        def _():
+            r.gkr[pl.ds(me, 1)] = block(b)[...][None]
+
     input_rows(r.wall, r.dp, r.dn)
     c_a += go([remote(r.dn, r.dnr, r.s_a, 2, head=core)])
     weight_grad(3, *weights)
@@ -915,13 +958,16 @@
     r.em[...] = total.astype(bf16)
     r.eall[row, mine] = r.em[...]
     c_f = fan(r.eall.at[cube_marks, mine], r.s_f, 0, [(r.em, r.eall.at[row, mine])] * (size - 1))
+    def send_weights(j):
+        for i in range(1, size):
+            c_y[0].add(r.wpart.at[lax.rem(g + i, size), :, j], r.wrv.at[g, :, j], seq=near[i])
+
     send_weights(3)
     send_weights(2)
     for j in range(2):
         weight_grad(j, *weights)
         send_weights(j)
-    r.wrv[pl.ds(g, 1), 0] = r.wpart[:, wrow(me)][None]
-    r.wrv[pl.ds(g, 1), 1] = r.wpart[:, wrow(partner)][None]
+    r.wrv[pl.ds(g, 1)] = r.wpart[pl.ds(g, 1)]
 
     got(c_f)
     c_a += go([remote(r.eall.at[:, mine], r.eall.at[:, mine], r.s_a, 3, head=core)])
@@ -940,12 +986,12 @@
             remote(r.gkm, r.gkall.at[here, mine], r.s_m, 0, seq=far[i]).start()
 
     got(c_a[2:4])
-    back = norm_back(n, g, count, other, r.xblk, r.dn, r.dnr, r.eall, r.gain, r.small)
-    r.lnf[...] = back
+    norm_back(n, g, count, other, r.xblk, r.dn, r.dnr, r.eall, r.gain, r.small, r.lnf)
     r.lns[...] = (r.lnf[:, mine] + r.dh[other]).astype(bf16)
     c_l = go([remote(r.lns, r.lnr.at[:, mine], r.s_l, 0, seq=partner)])
     got(c_p[1:2])
-    r.gxf[half] = r.dhf[...] + norm_back(n, g, count, half, r.xblk, r.dn, r.dnr, r.eall, r.gain, r.small)
+    norm_back(n, g, count, half, r.xblk, r.dn, r.dnr, r.eall, r.gain, r.small, r.lnf)
+    r.gxf[half] = r.dhf[...] + r.lnf[...]
     for a in range(2):
         for b in range(4):
             r.smx[4 * a + b:4 * a + b + 1] = r.small[a:a + 1, 128 * b:128 * b + 128]
@@ -963,11 +1009,11 @@
     c_l += go([remote(r.lnr.at[:, mine], r.lnr.at[:, mine], r.s_l, 2, head=core)])
     got(c_y)
     c_u = []
-    for k in (1, 0):
+    for k in (other, half):
         total = r.wrv[0, k].astype(f32)
         for d in range(1, size):
             total = total + r.wrv[d, k].astype(f32)
-        if k == 1:
+        if k is other:
             r.wsum[...] = total.astype(bf16)
             c_u = go([remote(r.wsum, r.wone, r.s_u, 0, seq=partner)])
 
@@ -990,13 +1036,15 @@
     r.gw[...] = total + r.wone[...].astype(f32)
     got(c_l[3:])
 
-    sent(c_t + c_w + c_v + c_n + c_h + c_p + c_x + c_d + c_g + c_q + c_a + c_e + c_f + c_z + c_y + c_l + c_s + c_u)
+    sent(c_t + c_w + c_v + c_h + c_p + c_x + c_d + c_g + c_q + c_a + c_e + c_f + c_z + c_y + c_l + c_s + c_u)
 
     @pl.when(is_owner(g))
     def _():
         gave(r.blkb.at[pl.ds(0, 3)], r.s_b)
         gave(r.blkd.at[pl.ds(0, 3)], r.s_c)
-        gave(r.resall.at[pl.ds(0, size - 1)], r.s_r)
+        for k in range(2):
+            part = r.resall.at[k, pl.ds(0, size - 1)]
+            remote(part, part, r.s_r, k, seq=near[1]).wait_send()
 
     @pl.when(jnp.logical_not(is_owner(g)))
     def _():
@@ -1058,7 +1106,7 @@
 def norm_kernel(n, cnt, xblk, gain, bias, normed, xp):
     half, g, _ = place(n)
     for b in range(2):
-        normed[b] = norm_rows(xblk[b], gain[...], bias[...])
+        norm_rows(xblk.at[b], gain, bias, normed.at[b])
     xp[...] = segment_sums(n, g, cnt[half], normed)
 
 
@@ -1082,7 +1130,7 @@
     xbar = (half_sum(n, xp) / (high - low).astype(f32)[:, None]).astype(bf16)
     xbar = lax.all_gather(xbar, "head", axis=1, tiled=True)
     wts = jnp.concatenate([wqkv, woutt[None]], axis=0)
-    wall = lax.all_gather(wts, "seq", axis=1, tiled=True)
+    wall = lax.all_gather(wts, "seq", axis=1, tiled=True).reshape(4, 16, 32, 256).swapaxes(0, 1)
     cotb = half_of(swap(n, cot), 2)
     halo = half_ring(n, jnp.stack([cotb[:, :192], cotb[:, -192:]]))
     dh = call(functools.partial(back_conv_kernel, n), sds((2, rows, 256)), [SMEM] + [VMEM] * 5, scratch)(
@@ -1120,14 +1168,14 @@
 
 def spread_plain(n, res):
     _, g, _ = place(n)
-    held = ((jnp.arange(4) == head_of(g)) & is_owner(g))[:, None, None]
-    return half_sum(n, jnp.where(held, res[None].astype(f32), 0.0)).astype(bf16)
+    held = ((jnp.arange(4) == head_of(g)) & is_owner(g))[None, :, None, None]
+    return half_sum(n, jnp.where(held, res[:, None].astype(f32), 0.0)).astype(bf16)
 
 
 def scores_kernel(n, cnt, normed, xbar, wall, dhrb, qt, kt, vt, qlt, klt, dot, wback, a1, e3, blkb, blkd, halv, hald, wt):
     half, _, _ = place(n)
     count = cnt[half]
-    wback[...] = wall[3].T
+    wback[...] = matrix(wall, 3).T
     project(n, count, normed, wall, wt, qt, kt, vt)
     value_edges(n, count, normed, wall, halv)
     landmarks(xbar, wt, qlt, klt)
@@ -1150,20 +1198,18 @@
     def _():
         one = Chain(qlt.at[here], klt.at[here], Refs(("recvb", "recvd") + CHAIN, (recvb, recvd) + refs))
         one.begin()
-        for k in range(SWEEPS):
-            one.sweep(k)
+        pl.loop(0, SWEEPS)(one.sweep)
         one.forward()
         one.backward()
         one.r.ecur[...] = jnp.zeros_like(one.r.ecur)
-        for k in range(SWEEPS):
-            one.power_grad(SWEEPS - 1 - k)
+        pl.loop(0, SWEEPS)(lambda i: one.power_grad(SWEEPS - 1 - i))
         dqz[0], dqz[1] = one.finish()
 
 
 def grads_kernel(n, cnt, normed, xbar, wall, wback, dhrb, qt, kt, vt, qlt, klt, dot, a1, e3, blkb, resall, rhv, rhd, taps,
-                 dqz, po, dn, ep, wpart, gtaps, tm, th, hv, hdt, hvr, vr, conv, dconv, gsum, att, dp, dlm):
+                 dqz, po, dn, ep, wpart, gtaps, base, tm, th, hv, hdt, hvr, vr, conv, dconv, gsum, att, dp, dlm):
     half, _, _ = place(n)
-    make_bands(taps, normed.shape[1], tm, th)
+    make_bands(taps, normed.shape[1], base, tm, th)
     value_conv(n, vt, rhv, tm, th, hv, vr, hvr, conv)
     value_conv_back(n, dot, rhd, tm, th, hdt, vr, hvr, dconv, gsum, gtaps)
     attend(resall, a1, conv, att)
@@ -1194,7 +1240,7 @@
         pl.loop(0, hid.shape[1] // GRID_W)(lambda i: kernel_grads(n, cnt[half], b, i, hid, zs, gacc))
     grid_sums(gacc, dh, cotb, gtaps, gk)
     for b in range(2):
-        lnb[b] = norm_back(n, g, cnt[half], b, xblk, dn, dnr, eall, gain, small)
+        norm_back(n, g, cnt[half], b, xblk, dn, dnr, eall, gain, small, lnb.at[b])
 
 
 def late_plain(n, counts, cotb, chalo, xblk, dh, po, ep, dn, wpart, gtaps, gain, obias, pbias, k7, k5, k3, scratch):
@@ -1214,7 +1260,8 @@
     )(counts, hid, halo, cotb, chalo, k7, k5, k3, pbias, xblk, dn, dnr, eall, gain, dh, gtaps)
     out = swap(n, lax.all_gather(outh, "head", axis=2, tiled=True))
     gx = swap(n, lax.all_gather(dh, "head", axis=2, tiled=True) + lnb)
-    gw = lax.psum_scatter(wpart.astype(f32), "seq", scatter_dimension=1, tiled=True)
+    parts = wpart.transpose(2, 1, 0, 3, 4).reshape(4, 512, 256)
+    gw = lax.psum_scatter(parts.astype(f32), "seq", scatter_dimension=1, tiled=True)
     gk, small = lax.psum((gk, small), "seq")
     gkall = lax.all_gather(gk, "head", axis=1, tiled=True)
     return out, gx, gw, small[0:2].reshape(8, 128), gkall
@@ -1222,7 +1269,7 @@
 
 def layer_plain(n, counts, tok, cot, gain, bias, wqkv, woutt, taps, obias, pbias, k7, k5, k3):
     rows = tok.shape[1]
-    made = layer_buffers(n, rows, wqkv.shape[1])
+    made = layer_buffers(n, rows, wqkv.shape[1]) | dict(wpart=((8, 2, 4, 32, 256), bf16))
 
     def out(*names):
         return [sds(*made[name]) for name in names]
@@ -1242,14 +1289,14 @@
     )(counts, normed, xbar, wall, dhrb)
     recvb, recvd, rhv, rhd = reduce_plain(n, blkb, blkd, halv, hald)
     dqz, res = call(
-        functools.partial(chain_kernel, n), [sds((2, 64, MARKS)), sds((BLK, MARKS), bf16)], [VMEM] * 4, tmp(*CHAIN[1:])
+        functools.partial(chain_kernel, n), [sds((2, 64, MARKS)), sds((2, PART, MARKS), bf16)], [VMEM] * 4, tmp(*CHAIN[1:])
     )(recvb, recvd, qlt, klt)
     resall = spread_plain(n, res)
     po, dn, ep, wpart, gtaps = call(
         functools.partial(grads_kernel, n),
         out("po", "dn", "ep", "wpart", "gtaps"),
         [SMEM] + [VMEM] * 19,
-        tmp("tm", "th", "hv", "hdt", "hvr", "vr", "conv", "dconv", "gsum", "att", "dp", "dlm"),
+        tmp("base", "tm", "th", "hv", "hdt", "hvr", "vr", "conv", "dconv", "gsum", "att", "dp", "dlm"),
     )(counts, normed, xbar, wall, wback, dhrb, qt, kt, vt, qlt, klt, dot, a1, e3, blkb, resall, rhv, rhd, taps, dqz)
     return late_plain(
         n, counts, cotb, chalo, xblk, dh, po, ep, dn, wpart, gtaps, gain, obias, pbias, k7, k5, k3, conv_tmp

time: 109 us -> 105 us (0.963); the launches traced: 109 us -> 104 us
  Pallas kernels: 108 us -> 103 us
    pallas_call x1, Pallas kernels: 105 us -> 100 us  [shards(): call(functools.partial(layer_kernel, n, names), [sds(*v) for v in results...]
where the time goes in v5:
time: 105 us; the launch traced here: 104 us
  Pallas kernels  103 us (98%)
    pallas_call x1, Pallas kernels, shards(): call(functools.partial(layer_kernel, n, names), [sds(*v) for v in results...  100 us
    pallas_call x1, Pallas kernels, shards(): call(result_kernel, [sds((2, rows, 512), bf16), sds((2, rows, 512)), sds(...  2.78 us

profile of v5, /device:TPU:0, one launch (start us, length us, event | category | flops | bytes accessed | tf_op | source)
XLA Modules:
  0.0 103.7 jit_solution(17626549397910861154)
XLA Ops:
  0.6 100.1 %shard_map.220 = (bf16[2,256,512]{2,1,0:T(8,128)(2,1)}, f32[2,256,512]{2,1,0:T(8,128)}, f32[4,32,256]{2,1,0:T(8,128)}, f32[8,128]{1,0:T(8,128)}, f32[56,512]{1,0:T(8,128)}) custom-call(s32[2]{0:T(128)} %refs_0_.1, bf16[2,256,512]{2,1,0:T(8,128)(2,1)} %refs_1_.1, bf16[2,256,512]{2,1,0:T(8,128)(2,1)} %refs_2_.1, f32[1,512]{1,0:T(1,128)} %bitcast.11, ...), custom_call_target="tpu_custom_call" | custom-call | tf_op jit(solution)/shard_map/pallas_call | solution.py:1313
  100.7 2.8 %shard_map.221 = (bf16[2,256,512]{2,1,0:T(8,128)(2,1)}, f32[2,256,512]{2,1,0:T(8,128)}, f32[3,32,256]{2,1,0:T(8,128)}, f32[32,256]{1,0:T(8,128)}, f32[1,512]{1,0...) custom-call(bf16[2,256,512]{2,1,0:T(8,128)(2,1)} %get-tuple-element., ...), custom_call_target="tpu_custom_call" | custom-call | tf_op jit(solution)/shard_map/pallas_call | solution.py:1324
